TPU v7x, 512 devices: a whole 4x4x16 slice. The times are simulated.
512 devices in a mesh: depth: 4 (over z_lo), row: 8 (over x, core), col: 16 (over z_hi, y).
Axes of the slice: x: 4, y: 4, z: 16 (z_hi: 4, z_lo: 4; z = z_hi * 4 + z_lo), core: 2. Of those that a mesh axis runs over, the one named last changes fastest.
Arguments:
- tokens: bfloat16 [512, 12288], P(('depth', 'col'), 'row'), may hold values from -6 to 6
- first_weight: bfloat16 [12288, 24576], P('row', ('depth', 'col')), may hold values from -0.0546875 to 0.0546875
- second_weight: bfloat16 [24576, 12288], P(('depth', 'col'), 'row'), may hold values from -0.0390625 to 0.0390625
- grad_out: bfloat16 [512, 12288], P(('depth', 'col'), 'row'), may hold values from -3 to 3
Outputs:
- block_out: bfloat16 [512, 12288], P(('depth', 'col'), 'row')
- input_grad: bfloat16 [512, 12288], P(('depth', 'col'), 'row')
- first_grad: bfloat16 [12288, 24576], P('row', ('depth', 'col'))
- second_grad: bfloat16 [24576, 12288], P(('depth', 'col'), 'row')
All inputs are finite; a program needn't handle non-finite values.
Results may differ from a plain program's by a relative error of at most 0.0049.
Values may be sent and summed in bfloat16 or wider, within the bound.
No kernel may reach another device: no remote copies, remote signals or barrier semaphores. Data moves between devices by JAX's collectives and lax.ppermute only.
A program may use at most 64 MiB of HBM per device.

v0:
```python
import math

import jax
import jax.numpy as jnp
from jax import lax
from jax.sharding import PartitionSpec as P

root_scale = math.sqrt(2.0 / math.pi)
cubic_coef = 0.044715


def gelu_value(values):
    tangent = jnp.tanh(root_scale * (values + cubic_coef * values * values * values))
    return 0.5 * values * (1.0 + tangent)


def gelu_slope(values):
    tangent = jnp.tanh(root_scale * (values + cubic_coef * values * values * values))
    return 0.5 * (1.0 + tangent) + 0.5 * values * (1.0 - tangent * tangent) * root_scale * (
        1.0 + 3.0 * cubic_coef * values * values
    )


def contract_rows(left_side, right_side):
    return lax.dot_general(
        left_side, right_side, (((0,), (0,)), ((), ())), preferred_element_type=jnp.float32
    )


def contract_cols(left_side, right_side):
    return lax.dot_general(
        left_side, right_side, (((1,), (1,)), ((), ())), preferred_element_type=jnp.float32
    )


def quarter_rows(local_rows):
    layer_count = local_rows.shape[0] * lax.axis_size("col")
    every_row = lax.all_gather(local_rows, ("depth", "col"), axis=0, tiled=True)
    layer_rows = lax.dynamic_slice_in_dim(
        every_row, lax.axis_index("depth") * layer_count, layer_count, 0
    )
    return (layer_rows, every_row)


def on_device(tokens, first_weight, second_weight, grad_out):
    layer_tokens, every_tokens = quarter_rows(tokens)
    replica_first = lax.all_gather(first_weight, "depth", axis=1, tiled=True)
    hidden_input = lax.psum(
        jnp.dot(layer_tokens, replica_first, preferred_element_type=jnp.float32), "row"
    )
    hidden = gelu_value(hidden_input).astype(jnp.bfloat16)
    hidden_whole = lax.all_to_all(hidden, "depth", split_axis=1, concat_axis=0, tiled=True)
    layer_grads, every_grads = quarter_rows(grad_out)
    replica_second = lax.all_gather(second_weight, "depth", axis=0, tiled=True)
    picked = hidden
    block_out = lax.psum_scatter(
        jnp.dot(picked, replica_second, preferred_element_type=jnp.float32),
        "col",
        scatter_dimension=0,
        tiled=True,
    )
    grad_partial = contract_cols(layer_grads, replica_second)
    grad_hidden = lax.psum(grad_partial, "row")
    grad_pre = (grad_hidden * gelu_slope(hidden_input)).astype(jnp.bfloat16)
    picked = grad_pre
    input_grad = lax.psum_scatter(
        contract_cols(picked, replica_first), "col", scatter_dimension=0, tiled=True
    ).astype(jnp.bfloat16)
    grad_whole = lax.all_to_all(grad_pre, "depth", split_axis=1, concat_axis=0, tiled=True)
    first_grad = contract_rows(every_tokens, grad_whole).astype(jnp.bfloat16)
    second_grad = contract_rows(hidden_whole, every_grads).astype(jnp.bfloat16)
    return (block_out.astype(jnp.bfloat16), input_grad, first_grad, second_grad)


def solution(mesh):
    return jax.shard_map(
        on_device,
        mesh=mesh,
        in_specs=(
            P(("depth", "col"), "row"),
            P("row", ("depth", "col")),
            P(("depth", "col"), "row"),
            P(("depth", "col"), "row"),
        ),
        out_specs=(
            P(("depth", "col"), "row"),
            P(("depth", "col"), "row"),
            P("row", ("depth", "col")),
            P(("depth", "col"), "row"),
        ),
        check_vma=False,
    )
```

profile of v0, /device:TPU:24, one launch (start us, length us, event | category | flops | bytes accessed | tf_op | source)
XLA Modules:
  0.0 1292.6 jit_solution(2360599872356249660)
XLA Ops:
  7.9 0.7 all-gather.9.cloned.1.call-update
  10.0 363.8 %all-gather.11.cloned.1.call-done = bf16[512,1536]{1,0:T(8,128)(2,1)} async-done(((bf16[8,1536]{1,0:T(8,128)(2,1)}), bf16[512,1536]{1,0:T(8,128)(2,1)}) %all-gather.11.cloned.1.call-update) | async-done | bytes 1572880 | tf_op jit(solution)/shard_map/all_gather | solution.py:38
  373.8 116.1 %all-gather.9.cloned.1.call-done = bf16[1536,1536]{1,0:T(8,128)(2,1)} async-done(((bf16[384,1536]{1,0:T(8,128)(2,1)}), bf16[1536,1536]{1,0:T(8,128)(2,1)}) %all-gather.9.cloned.1.call-update) | async-done | bytes 4718608 | tf_op jit(solution)/shard_map/all_gather | solution.py:54
  489.9 5.0 fusion.8
  494.8 356.8 %all-gather.5.cloned.1.call-done = bf16[512,1536]{1,0:T(8,128)(2,1)} async-done(((bf16[8,1536]{1,0:T(8,128)(2,1)}), bf16[512,1536]{1,0:T(8,128)(2,1)}) %all-gather.5.cloned.1.call-update) | async-done | bytes 1572880 | tf_op jit(solution)/shard_map/all_gather | solution.py:38
  851.6 116.0 %all-gather.7.cloned.1.call-done = bf16[1536,1536]{1,0:T(8,128)(2,1)} async-done(((bf16[1536,384]{1,0:T(8,128)(2,1)}), bf16[1536,1536]{1,0:T(8,128)(2,1)}) %all-gather.7.cloned.1.call-update) | async-done | bytes 4718608 | tf_op jit(solution)/shard_map/all_gather | solution.py:47
  967.6 4.1 fusion.10
  971.8 79.8 %all-reduce.3.cloned.1.call-done = (f32[128,1536]{1,0:T(8,128)}, f32[128,1536]{1,0:T(8,128)}) async-done(((f32[128,1536]{1,0:T(8,128)}, f32[128,1536]{1,0:T(8,128)}), (f32[128,1536]{1,0:T(8,128)}, f32[128,1536]{1,0:T(8,128)})) %all-reduce.3.cloned.1.call-update) | async-done | bytes 1572880 | tf_op jit(solution)/shard_map/psum | solution.py:48
  1051.6 1.9 fusion.7
  1053.5 4.9 fusion.15
  1058.4 0.8 copy.17
  1059.2 4.8 all-to-all-start
  1064.0 4.0 fusion.14
  1068.0 0.8 copy.16
  1068.8 4.9 all-to-all-done
  1073.7 3.5 all-to-all-start.1
  1077.2 0.8 fusion
  1078.0 1.4 copy.11
  1079.4 8.9 all-to-all-done.1
  1088.3 1.8 convolution_convert_fusion
  1090.1 82.9 %reduce-scatter.5.cloned.1.call-done = f32[8,1536]{1,0:T(8,128)} async-done(((f32[128,1536]{1,0:T(8,128)}), f32[8,1536]{1,0:T(8,128)}) %reduce-scatter.5.cloned.1.call-update) | async-done | bytes 49168 | tf_op jit(solution)/shard_map/reduce_scatter | solution.py:66
  1173.0 1.4 convert_element_type.24
  1174.4 109.9 %reduce-scatter.3.cloned.1.call-done = f32[8,1536]{1,0:T(8,128)} async-done(((f32[128,1536]{1,0:T(8,128)}), f32[8,1536]{1,0:T(8,128)}) %reduce-scatter.3.cloned.1.call-update) | async-done | bytes 49168 | tf_op jit(solution)/shard_map/reduce_scatter | solution.py:56
  1284.3 1.4 convert_element_type.22
  (17 shorter events, 2.2 us)
Async XLA Ops:
  7.2 366.6 %all-gather.11.cloned.1.call-start = ((), (), s32[]{:S(2)}) async-start(), calls=%async_computation.8 | async-start | bytes 1597440 | tf_op jit(solution)/shard_map/all_gather | solution.py:38
  7.9 482.0 %all-gather.9.cloned.1.call-start = ((), (), s32[]{:S(2)}) async-start(), calls=%async_computation.6 | async-start | bytes 5898240 | tf_op jit(solution)/shard_map/all_gather | solution.py:54
  8.6 843.0 %all-gather.5.cloned.1.call-start = ((), (), s32[]{:S(2)}) async-start(), calls=%async_computation.4 | async-start | bytes 1597440 | tf_op jit(solution)/shard_map/all_gather | solution.py:38
  9.4 958.2 %all-gather.7.cloned.1.call-start = ((), (), s32[]{:S(2)}) async-start(), calls=%async_computation.5 | async-start | bytes 5898240 | tf_op jit(solution)/shard_map/all_gather | solution.py:47
  10.0 1041.6 %all-reduce.3.cloned.1.call-start = ((), (), s32[]{:S(2)}) async-start(), calls=%async_computation.10 | async-start | bytes 3145728 | tf_op jit(solution)/shard_map/psum | solution.py:48
  971.7 201.3 %reduce-scatter.5.cloned.1.call-start = ((), (), s32[]{:S(2)}) async-start(), calls=%async_computation.9 | async-start | bytes 835584 | tf_op jit(solution)/shard_map/reduce_scatter | solution.py:66
  1059.2 14.5 %all-to-all-start = ((bf16[128,4,384]{2,0,1:T(8,128)(2,1)}), bf16[128,4,384]{2,0,1:T(8,128)(2,1)S(1)}, u32[]{:S(2)}, u32[]{:S(2)}) async-start(bf16[128,4,384]{2,0,1:T(8,128)(2,1)} %bitcast.25), calls=%async_computation.2 | async-start | bytes 786432 | tf_op jit(solution)/shard_map/all_to_all | solution.py:69
  1064.0 220.3 %reduce-scatter.3.cloned.1.call-start = ((), (), s32[]{:S(2)}) async-start(), calls=%async_computation.7 | async-start | bytes 835584 | tf_op jit(solution)/shard_map/reduce_scatter | solution.py:56
  1068.0 9.2 copy-start.1
  1073.7 14.6 %all-to-all-start.1 = ((bf16[128,4,384]{2,0,1:T(8,128)(2,1)}), bf16[128,4,384]{2,0,1:T(8,128)(2,1)S(1)}, u32[]{:S(2)}, u32[]{:S(2)}) async-start(bf16[128,4,384]{2,0,1:T(8,128)(2,1)} %bitcast.24), calls=%async_computation.3 | async-start | bytes 786432 | tf_op jit(solution)/shard_map/all_to_all | solution.py:52
  1078.0 10.3 copy-start
Sparse Core Ops, SparseCore 0:
  10.1 363.6 all-gather.10
  375.9 113.9 all-gather.8
  491.9 359.6 all-gather.4
  853.6 113.9 all-gather.6
  971.9 79.6 all-reduce.2
  1058.5 114.4 reduce-scatter.4
  1177.1 107.1 reduce-scatter.2
where the time goes:
time: 1290 us
  waiting for transfers between devices  1240 us (96%)
  matrix products  20.6 us (2%)
  between operations  14.2 us (1%)
    all_gather x2, waiting for transfers between devices, quarter_rows(): every_row = lax.all_gather(local_rows, ('depth', 'col'), axis=0, tiled=True)  721 us
    all_gather x1, waiting for transfers between devices, on_device(): replica_second = lax.all_gather(second_weight, 'depth', axis=0, tiled=True)  116 us
    all_gather x1, waiting for transfers between devices, on_device(): replica_first = lax.all_gather(first_weight, 'depth', axis=1, tiled=True)  116 us
    reduce_scatter x1, waiting for transfers between devices, on_device(): lax.psum_scatter(jnp.dot(picked, replica_second, preferred_element_type=j...  110 us
    reduce_scatter x1, waiting for transfers between devices, on_device(): lax.psum_scatter(contract_cols(picked, replica_first), 'col', scatter_dim...  82.9 us
    psum x1, waiting for transfers between devices, on_device(): lax.psum(jnp.dot(layer_tokens, replica_first, preferred_element_type=jnp....  79.8 us
  transfers between devices with their start and end apart: 9, of which 9 were waited for; matrix products, arithmetic and copies ran while one was open for 1% of the time, Pallas kernels for 0%

commit v1 on v0

v1 whole, which is shorter than its diff:
```python
import math

import jax
import jax.numpy as jnp
from jax import lax
from jax.sharding import Mesh, PartitionSpec as P

root_scale = math.sqrt(2.0 / math.pi)
cubic_coef = 0.044715

ROW = ("x", "core")


def gelu_pair(values):
    square = values * values
    tangent = jnp.tanh(root_scale * (values + cubic_coef * values * square))
    value = 0.5 * values * (1.0 + tangent)
    slope = 0.5 * (1.0 + tangent) + 0.5 * values * (1.0 - tangent * tangent) * root_scale * (
        1.0 + 3.0 * cubic_coef * square
    )
    return value, slope


def dot_over(left_side, right_side, left_dim, right_dim):
    return lax.dot_general(
        left_side,
        right_side,
        (((left_dim,), (right_dim,)), ((), ())),
        preferred_element_type=jnp.float32,
    )


def gather_rows(block, axis):
    size = lax.axis_size(axis)
    copies = jnp.broadcast_to(block[None], (size,) + block.shape)
    parts = lax.all_to_all(copies, axis, 0, 0)
    return parts.reshape(size * block.shape[0], block.shape[1])


def sum_rows(partial, axis):
    size = lax.axis_size(axis)
    rows, width = partial.shape
    parts = partial.astype(jnp.bfloat16).reshape(size, rows // size, width)
    parts = lax.all_to_all(parts, axis, 0, 0)
    return jnp.sum(parts.astype(jnp.float32), axis=0)


def on_device(tokens, first_weight, second_weight, grad_out):
    width = tokens.shape[1]
    units = first_weight.shape[1]
    both = jnp.concatenate([tokens, grad_out], axis=1)
    for axis in ("z_hi", "z_lo", "y"):
        both = gather_rows(both, axis)
    every_tokens, every_grads = both[:, :width], both[:, width:]
    partial = jnp.concatenate(
        [
            dot_over(every_tokens, first_weight, 1, 0).astype(jnp.bfloat16),
            dot_over(every_grads, second_weight, 1, 1).astype(jnp.bfloat16),
        ],
        axis=1,
    )
    summed = sum_rows(partial, ROW)
    hidden_share, slope = gelu_pair(summed[:, :units])
    pre_share = summed[:, units:] * slope
    shares = jnp.concatenate([hidden_share, pre_share], axis=1).astype(jnp.bfloat16)
    shares = gather_rows(shares, ROW)
    hidden, grad_pre = shares[:, :units], shares[:, units:]
    outs = jnp.concatenate(
        [
            dot_over(hidden, second_weight, 1, 0).astype(jnp.bfloat16),
            dot_over(grad_pre, first_weight, 1, 1).astype(jnp.bfloat16),
        ],
        axis=1,
    )
    first_grad = dot_over(every_tokens, grad_pre, 0, 0).astype(jnp.bfloat16)
    second_grad = dot_over(hidden, every_grads, 0, 0).astype(jnp.bfloat16)
    for axis in ("y", "z_lo", "z_hi"):
        outs = sum_rows(outs, axis)
    outs = outs.astype(jnp.bfloat16)
    return (outs[:, :width], outs[:, width:], first_grad, second_grad)


def solution(mesh):
    grid = Mesh(mesh.devices.reshape(4, 4, 2, 4, 4), ("z_lo", "x", "core", "z_hi", "y"))
    rows = P(("z_lo", "z_hi", "y"), ROW)
    columns = P(ROW, ("z_lo", "z_hi", "y"))
    return jax.shard_map(
        on_device,
        mesh=grid,
        in_specs=(rows, columns, rows, rows),
        out_specs=(rows, rows, columns, rows),
        check_vma=False,
    )
```

time: 1290 us -> 221 us (0.17)
  waiting for transfers between devices: 1240 us -> 9.79 us
  blocking collectives: 0 us -> 189 us
  between operations: 14.2 us -> 0.77 us
    all_gather x4 -> x0, waiting for transfers between devices: 953 us -> none  [the longest x2 721 us: quarter_rows(): every_row = lax.all_gather(local_rows, ('depth', 'col'), axis=0, tiled=True)]
    reduce_scatter x2 -> x0, waiting for transfers between devices: 193 us -> none  [the longest x1 110 us: on_device(): lax.psum_scatter(jnp.dot(picked, replica_second, preferred_element_type=j...]
    all_to_all x0 -> x7, blocking collectives: none -> 189 us  [the longest x4 109 us: gather_rows(): parts = lax.all_to_all(copies, axis, 0, 0)]
    psum x1 -> x0, waiting for transfers between devices: 79.8 us -> none  [on_device(): lax.psum(jnp.dot(layer_tokens, replica_first, preferred_element_type=jnp....]
  transfers between devices with their start and end apart: 9 -> 1, of which waited for: 9 -> 1; matrix products, arithmetic and copies ran while one was open for 1% -> 2% of each run, Pallas kernels for 0% -> 0%
where the time goes in v1:
time: 221 us; the launch traced here: 219 us
  blocking collectives  189 us (86%)
  waiting for transfers between devices  9.79 us (4%)
  matrix products  9.07 us (4%)
  other arithmetic  4.92 us (2%)
  starting transfers between devices  3.7 us (2%)
  local copies, waits for them, and re-layouts  2.48 us (1%)
    all_to_all x4, blocking collectives, gather_rows(): parts = lax.all_to_all(copies, axis, 0, 0)  109 us
    all_to_all x3, blocking collectives, sum_rows(): parts = lax.all_to_all(parts, axis, 0, 0)  79.7 us
    all_to_all x1, waiting for transfers between devices, sum_rows(): parts = lax.all_to_all(parts, axis, 0, 0)  9.79 us
    dot_general x6, matrix products, dot_over(): lax.dot_general(left_side, right_side, (((left_dim,), (right_dim,)), ((),...  9.07 us
  transfers between devices with their start and end apart: 1, of which 1 were waited for; matrix products, arithmetic and copies ran while one was open for 2% of the time, Pallas kernels for 0%

profile of v1, /device:TPU:24, one launch (start us, length us, event | category | flops | bytes accessed | tf_op | source)
XLA Modules:
  0.0 219.4 jit_solution(15798612832796965719)
XLA Ops:
  0.6 0.9 pad_maximum_fusion.3
  1.5 31.8 %all_to_all.40 = bf16[4,8,3072]{2,1,0:T(8,128)(2,1)S(1)} all-to-all(bf16[4,8,3072]{2,1,0:T(8,128)(2,1)S(1)} %broadcast_in_dim.12), channel_id=1, replica_groups=mesh['z_lo'=4,'x'=4,'core'=2,'z_hi'=4,'y'=4] {'z_hi'}, dimensions={0} | all-to-all | bytes 393216 | tf_op jit(solution)/shard_map/all_to_all | solution.py:36
  33.4 22.7 %all_to_all.41 = bf16[4,32,3072]{2,1,0:T(8,128)(2,1)S(1)} all-to-all(bf16[4,32,3072]{2,1,0:T(8,128)(2,1)S(1)} %broadcast_in_dim.28), channel_id=1, replica_groups=mesh['z_lo'=4,'x'=4,'core'=2,'z_hi'=4,'y'=4] {'z_lo'}, dimensions={0} | all-to-all | bytes 1572864 | tf_op jit(solution)/shard_map/all_to_all | solution.py:36
  56.2 0.4 broadcast_in_dim.30
  56.5 38.7 %all_to_all.42 = bf16[4,128,3072]{2,1,0:T(8,128)(2,1)S(1)} all-to-all(bf16[4,128,3072]{2,1,0:T(8,128)(2,1)S(1)} %broadcast_in_dim.30), channel_id=1, replica_groups=mesh['z_lo'=4,'x'=4,'core'=2,'z_hi'=4,'y'=4] {'y'}, dimensions={0} | all-to-all | bytes 6291456 | tf_op jit(solution)/shard_map/all_to_all | solution.py:36
  95.2 0.8 fusion.9
  96.1 0.8 copy-done.1
  96.9 0.8 fusion.6
  97.8 0.3 copy.9
  98.1 17.3 %all_to_all.43 = bf16[8,64,768]{2,1,0:T(8,128)(2,1)S(1)} all-to-all(bf16[8,64,768]{2,1,0:T(8,128)(2,1)S(1)} %bitcast.21), channel_id=1, replica_groups=mesh['z_lo'=4,'x'=4,'core'=2,'z_hi'=4,'y'=4] {'x','core'}, dimensions={0} | all-to-all | bytes 1572864 | tf_op jit(solution)/shard_map/all_to_all | solution.py:44
  115.7 15.7 %all_to_all.44 = bf16[8,64,768]{2,1,0:T(8,128)(2,1)S(1)} all-to-all(bf16[8,64,768]{2,1,0:T(8,128)(2,1)S(1)} %broadcast_in_dim.31), channel_id=1, replica_groups=mesh['z_lo'=4,'x'=4,'core'=2,'z_hi'=4,'y'=4] {'x','core'}, dimensions={0} | all-to-all | bytes 1572864 | tf_op jit(solution)/shard_map/all_to_all | solution.py:36
  131.4 1.0 convolution_convert_fusion
  132.4 0.3 copy-done.4
  132.6 1.0 convolution_convert_fusion.1
  133.6 0.4 pad_maximum_fusion
  134.1 40.8 %all_to_all.45 = bf16[4,128,3072]{2,1,0:T(8,128)(2,1)} all-to-all(bf16[4,128,3072]{2,1,0:T(8,128)(2,1)S(1)} %bitcast.12), channel_id=1, replica_groups=mesh['z_lo'=4,'x'=4,'core'=2,'z_hi'=4,'y'=4] {'y'}, dimensions={0} | all-to-all | bytes 6291456 | tf_op jit(solution)/shard_map/all_to_all | solution.py:44
  174.9 2.5 %reduce_sum.46 = bf16[128,3072]{1,0:T(8,128)(2,1)S(1)} reduce(bf16[4,128,3072]{2,1,0:T(8,128)(2,1)} %all_to_all.45, bf16[]{:T(256)} %constant.15.clone.1), dimensions={0}, to_apply=%region_1.0 | reduce | flops 1179648 | bytes 3932162 | tf_op jit(solution)/shard_map/reduce_sum | solution.py:45
  177.4 21.6 %all_to_all.46 = bf16[4,32,3072]{2,1,0:T(8,128)(2,1)S(1)} all-to-all(bf16[4,32,3072]{2,1,0:T(8,128)(2,1)S(1)} %bitcast.22), channel_id=1, replica_groups=mesh['z_lo'=4,'x'=4,'core'=2,'z_hi'=4,'y'=4] {'z_lo'}, dimensions={0} | all-to-all | bytes 1572864 | tf_op jit(solution)/shard_map/all_to_all | solution.py:44
  199.0 0.8 reduce_sum.47
  199.8 3.7 %all-to-all-start.7 = ((bf16[4,8,3072]{2,1,0:T(8,128)(2,1)}), bf16[4,8,3072]{2,1,0:T(8,128)(2,1)S(1)}, u32[]{:S(2)}, u32[]{:S(2)}) async-start(bf16[4,8,3072]{2,1,0:T(8,128)(2,1)} %bitcast.7), calls=%async_computation.7 | async-start | bytes 393216 | tf_op jit(solution)/shard_map/all_to_all | solution.py:44
  203.5 3.4 %convolution_convert_fusion.2 = bf16[384,1536]{1,0:T(8,128)(2,1)} fusion(bf16[512,3072]{1,0:T(8,128)(2,1)} %bitcast.19, bf16[512,768]{1,0:T(8,128)(2,1)S(1)} %bitcast.15), kind=kOutput, calls=%fused_computation.3 | convolution fusion | flops 604569600 | bytes 3145728 | tf_op jit(solution)/shard_map/dot_general | solution.py:25
  206.9 2.0 convolution_convert_fusion.3
  208.9 9.8 %all-to-all-done.7 = bf16[4,8,3072]{2,1,0:T(8,128)(2,1)S(1)} async-done(((bf16[4,8,3072]{2,1,0:T(8,128)(2,1)}), bf16[4,8,3072]{2,1,0:T(8,128)(2,1)S(1)}, u32[]{:S(2)}, u32[]{:S(2)}) %all-to-all-start.7) | async-done | bytes 196640 | tf_op jit(solution)/shard_map/all_to_all | solution.py:44
  218.8 0.6 fusion.17
  (16 shorter events, 0.4 us)
Async XLA Ops:
  0.6 96.3 %copy-start = (bf16[1536,384]{1,0:T(8,128)(2,1)S(1)}, bf16[1536,384]{1,0:T(8,128)(2,1)}, u32[]{:S(2)}) copy-start(bf16[1536,384]{1,0:T(8,128)(2,1)} %param.5) | copy-start | bytes 3538948
  56.5 38.7 %copy-start.3 = (bf16[384,1536]{1,0:T(8,128)(2,1)S(1)}, bf16[384,1536]{1,0:T(8,128)(2,1)}, u32[]{:S(2)}) copy-start(bf16[384,1536]{1,0:T(8,128)(2,1)} %param.6) | copy-start | bytes 3538948
  95.2 1.7 copy-start.1
  131.4 1.3 copy-start.4
  199.8 18.9 %all-to-all-start.7 = ((bf16[4,8,3072]{2,1,0:T(8,128)(2,1)}), bf16[4,8,3072]{2,1,0:T(8,128)(2,1)S(1)}, u32[]{:S(2)}, u32[]{:S(2)}) async-start(bf16[4,8,3072]{2,1,0:T(8,128)(2,1)} %bitcast.7), calls=%async_computation.7 | async-start | bytes 393216 | tf_op jit(solution)/shard_map/all_to_all | solution.py:44
  203.5 3.4 %copy-start.2 = (bf16[4,128,3072]{2,1,0:T(8,128)(2,1)S(1)}, bf16[4,128,3072]{2,1,0:T(8,128)(2,1)}, u32[]{:S(2)}) copy-start(bf16[4,128,3072]{2,1,0:T(8,128)(2,1)} %copy-done.1) | copy-start | bytes 9437188

commit v2 on v1

v2 whole, which is shorter than its diff:
```python
import math

import jax
import jax.numpy as jnp
from jax import lax
from jax.experimental import pallas as pl
from jax.experimental.pallas import tpu as pltpu
from jax.sharding import Mesh, PartitionSpec as P

root_scale = math.sqrt(2.0 / math.pi)
cubic_coef = 0.044715

GRID = ("z_lo", "x", "core", "z_hi", "y")
SIZES = (4, 4, 2, 4, 4)
ROW = ("x", "core")
BLOCK = 32
PIECE = 128
HALF = 64
SWAP = ((0, 1), (1, 0))
params = pltpu.CompilerParams(vmem_limit_bytes=32 << 20)


def place_of(z_lo, x, core, z_hi, y):
    return (((z_lo * 4 + x) * 2 + core) * 4 + z_hi) * 4 + y


def every_place():
    for z_lo in range(4):
        for x in range(4):
            for core in range(2):
                for z_hi in range(4):
                    for y in range(4):
                        yield z_lo, x, core, z_hi, y


def near_groups():
    groups = []
    for x in range(4):
        for z_hi in range(4):
            for other in range(4):
                groups.append([place_of(i, x, 0, z_hi, other) for i in range(4)])
                groups.append([place_of(other, x, 1, z_hi, i) for i in range(4)])
    return groups


def far_shift(step):
    pairs = []
    for z_lo, x, core, z_hi, y in every_place():
        if core == 0:
            target = place_of(z_lo, x, core, z_hi, (y + step) % 4)
        else:
            z = (z_hi * 4 + z_lo + step) % 16
            target = place_of(z % 4, x, core, z // 4, y)
        pairs.append((place_of(z_lo, x, core, z_hi, y), target))
    return pairs


def moved(value, step):
    return lax.ppermute(value, GRID, far_shift(step))


def dot_over(left_side, right_side, left_dim, right_dim):
    return lax.dot_general(
        left_side,
        right_side,
        (((left_dim,), (right_dim,)), ((), ())),
        preferred_element_type=jnp.float32,
    )


def copies_of(block, count):
    return jnp.broadcast_to(block[None], (count,) + block.shape)


def common_block(core, own, piece, part):
    index = lax.rem(own + piece, 4)
    return jnp.where(core == 0, index * 4 + part, part * 4 + index)


def first_kernel(place, p0, p1, p2a, p2b, p3, first, second, both, kept, given, sums):
    core, own = place[0], place[1]
    width = first.shape[0]
    units = first.shape[1]
    both[0:128, :] = p0[...]
    both[128:256, :] = p1[...]
    both[256:320, :] = p2a[...]
    both[320:384, :] = p2b[...]
    both[384:512, :] = p3[...]
    sums[:, :units] = dot_over(both[:, :width], first[...], 1, 0)
    sums[:, units:] = dot_over(both[:, width:], second[...], 1, 1)
    for piece in range(4):
        for part in range(4):
            block = common_block(core, own, piece, part)
            start = pl.multiple_of(lax.rem(block, 8) * BLOCK, BLOCK)
            at = (piece * 4 + part) * BLOCK
            mine = block // 8 == core

            @pl.when(mine)
            def _():
                kept[pl.ds(start, BLOCK), :] = sums[at : at + BLOCK, :]

            @pl.when(jnp.logical_not(mine))
            def _():
                given[pl.ds(start, BLOCK), :] = sums[at : at + BLOCK, :]


def gelu_kernel(parts, shares):
    units = shares.shape[2] // 2
    total = parts[0] + parts[1] + parts[2] + parts[3]
    values, slopes = total[:, :units], total[:, units:]
    square = values * values
    tangent = jnp.tanh(root_scale * (values + cubic_coef * values * square))
    hidden = 0.5 * values * (1.0 + tangent)
    slope = 0.5 * (1.0 + tangent) + 0.5 * values * (1.0 - tangent * tangent) * root_scale * (
        1.0 + 3.0 * cubic_coef * square
    )
    pre = slopes * slope
    for copy in range(4):
        shares[copy, :, :units] = hidden.astype(jnp.bfloat16)
        shares[copy, :, units:] = pre.astype(jnp.bfloat16)


def second_kernel(place, shares, first, second, o0, o1, o2a, o2b, o3, local):
    core, own = place[0], place[1]
    width = first.shape[0]
    units = first.shape[1]
    for piece in range(4):
        for part in range(4):
            block = common_block(core, own, piece, part)
            start = pl.multiple_of(block * BLOCK, BLOCK)
            at = (piece * 4 + part) * BLOCK
            local[at : at + BLOCK, :] = shares[pl.ds(start, BLOCK), :]
    for side in range(2):
        rows = local[:, side * units : (side + 1) * units]
        if side == 0:
            outs = dot_over(rows, second[...], 1, 0)
        else:
            outs = dot_over(rows, first[...], 1, 1)
        columns = slice(side * width, (side + 1) * width)
        o0[:, columns] = outs[0:128]
        o1[:, columns] = outs[128:256].astype(jnp.bfloat16)
        o2a[:, columns] = outs[256:320].astype(jnp.bfloat16)
        o2b[:, columns] = outs[320:384].astype(jnp.bfloat16)
        o3[:, columns] = outs[384:512].astype(jnp.bfloat16)


def summed(parts):
    return jnp.sum(parts.astype(jnp.float32), axis=0).astype(jnp.bfloat16)


def shape_of(rows, columns, dtype):
    return jax.ShapeDtypeStruct((rows, columns), dtype)


def on_device(tokens, first_weight, second_weight, grad_out):
    width = tokens.shape[1]
    units = first_weight.shape[1]
    core = lax.axis_index("core")
    own = jnp.where(core == 0, lax.axis_index("y"), lax.axis_index("z_lo"))
    place = jnp.stack([core, own]).astype(jnp.int32)
    scalars = pl.BlockSpec(memory_space=pltpu.SMEM)
    whole = pl.BlockSpec(memory_space=pltpu.VMEM)
    near = near_groups()

    both = jnp.concatenate([tokens, grad_out], axis=1)
    both = lax.all_to_all(copies_of(both, 4), "z_hi", 0, 0).reshape(BLOCK, 2 * width)
    both = lax.all_to_all(copies_of(both, 4), GRID, 0, 0, axis_index_groups=near)
    both = both.reshape(PIECE, 2 * width)
    p1 = moved(both, -1)
    p3 = moved(both, 1)
    p2a = moved(both[:HALF], -2)
    p2b = moved(both[HALF:], 2)

    every, kept, given = pl.pallas_call(
        first_kernel,
        out_shape=(
            shape_of(512, 2 * width, jnp.bfloat16),
            shape_of(256, 2 * units, jnp.float32),
            shape_of(256, 2 * units, jnp.float32),
        ),
        in_specs=[scalars] + [whole] * 7,
        out_specs=(whole, whole, whole),
        scratch_shapes=[pltpu.VMEM((512, 2 * units), jnp.float32)],
        compiler_params=params,
    )(place, both, p1, p2a, p2b, p3, first_weight, second_weight)
    kept = kept + lax.ppermute(given, "core", SWAP)
    parts = lax.all_to_all(kept.reshape(4, HALF, 2 * units), "x", 0, 0)
    shares = pl.pallas_call(
        gelu_kernel,
        out_shape=jax.ShapeDtypeStruct((4, HALF, 2 * units), jnp.bfloat16),
        in_specs=[whole],
        out_specs=whole,
        compiler_params=params,
    )(parts)
    shares = lax.all_to_all(shares, "x", 0, 0).reshape(256, 2 * units)
    shares = lax.all_gather(shares, "core", axis=0, tiled=True)
    o0, o1, o2a, o2b, o3, local = pl.pallas_call(
        second_kernel,
        out_shape=(
            shape_of(PIECE, 2 * width, jnp.float32),
            shape_of(PIECE, 2 * width, jnp.bfloat16),
            shape_of(HALF, 2 * width, jnp.bfloat16),
            shape_of(HALF, 2 * width, jnp.bfloat16),
            shape_of(PIECE, 2 * width, jnp.bfloat16),
            shape_of(512, 2 * units, jnp.bfloat16),
        ),
        in_specs=[scalars] + [whole] * 3,
        out_specs=(whole,) * 6,
        compiler_params=params,
    )(place, shares, first_weight, second_weight)
    r1 = moved(o1, 1)
    r3 = moved(o3, -1)
    r2a = moved(o2a, 2)
    r2b = moved(o2b, -2)
    hidden, grad_pre = local[:, :units], local[:, units:]
    first_grad = dot_over(every[:, :width], grad_pre, 0, 0).astype(jnp.bfloat16)
    second_grad = dot_over(hidden, every[:, width:], 0, 0).astype(jnp.bfloat16)
    r2 = jnp.concatenate([r2a, r2b], axis=0)
    outs = o0 + r1.astype(jnp.float32) + r3.astype(jnp.float32) + r2.astype(jnp.float32)
    outs = outs.astype(jnp.bfloat16).reshape(4, BLOCK, 2 * width)
    outs = summed(lax.all_to_all(outs, GRID, 0, 0, axis_index_groups=near))
    outs = summed(lax.all_to_all(outs.reshape(4, 8, 2 * width), "z_hi", 0, 0))
    return (outs[:, :width], outs[:, width:], first_grad, second_grad)


def solution(mesh):
    grid = Mesh(mesh.devices.reshape(SIZES), GRID)
    rows = P(("z_lo", "z_hi", "y"), ROW)
    columns = P(ROW, ("z_lo", "z_hi", "y"))
    return jax.shard_map(
        on_device,
        mesh=grid,
        in_specs=(rows, columns, rows, rows),
        out_specs=(rows, rows, columns, rows),
        check_vma=False,
    )
```

time: 221 us -> 181 us (0.82)
  blocking collectives: 189 us -> 96.4 us
  starting transfers between devices: 3.7 us -> 31.6 us
  waiting for transfers between devices: 9.79 us -> 35.5 us
  Pallas kernels: 0 us -> 6.09 us
  matrix products: 9.07 us -> 4.92 us
    all_to_all x7 -> x5, blocking collectives: 189 us -> 94.1 us  [the longest x1 31.8 us: on_device(): lax.all_to_all(copies_of(both, 4), 'z_hi', 0, 0).reshape(BLOCK, 2 * width)]
    ppermute x0 -> x9, starting transfers between devices: none -> 28.3 us  [the longest x8 26.4 us: moved(): return lax.ppermute(value, GRID, far_shift(step))]
    ppermute x0 -> x9, waiting for transfers between devices: none -> 26.9 us  [the longest x8 24.7 us: moved(): return lax.ppermute(value, GRID, far_shift(step))]
    pallas_call x0 -> x3, Pallas kernels: none -> 6.09 us  [the longest x1 3.64 us: on_device(): pl.pallas_call(first_kernel, out_shape=(shape_of(512, 2 * width, jnp.bflo...]
    dot_general x6 -> x2, matrix products: 9.07 us -> 4.92 us  [dot_over(): lax.dot_general(left_side, right_side, (((left_dim,), (right_dim,)), ((),...]
    all_gather x0 -> x1, blocking collectives: none -> 2.36 us  [on_device(): shares = lax.all_gather(shares, 'core', axis=0, tiled=True)]
  transfers between devices with their start and end apart: 1 -> 10, of which waited for: 1 -> 7; matrix products, arithmetic and copies ran while one was open for 2% -> 3% of each run, Pallas kernels for 0% -> 0%
where the time goes in v2:
time: 181 us; the launch traced here: 180 us
  blocking collectives  96.4 us (53%)
  waiting for transfers between devices  35.5 us (20%)
  starting transfers between devices  31.6 us (17%)
  Pallas kernels  6.09 us (3%)
  matrix products  4.92 us (3%)
  other arithmetic  3.36 us (2%)
    all_to_all x1, blocking collectives, on_device(): lax.all_to_all(copies_of(both, 4), 'z_hi', 0, 0).reshape(BLOCK, 2 * width)  31.8 us
    ppermute x8, starting transfers between devices, moved(): return lax.ppermute(value, GRID, far_shift(step))  26.4 us
    ppermute x8, waiting for transfers between devices, moved(): return lax.ppermute(value, GRID, far_shift(step))  24.7 us
    all_to_all x1, blocking collectives, on_device(): outs = summed(lax.all_to_all(outs, GRID, 0, 0, axis_index_groups=near))  18.2 us
    all_to_all x1, blocking collectives, on_device(): lax.all_to_all(copies_of(both, 4), GRID, 0, 0, axis_index_groups=near)  17.6 us
    all_to_all x1, blocking collectives, on_device(): parts = lax.all_to_all(kept.reshape(4, HALF, 2 * units), 'x', 0, 0)  16.7 us
    all_to_all x1, blocking collectives, on_device(): shares = lax.all_to_all(shares, 'x', 0, 0).reshape(256, 2 * units)  9.77 us
    all_to_all x1, waiting for transfers between devices, on_device(): outs = summed(lax.all_to_all(outs.reshape(4, 8, 2 * width), 'z_hi', 0, 0))  8.56 us
  transfers between devices with their start and end apart: 10, of which 7 were waited for; matrix products, arithmetic and copies ran while one was open for 3% of the time, Pallas kernels for 0%

profile of v2, /device:TPU:24, one launch (start us, length us, event | category | flops | bytes accessed | tf_op | source)
XLA Modules:
  0.0 180.4 jit_solution(726004844005125337)
XLA Ops:
  1.4 31.8 %all_to_all.30 = bf16[4,8,3072]{2,1,0:T(8,128)(2,1)S(1)} all-to-all(bf16[4,8,3072]{2,1,0:T(8,128)(2,1)S(1)} %broadcast_in_dim.6), channel_id=1, replica_groups=mesh['z_lo'=4,'x'=4,'core'=2,'z_hi'=4,'y'=4] {'z_hi'}, dimensions={0} | all-to-all | bytes 393216 | tf_op jit(solution)/shard_map/all_to_all | solution.py:166
  33.3 17.6 %all_to_all.31 = bf16[4,32,3072]{2,1,0:T(8,128)(2,1)S(1)} all-to-all(bf16[4,32,3072]{2,1,0:T(8,128)(2,1)S(1)} %broadcast_in_dim.15), channel_id=1, replica_groups={{0,128,256,384},{16,17,18,19},{1,129,257,385},{144,145,146,147},{2,130,..., dimensions={0} | all-to-all | bytes 1572864 | tf_op jit(solution)/shard_map/all_to_all | solution.py:167
  51.0 2.1 %collective-permute-start.3 = (bf16[128,3072]{1,0:T(8,128)(2,1)S(1)}, bf16[128,3072]{1,0:T(8,128)(2,1)}, u32[]{:S(2)}, u32[]{:S(2)}) collective-permute-start(bf16[128,3072]{1,0:T(8,128)(2,1)S(1)} %bitcast.10), channel_id=1, source_target_pairs={{0,1},{1,2},{2,3},{3,0},{4,5},{5,6},{6,7},{7,4},{8,9},{9,10},{10,1... | collective-permute-start | bytes 2359304 | tf_op jit(solution)/shard_map/ppermute | solution.py:59
  53.1 3.7 %collective-permute-start = (bf16[128,3072]{1,0:T(8,128)(2,1)S(1)}, bf16[128,3072]{1,0:T(8,128)(2,1)}, u32[]{:S(2)}, u32[]{:S(2)}) collective-permute-start(bf16[128,3072]{1,0:T(8,128)(2,1)S(1)} %bitcast.11), channel_id=1, source_target_pairs={{0,3},{1,0},{2,1},{3,2},{4,7},{5,4},{6,5},{7,6},{8,11},{9,8},{10,9... | collective-permute-start | bytes 2359304 | tf_op jit(solution)/shard_map/ppermute | solution.py:59
  57.8 3.1 %collective-permute-start.1 = (bf16[64,3072]{1,0:T(8,128)(2,1)}, bf16[64,3072]{1,0:T(8,128)(2,1)S(1)}, u32[]{:S(2)}, u32[]{:S(2)}) collective-permute-start(bf16[64,3072]{1,0:T(8,128)(2,1)} %bitcast.4), channel_id=1, source_target_pairs={{0,2},{1,3},{2,0},{3,1},{4,6},{5,7},{6,4},{7,5},{8,10},{9,11},{10,... | collective-permute-start | bytes 1179656 | tf_op jit(solution)/shard_map/ppermute | solution.py:59
  60.9 4.2 %collective-permute-start.2 = (bf16[64,3072]{1,0:T(8,128)(2,1)}, bf16[64,3072]{1,0:T(8,128)(2,1)}, u32[]{:S(2)}, u32[]{:S(2)}) collective-permute-start(bf16[64,3072]{1,0:T(8,128)(2,1)} %bitcast.5), channel_id=1, source_target_pairs={{0,2},{1,3},{2,0},{3,1},{4,6},{5,7},{6,4},{7,5},{8,10},{9,11},{10,... | collective-permute-start | bytes 1179656 | tf_op jit(solution)/shard_map/ppermute | solution.py:59
  65.2 7.1 %collective-permute-done.1.p2a = bf16[64,3072]{1,0:T(8,128)(2,1)S(1)} collective-permute-done((bf16[64,3072]{1,0:T(8,128)(2,1)}, bf16[64,3072]{1,0:T(8,128)(2,1)S(1)}, u32[]{:S(2)}, u32[]{:S(2)}) %collective-permute-start.1) | collective-permute-done | bytes 393248 | tf_op jit(solution)/shard_map/ppermute | solution.py:59
  72.3 4.3 %collective-permute-done.2.p2b = bf16[64,3072]{1,0:T(8,128)(2,1)} collective-permute-done((bf16[64,3072]{1,0:T(8,128)(2,1)}, bf16[64,3072]{1,0:T(8,128)(2,1)}, u32[]{:S(2)}, u32[]{:S(2)}) %collective-permute-start.2) | collective-permute-done | bytes 393248 | tf_op jit(solution)/shard_map/ppermute | solution.py:59
  76.7 3.6 %shard_map.75 = (bf16[512,3072]{1,0:T(8,128)(2,1)S(1)}, f32[256,768]{1,0:T(8,128)S(1)}, f32[256,768]{1,0:T(8,128)S(1)}) custom-call(s32[2]{0:T(128)S(1)} %pad_add_fusion.place, bf16[128,3072]{1,0:T(8,128)(2,1)S(1)} %bitcast.12, bf16[128,3072]{1,0:T(8,128)(2,1)} %collective-permute-done.p1, bf16[64,3072]{1,0:T(8,128)(2,1)S(1)} %collective-permute-done.1.p2a, ...), custom_call_target="tpu_custom_call" | custom-call | tf_op jit(solution)/shard_map/pallas_call | solution.py:174
  82.3 2.3 %collective-permute-done.4 = f32[256,768]{1,0:T(8,128)S(1)} collective-permute-done((f32[256,768]{1,0:T(8,128)S(1)}, f32[256,768]{1,0:T(8,128)S(1)}, u32[]{:S(2)}, u32[]{:S(2)}) %collective-permute-start.4) | collective-permute-done | bytes 786464 | tf_op jit(solution)/shard_map/ppermute | solution.py:186
  84.7 16.7 %all_to_all.32.parts = f32[4,64,768]{2,1,0:T(8,128)S(1)} all-to-all(f32[4,64,768]{2,1,0:T(8,128)S(1)} %bitcast.14), channel_id=1, replica_groups=mesh['z_lo'=4,'x'=4,'core'=2,'z_hi'=4,'y'=4] {'x'}, dimensions={0} | all-to-all | bytes 1572864 | tf_op jit(solution)/shard_map/all_to_all | solution.py:187
  101.5 9.8 %all_to_all.33 = bf16[4,64,768]{2,1,0:T(8,128)(2,1)S(1)} all-to-all(bf16[4,64,768]{2,1,0:T(8,128)(2,1)S(1)} %shard_map.76), channel_id=1, replica_groups=mesh['z_lo'=4,'x'=4,'core'=2,'z_hi'=4,'y'=4] {'x'}, dimensions={0} | all-to-all | bytes 786432 | tf_op jit(solution)/shard_map/all_to_all | solution.py:195
  111.2 2.4 %all_gather.3.shares = bf16[512,768]{1,0:T(8,128)(2,1)S(1)} all-gather(bf16[256,768]{1,0:T(8,128)(2,1)S(1)} %bitcast.15), channel_id=1, replica_groups=mesh['z_lo'=4,'x'=4,'core'=2,'z_hi'=4,'y'=4] {'core'}, dimensions={0}, use_global_device_ids=true | all-gather | bytes 1179648 | tf_op jit(solution)/shard_map/all_gather | solution.py:196
  113.6 2.4 %shard_map.77 = (f32[128,3072]{1,0:T(8,128)S(1)}, bf16[128,3072]{1,0:T(8,128)(2,1)S(1)}, bf16[64,3072]{1,0:T(8,128)(2,1)S(1)}, bf16[64,3072]{1,0:T(8,128)(2,1)S(...) custom-call(s32[2]{0:T(128)S(1)} %pad_add_fusion.place, bf16[512,768]{1,0:T(8,128)(2,1)S(1)} %all_gather.3.shares, ...), custom_call_target="tpu_custom_call" | custom-call | tf_op jit(solution)/shard_map/pallas_call | solution.py:197
  117.9 3.9 %collective-permute-start.6 = (bf16[128,3072]{1,0:T(8,128)(2,1)S(1)}, bf16[128,3072]{1,0:T(8,128)(2,1)S(1)}, u32[]{:S(2)}, u32[]{:S(2)}) collective-permute-start(bf16[128,3072]{1,0:T(8,128)(2,1)S(1)} %get-tuple-element.17), channel_id=1, source_target_pairs={{0,3},{1,0},{2,1},{3,2},{4,7},{5,4},{6,5},{7,6},{8,11},{9,8},{10,9... | collective-permute-start | bytes 2359304 | tf_op jit(solution)/shard_map/ppermute | solution.py:59
  121.8 4.0 %collective-permute-start.7 = (bf16[64,3072]{1,0:T(8,128)(2,1)S(1)}, bf16[64,3072]{1,0:T(8,128)(2,1)S(1)}, u32[]{:S(2)}, u32[]{:S(2)}) collective-permute-start(bf16[64,3072]{1,0:T(8,128)(2,1)S(1)} %get-tuple-element.18), channel_id=1, source_target_pairs={{0,2},{1,3},{2,0},{3,1},{4,6},{5,7},{6,4},{7,5},{8,10},{9,11},{10,... | collective-permute-start | bytes 1179656 | tf_op jit(solution)/shard_map/ppermute | solution.py:59
  125.8 3.3 %collective-permute-start.8 = (bf16[64,3072]{1,0:T(8,128)(2,1)S(1)}, bf16[64,3072]{1,0:T(8,128)(2,1)S(1)}, u32[]{:S(2)}, u32[]{:S(2)}) collective-permute-start(bf16[64,3072]{1,0:T(8,128)(2,1)S(1)} %get-tuple-element.19), channel_id=1, source_target_pairs={{0,2},{1,3},{2,0},{3,1},{4,6},{5,7},{6,4},{7,5},{8,10},{9,11},{10,... | collective-permute-start | bytes 1179656 | tf_op jit(solution)/shard_map/ppermute | solution.py:59
  129.2 8.9 %collective-permute-done.7 = bf16[64,3072]{1,0:T(8,128)(2,1)S(1)} collective-permute-done((bf16[64,3072]{1,0:T(8,128)(2,1)S(1)}, bf16[64,3072]{1,0:T(8,128)(2,1)S(1)}, u32[]{:S(2)}, u32[]{:S(2)}) %collective-permute-start.7) | collective-permute-done | bytes 393248 | tf_op jit(solution)/shard_map/ppermute | solution.py:59
  138.1 4.2 %collective-permute-done.8 = bf16[64,3072]{1,0:T(8,128)(2,1)S(1)} collective-permute-done((bf16[64,3072]{1,0:T(8,128)(2,1)S(1)}, bf16[64,3072]{1,0:T(8,128)(2,1)S(1)}, u32[]{:S(2)}, u32[]{:S(2)}) %collective-permute-start.8) | collective-permute-done | bytes 393248 | tf_op jit(solution)/shard_map/ppermute | solution.py:59
  142.8 18.2 %all_to_all.34 = bf16[4,32,3072]{2,1,0:T(8,128)(2,1)} all-to-all(bf16[4,32,3072]{2,1,0:T(8,128)(2,1)S(1)} %bitcast.13), channel_id=1, replica_groups={{0,128,256,384},{16,17,18,19},{1,129,257,385},{144,145,146,147},{2,130,..., dimensions={0} | all-to-all | bytes 1572864 | tf_op jit(solution)/shard_map/all_to_all | solution.py:221
  162.9 3.4 %all-to-all-start.5 = ((bf16[4,8,3072]{2,1,0:T(8,128)(2,1)}), bf16[4,8,3072]{2,1,0:T(8,128)(2,1)S(1)}, u32[]{:S(2)}, u32[]{:S(2)}) async-start(bf16[4,8,3072]{2,1,0:T(8,128)(2,1)} %bitcast.9), calls=%async_computation.5 | async-start | bytes 393216 | tf_op jit(solution)/shard_map/all_to_all | solution.py:222
  166.3 2.9 %convolution_convert_fusion = bf16[384,1536]{1,0:T(8,128)(2,1)} fusion(bf16[512,3072]{1,0:T(8,128)(2,1)S(1)} %copy-done.3, bf16[512,768]{1,0:T(8,128)(2,1)} %copy-done.4), kind=kOutput, calls=%fused_computation | convolution fusion | flops 604569600 | bytes 3145728 | tf_op jit(solution)/shard_map/dot_general | solution.py:63
  169.2 2.0 %convolution_convert_fusion.1 = bf16[1536,384]{1,0:T(8,128)(2,1)} fusion(bf16[512,3072]{1,0:T(8,128)(2,1)S(1)} %copy-done.3, bf16[512,768]{1,0:T(8,128)(2,1)S(1)} %copy-done.5), kind=kOutput, calls=%fused_computation.1 | convolution fusion | flops 604569600 | bytes 3145728 | tf_op jit(solution)/shard_map/dot_general | solution.py:63
  171.2 8.6 %all-to-all-done.5 = bf16[4,8,3072]{2,1,0:T(8,128)(2,1)S(1)} async-done(((bf16[4,8,3072]{2,1,0:T(8,128)(2,1)}), bf16[4,8,3072]{2,1,0:T(8,128)(2,1)S(1)}, u32[]{:S(2)}, u32[]{:S(2)}) %all-to-all-start.5) | async-done | bytes 196640 | tf_op jit(solution)/shard_map/all_to_all | solution.py:222
  (29 shorter events, 9.1 us)
Async XLA Ops:
  33.3 43.4 %copy-start = (bf16[1536,384]{1,0:T(8,128)(2,1)S(1)}, bf16[1536,384]{1,0:T(8,128)(2,1)}, u32[]{:S(2)}) copy-start(bf16[1536,384]{1,0:T(8,128)(2,1)} %first.3) | copy-start | bytes 3538948
  33.3 43.4 %copy-start.1 = (bf16[384,1536]{1,0:T(8,128)(2,1)S(1)}, bf16[384,1536]{1,0:T(8,128)(2,1)}, u32[]{:S(2)}) copy-start(bf16[384,1536]{1,0:T(8,128)(2,1)} %second.3) | copy-start | bytes 3538948
  51.0 25.7 %collective-permute-start.3 = (bf16[128,3072]{1,0:T(8,128)(2,1)S(1)}, bf16[128,3072]{1,0:T(8,128)(2,1)}, u32[]{:S(2)}, u32[]{:S(2)}) collective-permute-start(bf16[128,3072]{1,0:T(8,128)(2,1)S(1)} %bitcast.10), channel_id=1, source_target_pairs={{0,1},{1,2},{2,3},{3,0},{4,5},{5,6},{6,7},{7,4},{8,9},{9,10},{10,1... | collective-permute-start | bytes 2359304 | tf_op jit(solution)/shard_map/ppermute | solution.py:59
  53.1 23.6 %collective-permute-start = (bf16[128,3072]{1,0:T(8,128)(2,1)S(1)}, bf16[128,3072]{1,0:T(8,128)(2,1)}, u32[]{:S(2)}, u32[]{:S(2)}) collective-permute-start(bf16[128,3072]{1,0:T(8,128)(2,1)S(1)} %bitcast.11), channel_id=1, source_target_pairs={{0,3},{1,0},{2,1},{3,2},{4,7},{5,4},{6,5},{7,6},{8,11},{9,8},{10,9... | collective-permute-start | bytes 2359304 | tf_op jit(solution)/shard_map/ppermute | solution.py:59
  57.8 14.6 %collective-permute-start.1 = (bf16[64,3072]{1,0:T(8,128)(2,1)}, bf16[64,3072]{1,0:T(8,128)(2,1)S(1)}, u32[]{:S(2)}, u32[]{:S(2)}) collective-permute-start(bf16[64,3072]{1,0:T(8,128)(2,1)} %bitcast.4), channel_id=1, source_target_pairs={{0,2},{1,3},{2,0},{3,1},{4,6},{5,7},{6,4},{7,5},{8,10},{9,11},{10,... | collective-permute-start | bytes 1179656 | tf_op jit(solution)/shard_map/ppermute | solution.py:59
  60.9 15.7 %collective-permute-start.2 = (bf16[64,3072]{1,0:T(8,128)(2,1)}, bf16[64,3072]{1,0:T(8,128)(2,1)}, u32[]{:S(2)}, u32[]{:S(2)}) collective-permute-start(bf16[64,3072]{1,0:T(8,128)(2,1)} %bitcast.5), channel_id=1, source_target_pairs={{0,2},{1,3},{2,0},{3,1},{4,6},{5,7},{6,4},{7,5},{8,10},{9,11},{10,... | collective-permute-start | bytes 1179656 | tf_op jit(solution)/shard_map/ppermute | solution.py:59
  80.4 21.0 %copy-start.2 = (bf16[512,3072]{1,0:T(8,128)(2,1)}, bf16[512,3072]{1,0:T(8,128)(2,1)S(1)}, u32[]{:S(2)}) copy-start(bf16[512,3072]{1,0:T(8,128)(2,1)S(1)} %get-tuple-element.20) | copy-start | bytes 9437188
  80.4 4.2 %collective-permute-start.4 = (f32[256,768]{1,0:T(8,128)S(1)}, f32[256,768]{1,0:T(8,128)S(1)}, u32[]{:S(2)}, u32[]{:S(2)}) collective-permute-start(f32[256,768]{1,0:T(8,128)S(1)} %get-tuple-element.14), channel_id=1, source_target_pairs={{0,16},{16,0},{1,17},{17,1},{2,18},{18,2},{3,19},{19,3},{4,20},{20... | collective-permute-start | bytes 2359304 | tf_op jit(solution)/shard_map/ppermute | solution.py:186
  116.0 26.8 %copy-start.4 = (bf16[512,768]{1,0:T(8,128)(2,1)}, bf16[512,768]{1,0:T(8,128)(2,1)S(1)}, u32[]{:S(2)}) copy-start(bf16[512,768]{1,0:T(8,128)(2,1)S(1)} %get-tuple-element.21) | copy-start | bytes 2359300
  116.0 26.3 %collective-permute-start.5 = (bf16[128,3072]{1,0:T(8,128)(2,1)S(1)}, bf16[128,3072]{1,0:T(8,128)(2,1)S(1)}, u32[]{:S(2)}, u32[]{:S(2)}) collective-permute-start(bf16[128,3072]{1,0:T(8,128)(2,1)S(1)} %get-tuple-element.16), channel_id=1, source_target_pairs={{0,1},{1,2},{2,3},{3,0},{4,5},{5,6},{6,7},{7,4},{8,9},{9,10},{10,1... | collective-permute-start | bytes 2359304 | tf_op jit(solution)/shard_map/ppermute | solution.py:59
  117.9 24.4 %collective-permute-start.6 = (bf16[128,3072]{1,0:T(8,128)(2,1)S(1)}, bf16[128,3072]{1,0:T(8,128)(2,1)S(1)}, u32[]{:S(2)}, u32[]{:S(2)}) collective-permute-start(bf16[128,3072]{1,0:T(8,128)(2,1)S(1)} %get-tuple-element.17), channel_id=1, source_target_pairs={{0,3},{1,0},{2,1},{3,2},{4,7},{5,4},{6,5},{7,6},{8,11},{9,8},{10,9... | collective-permute-start | bytes 2359304 | tf_op jit(solution)/shard_map/ppermute | solution.py:59
  121.8 16.3 %collective-permute-start.7 = (bf16[64,3072]{1,0:T(8,128)(2,1)S(1)}, bf16[64,3072]{1,0:T(8,128)(2,1)S(1)}, u32[]{:S(2)}, u32[]{:S(2)}) collective-permute-start(bf16[64,3072]{1,0:T(8,128)(2,1)S(1)} %get-tuple-element.18), channel_id=1, source_target_pairs={{0,2},{1,3},{2,0},{3,1},{4,6},{5,7},{6,4},{7,5},{8,10},{9,11},{10,... | collective-permute-start | bytes 1179656 | tf_op jit(solution)/shard_map/ppermute | solution.py:59
  125.8 16.5 %collective-permute-start.8 = (bf16[64,3072]{1,0:T(8,128)(2,1)S(1)}, bf16[64,3072]{1,0:T(8,128)(2,1)S(1)}, u32[]{:S(2)}, u32[]{:S(2)}) collective-permute-start(bf16[64,3072]{1,0:T(8,128)(2,1)S(1)} %get-tuple-element.19), channel_id=1, source_target_pairs={{0,2},{1,3},{2,0},{3,1},{4,6},{5,7},{6,4},{7,5},{8,10},{9,11},{10,... | collective-permute-start | bytes 1179656 | tf_op jit(solution)/shard_map/ppermute | solution.py:59
  142.3 24.0 %copy-start.3 = (bf16[512,3072]{1,0:T(8,128)(2,1)S(1)}, bf16[512,3072]{1,0:T(8,128)(2,1)}, u32[]{:S(2)}) copy-start(bf16[512,3072]{1,0:T(8,128)(2,1)} %copy-done.2) | copy-start | bytes 9437188
  162.9 16.9 %all-to-all-start.5 = ((bf16[4,8,3072]{2,1,0:T(8,128)(2,1)}), bf16[4,8,3072]{2,1,0:T(8,128)(2,1)S(1)}, u32[]{:S(2)}, u32[]{:S(2)}) async-start(bf16[4,8,3072]{2,1,0:T(8,128)(2,1)} %bitcast.9), calls=%async_computation.5 | async-start | bytes 393216 | tf_op jit(solution)/shard_map/all_to_all | solution.py:222
  166.3 2.9 %copy-start.5 = (bf16[512,768]{1,0:T(8,128)(2,1)S(1)}, bf16[512,768]{1,0:T(8,128)(2,1)}, u32[]{:S(2)}) copy-start(bf16[512,768]{1,0:T(8,128)(2,1)} %copy-done.4) | copy-start | bytes 2359300

commit v3 on v2

v3 whole, which is shorter than its diff:
```python
import math

import jax
import jax.numpy as jnp
from jax import lax
from jax.experimental import pallas as pl
from jax.experimental.pallas import tpu as pltpu
from jax.sharding import Mesh, PartitionSpec as P

root_scale = math.sqrt(2.0 / math.pi)
cubic_coef = 0.044715

GRID = ("z_lo", "x", "core", "z_hi", "y")
SIZES = (4, 4, 2, 4, 4)
ROW = ("x", "core")
SWAP = ((0, 1), (1, 0))
BLOCK = 32
PIECE = 128
SHARE = 64
LONG = 64
SHORT = PIECE - LONG
ORDER = (0, 1, 3, 2)
params = pltpu.CompilerParams(vmem_limit_bytes=20 << 20)


def place_of(z_lo, x, core, z_hi, y):
    return (((z_lo * 4 + x) * 2 + core) * 4 + z_hi) * 4 + y


def every_place():
    for z_lo in range(4):
        for x in range(4):
            for core in range(2):
                for z_hi in range(4):
                    for y in range(4):
                        yield z_lo, x, core, z_hi, y


def near_groups():
    groups = []
    for x in range(4):
        for z_hi in range(4):
            for other in range(4):
                groups.append([place_of(i, x, 0, z_hi, other) for i in range(4)])
                groups.append([place_of(other, x, 1, z_hi, i) for i in range(4)])
    return groups


def far_shift(step):
    pairs = []
    for z_lo, x, core, z_hi, y in every_place():
        if core == 0:
            target = place_of(z_lo, x, core, z_hi, (y + step) % 4)
        else:
            z = (z_hi * 4 + z_lo + step) % 16
            target = place_of(z % 4, x, core, z // 4, y)
        pairs.append((place_of(z_lo, x, core, z_hi, y), target))
    return pairs


def moved(value, step):
    return lax.ppermute(value, GRID, far_shift(step))


def dot_over(left_side, right_side, left_dim, right_dim):
    return lax.dot_general(
        left_side,
        right_side,
        (((left_dim,), (right_dim,)), ((), ())),
        preferred_element_type=jnp.float32,
    )


def copies_of(block, count):
    return jnp.broadcast_to(block[None], (count,) + block.shape)


def common_block(core, own, piece, part):
    index = lax.rem(own + piece, 4)
    return jnp.where(core == 0, index * 4 + part, part * 4 + index)


def first_kernel(p0, first, second, sums):
    width = first.shape[0]
    units = first.shape[1]
    sums[:, :units] = dot_over(p0[:, :width], first[...], 1, 0)
    sums[:, units:] = dot_over(p0[:, width:], second[...], 1, 1)


def last_kernel(place, sums, p1, p3, p2a, p2b, first, second, both, kept, given, rest):
    core, own = place[0], place[1]
    width = first.shape[0]
    units = first.shape[1]
    both[0:128, :] = p1[...]
    both[128:256, :] = p3[...]
    both[256 : 256 + SHORT, :] = p2a[...]
    both[256 + SHORT : 384, :] = p2b[...]
    rest[:, :units] = dot_over(both[:, :width], first[...], 1, 0)
    rest[:, units:] = dot_over(both[:, width:], second[...], 1, 1)
    for slot in range(4):
        source, base = (sums, 0) if slot == 0 else (rest, PIECE)
        for part in range(4):
            block = common_block(core, own, ORDER[slot], part)
            start = pl.multiple_of(lax.rem(block, 8) * BLOCK, BLOCK)
            at = (slot * 4 + part) * BLOCK - base
            mine = block // 8 == core

            @pl.when(mine)
            def _():
                kept[pl.ds(start, BLOCK), :] = source[at : at + BLOCK, :]

            @pl.when(jnp.logical_not(mine))
            def _():
                given[pl.ds(start, BLOCK), :] = source[at : at + BLOCK, :]


def add_kernel(kept, more, total, sent):
    values = kept[...] + more[...]
    total[...] = values
    sent[...] = values.astype(jnp.bfloat16)


def lost(values):
    return values - values.astype(jnp.bfloat16).astype(jnp.float32)


def total_of(parts, own_lost):
    wide = [parts[i].astype(jnp.float32) for i in range(4)]
    return ((wide[0] + wide[1]) + (wide[2] + wide[3])) + own_lost


def gelu_kernel(place, parts, kept, shares):
    units = shares.shape[2] // 2
    total = total_of(parts, lost(kept[place[2]]))
    values, slopes = total[:, :units], total[:, units:]
    square = values * values
    tangent = jnp.tanh(root_scale * (values + cubic_coef * values * square))
    hidden = 0.5 * values * (1.0 + tangent)
    slope = 0.5 * (1.0 + tangent) + 0.5 * values * (1.0 - tangent * tangent) * root_scale * (
        1.0 + 3.0 * cubic_coef * square
    )
    pre = slopes * slope
    for copy in range(4):
        shares[copy, :, :units] = hidden.astype(jnp.bfloat16)
        shares[copy, :, units:] = pre.astype(jnp.bfloat16)


def out_rows(rows, first, second):
    units = first.shape[1]
    return (
        dot_over(rows[:, :units], second[...], 1, 0),
        dot_over(rows[:, units:], first[...], 1, 1),
    )


def second_kernel(place, shares, first, second, o1, o2a, o2b, o3, local):
    core, own = place[0], place[1]
    width = first.shape[0]
    for slot in range(4):
        for part in range(4):
            block = common_block(core, own, ORDER[slot], part)
            start = pl.multiple_of(block * BLOCK, BLOCK)
            at = (slot * 4 + part) * BLOCK
            local[at : at + BLOCK, :] = shares[pl.ds(start, BLOCK), :]
    sides = out_rows(local[128:512, :], first, second)
    for side in range(2):
        outs = sides[side].astype(jnp.bfloat16)
        columns = slice(side * width, (side + 1) * width)
        o1[:, columns] = outs[0:128]
        o3[:, columns] = outs[128:256]
        o2a[:, columns] = outs[256 : 256 + LONG]
        o2b[:, columns] = outs[256 + LONG : 384]


def own_kernel(local, first, second, o0):
    width = first.shape[0]
    sides = out_rows(local[0:128, :], first, second)
    o0[:, :width] = sides[0]
    o0[:, width:] = sides[1]


def far_kernel(place, o0, r1, r2a, r2b, r3, outs, own_lost):
    for part in range(4):
        rows = slice(part * BLOCK, (part + 1) * BLOCK)
        if part < 2:
            r2 = r2a[rows, :]
        else:
            r2 = r2b[part * BLOCK - LONG : part * BLOCK - LONG + BLOCK, :]
        total = o0[rows, :] + r1[rows, :].astype(jnp.float32)
        total = total + r3[rows, :].astype(jnp.float32) + r2.astype(jnp.float32)
        outs[part] = total.astype(jnp.bfloat16)

        @pl.when(place[3] == part)
        def _():
            own_lost[...] = lost(total)


def near_kernel(place, parts, own_lost, outs, next_lost):
    total = total_of(parts, own_lost[...])
    outs[...] = total.astype(jnp.bfloat16)
    for part in range(4):

        @pl.when(place[4] == part)
        def _():
            next_lost[...] = lost(total[part * 8 : part * 8 + 8, :])


def end_kernel(parts, own_lost, block_out, input_grad):
    width = block_out.shape[1]
    outs = total_of(parts, own_lost[...]).astype(jnp.bfloat16)
    block_out[...] = outs[:, :width]
    input_grad[...] = outs[:, width:]


def shape_of(rows, columns, dtype):
    return jax.ShapeDtypeStruct((rows, columns), dtype)


def cost_of(rows):
    return pl.CostEstimate(
        flops=4 * rows * 1536 * 384, bytes_accessed=rows * 12288 + 2400000, transcendentals=0
    )


def on_device(tokens, first_weight, second_weight, grad_out):
    width = tokens.shape[1]
    units = first_weight.shape[1]
    core = lax.axis_index("core")
    y, z_lo = lax.axis_index("y"), lax.axis_index("z_lo")
    own, other = jnp.where(core == 0, y, z_lo), jnp.where(core == 0, z_lo, y)
    x, z_hi = lax.axis_index("x"), lax.axis_index("z_hi")
    place = jnp.stack([core, own, x, other, z_hi]).astype(jnp.int32)
    scalars = pl.BlockSpec(memory_space=pltpu.SMEM)
    whole = pl.BlockSpec(memory_space=pltpu.VMEM)
    near = near_groups()

    both = jnp.concatenate([tokens, grad_out], axis=1)
    both = lax.all_to_all(copies_of(both, 4), "z_hi", 0, 0).reshape(BLOCK, 2 * width)
    both = lax.all_to_all(copies_of(both, 4), GRID, 0, 0, axis_index_groups=near)
    both = both.reshape(PIECE, 2 * width)
    p3 = moved(both, 1)
    p1 = moved(both, -1)
    p2b = moved(both[SHORT:], 2)
    p2a = moved(both[:SHORT], -2)

    sums = pl.pallas_call(
        first_kernel,
        out_shape=shape_of(PIECE, 2 * units, jnp.float32),
        in_specs=[whole] * 3,
        out_specs=whole,
        compiler_params=params,
        cost_estimate=cost_of(128),
    )(both, first_weight, second_weight)
    every, kept, given = pl.pallas_call(
        last_kernel,
        out_shape=(
            shape_of(384, 2 * width, jnp.bfloat16),
            shape_of(256, 2 * units, jnp.float32),
            shape_of(256, 2 * units, jnp.float32),
        ),
        in_specs=[scalars] + [whole] * 7,
        out_specs=(whole, whole, whole),
        scratch_shapes=[pltpu.VMEM((384, 2 * units), jnp.float32)],
        compiler_params=params,
        cost_estimate=cost_of(384),
    )(place, sums, p1, p3, p2a, p2b, first_weight, second_weight)
    kept, sent = pl.pallas_call(
        add_kernel,
        out_shape=(
            shape_of(256, 2 * units, jnp.float32),
            shape_of(256, 2 * units, jnp.bfloat16),
        ),
        in_specs=[whole] * 2,
        out_specs=(whole, whole),
        compiler_params=params,
    )(kept, lax.ppermute(given, "core", SWAP))
    parts = lax.all_to_all(sent.reshape(4, SHARE, 2 * units), "x", 0, 0)
    shares = pl.pallas_call(
        gelu_kernel,
        out_shape=jax.ShapeDtypeStruct((4, SHARE, 2 * units), jnp.bfloat16),
        in_specs=[scalars, whole, whole],
        out_specs=whole,
        compiler_params=params,
    )(place, parts, kept.reshape(4, SHARE, 2 * units))
    shares = lax.all_to_all(shares, "x", 0, 0).reshape(256, 2 * units)
    shares = lax.all_gather(shares, "core", axis=0, tiled=True)
    o1, o2a, o2b, o3, local = pl.pallas_call(
        second_kernel,
        out_shape=(
            shape_of(PIECE, 2 * width, jnp.bfloat16),
            shape_of(LONG, 2 * width, jnp.bfloat16),
            shape_of(SHORT, 2 * width, jnp.bfloat16),
            shape_of(PIECE, 2 * width, jnp.bfloat16),
            shape_of(512, 2 * units, jnp.bfloat16),
        ),
        in_specs=[scalars] + [whole] * 3,
        out_specs=(whole,) * 5,
        compiler_params=params,
        cost_estimate=cost_of(384),
    )(place, shares, first_weight, second_weight)
    r1 = moved(o1, 1)
    r3 = moved(o3, -1)
    r2a = moved(o2a, 2)
    r2b = moved(o2b, -2)
    o0 = pl.pallas_call(
        own_kernel,
        out_shape=shape_of(PIECE, 2 * width, jnp.float32),
        in_specs=[whole] * 3,
        out_specs=whole,
        compiler_params=params,
        cost_estimate=cost_of(128),
    )(local, first_weight, second_weight)
    hidden, grad_pre = local[:, :units], local[:, units:]
    first_grad = dot_over(every[:, :width], grad_pre[PIECE:], 0, 0)
    first_grad = first_grad + dot_over(both[:, :width], grad_pre[:PIECE], 0, 0)
    second_grad = dot_over(hidden[PIECE:], every[:, width:], 0, 0)
    second_grad = second_grad + dot_over(hidden[:PIECE], both[:, width:], 0, 0)
    first_grad = first_grad.astype(jnp.bfloat16)
    second_grad = second_grad.astype(jnp.bfloat16)
    o0, first_grad, second_grad = lax.optimization_barrier((o0, first_grad, second_grad))
    outs, own_lost = pl.pallas_call(
        far_kernel,
        out_shape=(
            jax.ShapeDtypeStruct((4, BLOCK, 2 * width), jnp.bfloat16),
            shape_of(BLOCK, 2 * width, jnp.float32),
        ),
        in_specs=[scalars] + [whole] * 5,
        out_specs=(whole, whole),
        compiler_params=params,
    )(place, o0, r1, r2a, r2b, r3)
    outs = lax.all_to_all(outs, GRID, 0, 0, axis_index_groups=near)
    outs, own_lost = pl.pallas_call(
        near_kernel,
        out_shape=(
            shape_of(BLOCK, 2 * width, jnp.bfloat16),
            shape_of(8, 2 * width, jnp.float32),
        ),
        in_specs=[scalars, whole, whole],
        out_specs=(whole, whole),
        compiler_params=params,
    )(place, outs, own_lost)
    outs = lax.all_to_all(outs.reshape(4, 8, 2 * width), "z_hi", 0, 0)
    block_out, input_grad = pl.pallas_call(
        end_kernel,
        out_shape=(shape_of(8, width, jnp.bfloat16), shape_of(8, width, jnp.bfloat16)),
        in_specs=[whole, whole],
        out_specs=(whole, whole),
        compiler_params=params,
    )(outs, own_lost)
    return (block_out, input_grad, first_grad, second_grad)


def solution(mesh):
    grid = Mesh(mesh.devices.reshape(SIZES), GRID)
    rows = P(("z_lo", "z_hi", "y"), ROW)
    columns = P(ROW, ("z_lo", "z_hi", "y"))
    return jax.shard_map(
        on_device,
        mesh=grid,
        in_specs=(rows, columns, rows, rows),
        out_specs=(rows, rows, columns, rows),
        check_vma=False,
    )
```

time: 181 us -> 179 us (0.989)
  waiting for transfers between devices: 35.5 us -> 20.3 us
  blocking collectives: 96.4 us -> 109 us
  Pallas kernels: 6.09 us -> 9.61 us
  other arithmetic: 3.36 us -> 0.76 us
    all_to_all x2 -> x3, blocking collectives: 34.8 us -> 46.2 us  [the longest x1 17.2 us: on_device(): outs = lax.all_to_all(outs.reshape(4, 8, 2 * width), 'z_hi', 0, 0)]
    all_to_all x1 -> x0, waiting for transfers between devices: 8.56 us -> none  [on_device(): outs = summed(lax.all_to_all(outs.reshape(4, 8, 2 * width), 'z_hi', 0, 0))]
    ppermute x8, waiting for transfers between devices: 24.7 us -> 18 us  [moved(): return lax.ppermute(value, GRID, far_shift(step))]
    pallas_call x3 -> x9, Pallas kernels: 6.09 us -> 9.61 us  [the longest x1 3.21 us: on_device(): pl.pallas_call(last_kernel, out_shape=(shape_of(384, 2 * width, jnp.bfloa...]
    all_to_all x1 -> x0, starting transfers between devices: 3.36 us -> none  [on_device(): outs = summed(lax.all_to_all(outs.reshape(4, 8, 2 * width), 'z_hi', 0, 0))]
    ppermute x8, starting transfers between devices: 26.4 us -> 29.3 us  [moved(): return lax.ppermute(value, GRID, far_shift(step))]
    reduce_sum x2 -> x0, other arithmetic: 2 us -> none  [summed(): return jnp.sum(parts.astype(jnp.float32), axis=0).astype(jnp.bfloat16)]
    dot_general x2 -> x4, matrix products: 4.92 us -> 4.79 us  [dot_over(): lax.dot_general(left_side, right_side, (((left_dim,), (right_dim,)), ((),...]
  transfers between devices with their start and end apart: 10 -> 9, of which waited for: 7 -> 7; matrix products, arithmetic and copies ran while one was open for 3% -> 3% of each run, Pallas kernels for 0% -> 1%
where the time goes in v3:
time: 179 us; the launch traced here: 178 us
  blocking collectives  109 us (61%)
  starting transfers between devices  31.2 us (17%)
  waiting for transfers between devices  20.3 us (11%)
  Pallas kernels  9.61 us (5%)
  matrix products  4.79 us (3%)
    all_to_all x1, blocking collectives, on_device(): lax.all_to_all(copies_of(both, 4), 'z_hi', 0, 0).reshape(BLOCK, 2 * width)  32 us
    ppermute x8, starting transfers between devices, moved(): return lax.ppermute(value, GRID, far_shift(step))  29.3 us
    all_to_all x1, blocking collectives, on_device(): lax.all_to_all(copies_of(both, 4), GRID, 0, 0, axis_index_groups=near)  19 us
    ppermute x8, waiting for transfers between devices, moved(): return lax.ppermute(value, GRID, far_shift(step))  18 us
    all_to_all x1, blocking collectives, on_device(): outs = lax.all_to_all(outs.reshape(4, 8, 2 * width), 'z_hi', 0, 0)  17.2 us
    all_to_all x1, blocking collectives, on_device(): outs = lax.all_to_all(outs, GRID, 0, 0, axis_index_groups=near)  16.6 us
    all_to_all x1, blocking collectives, on_device(): parts = lax.all_to_all(sent.reshape(4, SHARE, 2 * units), 'x', 0, 0)  12.5 us
    all_to_all x1, blocking collectives, on_device(): shares = lax.all_to_all(shares, 'x', 0, 0).reshape(256, 2 * units)  9.77 us
  transfers between devices with their start and end apart: 9, of which 7 were waited for; matrix products, arithmetic and copies ran while one was open for 3% of the time, Pallas kernels for 1%

profile of v3, /device:TPU:24, one launch (start us, length us, event | category | flops | bytes accessed | tf_op | source)
XLA Modules:
  0.0 177.9 jit_solution(11869118055099571977)
XLA Ops:
  1.4 32.0 %all_to_all.30 = bf16[4,8,3072]{2,1,0:T(8,128)(2,1)S(1)} all-to-all(bf16[4,8,3072]{2,1,0:T(8,128)(2,1)S(1)} %broadcast_in_dim.6), channel_id=1, replica_groups=mesh['z_lo'=4,'x'=4,'core'=2,'z_hi'=4,'y'=4] {'z_hi'}, dimensions={0} | all-to-all | bytes 393216 | tf_op jit(solution)/shard_map/all_to_all | solution.py:238
  33.5 19.0 %all_to_all.31 = bf16[4,32,3072]{2,1,0:T(8,128)(2,1)S(1)} all-to-all(bf16[4,32,3072]{2,1,0:T(8,128)(2,1)S(1)} %broadcast_in_dim.15), channel_id=1, replica_groups={{0,128,256,384},{16,17,18,19},{1,129,257,385},{144,145,146,147},{2,130,..., dimensions={0} | all-to-all | bytes 1572864 | tf_op jit(solution)/shard_map/all_to_all | solution.py:239
  52.5 2.6 %collective-permute-start = (bf16[128,3072]{1,0:T(8,128)(2,1)S(1)}, bf16[128,3072]{1,0:T(8,128)(2,1)}, u32[]{:S(2)}, u32[]{:S(2)}) collective-permute-start(bf16[128,3072]{1,0:T(8,128)(2,1)S(1)} %bitcast.13), channel_id=1, source_target_pairs={{0,3},{1,0},{2,1},{3,2},{4,7},{5,4},{6,5},{7,6},{8,11},{9,8},{10,9... | collective-permute-start | bytes 2359304 | tf_op jit(solution)/shard_map/ppermute | solution.py:62
  55.1 4.4 %collective-permute-start.1 = (bf16[128,3072]{1,0:T(8,128)(2,1)S(1)}, bf16[128,3072]{1,0:T(8,128)(2,1)}, u32[]{:S(2)}, u32[]{:S(2)}) collective-permute-start(bf16[128,3072]{1,0:T(8,128)(2,1)S(1)} %bitcast.14), channel_id=1, source_target_pairs={{0,1},{1,2},{2,3},{3,0},{4,5},{5,6},{6,7},{7,4},{8,9},{9,10},{10,1... | collective-permute-start | bytes 2359304 | tf_op jit(solution)/shard_map/ppermute | solution.py:62
  60.5 1.9 %collective-permute-start.2 = (bf16[64,3072]{1,0:T(8,128)(2,1)}, bf16[64,3072]{1,0:T(8,128)(2,1)S(1)}, u32[]{:S(2)}, u32[]{:S(2)}) collective-permute-start(bf16[64,3072]{1,0:T(8,128)(2,1)} %bitcast.7), channel_id=1, source_target_pairs={{0,2},{1,3},{2,0},{3,1},{4,6},{5,7},{6,4},{7,5},{8,10},{9,11},{10,... | collective-permute-start | bytes 1179656 | tf_op jit(solution)/shard_map/ppermute | solution.py:62
  62.4 5.4 %collective-permute-start.3 = (bf16[64,3072]{1,0:T(8,128)(2,1)}, bf16[64,3072]{1,0:T(8,128)(2,1)}, u32[]{:S(2)}, u32[]{:S(2)}) collective-permute-start(bf16[64,3072]{1,0:T(8,128)(2,1)} %bitcast.8), channel_id=1, source_target_pairs={{0,2},{1,3},{2,0},{3,1},{4,6},{5,7},{6,4},{7,5},{8,10},{9,11},{10,... | collective-permute-start | bytes 1179656 | tf_op jit(solution)/shard_map/ppermute | solution.py:62
  68.6 3.2 %collective-permute-done.2.p2a = bf16[64,3072]{1,0:T(8,128)(2,1)S(1)} collective-permute-done((bf16[64,3072]{1,0:T(8,128)(2,1)}, bf16[64,3072]{1,0:T(8,128)(2,1)S(1)}, u32[]{:S(2)}, u32[]{:S(2)}) %collective-permute-start.2) | collective-permute-done | bytes 393248 | tf_op jit(solution)/shard_map/ppermute | solution.py:62
  71.8 4.3 %collective-permute-done.3.p2b = bf16[64,3072]{1,0:T(8,128)(2,1)} collective-permute-done((bf16[64,3072]{1,0:T(8,128)(2,1)}, bf16[64,3072]{1,0:T(8,128)(2,1)}, u32[]{:S(2)}, u32[]{:S(2)}) %collective-permute-start.3) | collective-permute-done | bytes 393248 | tf_op jit(solution)/shard_map/ppermute | solution.py:62
  77.5 3.2 %shard_map.76 = (bf16[384,3072]{1,0:T(8,128)(2,1)S(1)}, f32[256,768]{1,0:T(8,128)S(1)}, f32[256,768]{1,0:T(8,128)S(1)}) custom-call(s32[5]{0:T(128)S(1)} %stack.23.place, f32[128,768]{1,0:T(8,128)S(1)} %shard_map.75.sums, bf16[128,3072]{1,0:T(8,128)(2,1)} %collective-permute-done.p1, bf16[128,3072]{1,0:T(8,128)(2,1)} %collective-permute-done.1.p3, ...), custom_call_target="tpu_custom_call" | custom-call | flops 905969664 | bytes 7118592 | tf_op jit(solution)/shard_map/pallas_call | solution.py:254
  80.7 1.9 %collective-permute-start.4 = (f32[256,768]{1,0:T(8,128)S(1)}, f32[256,768]{1,0:T(8,128)S(1)}, u32[]{:S(2)}, u32[]{:S(2)}) collective-permute-start(f32[256,768]{1,0:T(8,128)S(1)} %get-tuple-element.24), channel_id=1, source_target_pairs={{0,16},{16,0},{1,17},{17,1},{2,18},{18,2},{3,19},{19,3},{4,20},{20... | collective-permute-start | bytes 2359304 | tf_op jit(solution)/shard_map/ppermute | solution.py:276
  82.6 2.3 %collective-permute-done.4.more = f32[256,768]{1,0:T(8,128)S(1)} collective-permute-done((f32[256,768]{1,0:T(8,128)S(1)}, f32[256,768]{1,0:T(8,128)S(1)}, u32[]{:S(2)}, u32[]{:S(2)}) %collective-permute-start.4) | collective-permute-done | bytes 786464 | tf_op jit(solution)/shard_map/ppermute | solution.py:276
  85.0 12.5 %all_to_all.32.parts = bf16[4,64,768]{2,1,0:T(8,128)(2,1)S(1)} all-to-all(bf16[4,64,768]{2,1,0:T(8,128)(2,1)S(1)} %bitcast.19), channel_id=1, replica_groups=mesh['z_lo'=4,'x'=4,'core'=2,'z_hi'=4,'y'=4] {'x'}, dimensions={0} | all-to-all | bytes 786432 | tf_op jit(solution)/shard_map/all_to_all | solution.py:277
  98.1 9.8 %all_to_all.33 = bf16[4,64,768]{2,1,0:T(8,128)(2,1)S(1)} all-to-all(bf16[4,64,768]{2,1,0:T(8,128)(2,1)S(1)} %shard_map.78), channel_id=1, replica_groups=mesh['z_lo'=4,'x'=4,'core'=2,'z_hi'=4,'y'=4] {'x'}, dimensions={0} | all-to-all | bytes 786432 | tf_op jit(solution)/shard_map/all_to_all | solution.py:285
  107.9 2.4 %all_gather.3.shares = bf16[512,768]{1,0:T(8,128)(2,1)S(1)} all-gather(bf16[256,768]{1,0:T(8,128)(2,1)S(1)} %bitcast.21), channel_id=1, replica_groups=mesh['z_lo'=4,'x'=4,'core'=2,'z_hi'=4,'y'=4] {'core'}, dimensions={0}, use_global_device_ids=true | all-gather | bytes 1179648 | tf_op jit(solution)/shard_map/all_gather | solution.py:286
  110.2 1.9 %shard_map.79 = (bf16[128,3072]{1,0:T(8,128)(2,1)S(1)}, bf16[64,3072]{1,0:T(8,128)(2,1)S(1)}, bf16[64,3072]{1,0:T(8,128)(2,1)S(1)}, bf16[128,3072]{1,0:T(8,128)(2,1)S(1)}, bf16[512,768]{1,0:T(8,128)(2,1)S(1)}) custom-call(s32[5]{0:T(128)S(1)} %stack.23.place, bf16[512,768]{1,0:T(8,128)(2,1)S(1)} %all_gather.3.shares, bf16[1536,384]{1,0:T(8,128)(2,1)S(1)} %copy-done, ...), custom_call_target="tpu_custom_call" | custom-call | flops 905969664 | bytes 7118592 | tf_op jit(solution)/shard_map/pallas_call | solution.py:287
  112.7 5.7 %collective-permute-start.5 = (bf16[128,3072]{1,0:T(8,128)(2,1)S(1)}, bf16[128,3072]{1,0:T(8,128)(2,1)S(1)}, u32[]{:S(2)}, u32[]{:S(2)}) collective-permute-start(bf16[128,3072]{1,0:T(8,128)(2,1)S(1)} %get-tuple-element.30), channel_id=1, source_target_pairs={{0,1},{1,2},{2,3},{3,0},{4,5},{5,6},{6,7},{7,4},{8,9},{9,10},{10,1... | collective-permute-start | bytes 2359304 | tf_op jit(solution)/shard_map/ppermute | solution.py:62
  118.3 1.9 %collective-permute-start.8 = (bf16[128,3072]{1,0:T(8,128)(2,1)S(1)}, bf16[128,3072]{1,0:T(8,128)(2,1)S(1)}, u32[]{:S(2)}, u32[]{:S(2)}) collective-permute-start(bf16[128,3072]{1,0:T(8,128)(2,1)S(1)} %get-tuple-element.33), channel_id=1, source_target_pairs={{0,3},{1,0},{2,1},{3,2},{4,7},{5,4},{6,5},{7,6},{8,11},{9,8},{10,9... | collective-permute-start | bytes 2359304 | tf_op jit(solution)/shard_map/ppermute | solution.py:62
  120.3 3.4 %collective-permute-start.6 = (bf16[64,3072]{1,0:T(8,128)(2,1)S(1)}, bf16[64,3072]{1,0:T(8,128)(2,1)S(1)}, u32[]{:S(2)}, u32[]{:S(2)}) collective-permute-start(bf16[64,3072]{1,0:T(8,128)(2,1)S(1)} %get-tuple-element.31), channel_id=1, source_target_pairs={{0,2},{1,3},{2,0},{3,1},{4,6},{5,7},{6,4},{7,5},{8,10},{9,11},{10,... | collective-permute-start | bytes 1179656 | tf_op jit(solution)/shard_map/ppermute | solution.py:62
  123.6 4.0 %collective-permute-start.7 = (bf16[64,3072]{1,0:T(8,128)(2,1)S(1)}, bf16[64,3072]{1,0:T(8,128)(2,1)S(1)}, u32[]{:S(2)}, u32[]{:S(2)}) collective-permute-start(bf16[64,3072]{1,0:T(8,128)(2,1)S(1)} %get-tuple-element.32), channel_id=1, source_target_pairs={{0,2},{1,3},{2,0},{3,1},{4,6},{5,7},{6,4},{7,5},{8,10},{9,11},{10,... | collective-permute-start | bytes 1179656 | tf_op jit(solution)/shard_map/ppermute | solution.py:62
  130.7 2.0 %fusion = bf16[1536,384]{1,0:T(8,128)(2,1)} fusion(f32[1536,384]{1,0:T(8,128)S(1)} %fusion.6, bf16[384,3072]{1,0:T(8,128)(2,1)S(1)} %get-tuple-element.28, bf16[512,768]{1,0:T(8,128)(2,1)S(1)} %get-tuple-element.27.local), kind=kOutput, calls=%fused_computation.2 | convolution fusion | flops 454164480 | bytes 5013504 | tf_op jit(solution)/shard_map/dot_general | solution.py:66
  132.7 3.3 %collective-permute-done.6.r2a = bf16[64,3072]{1,0:T(8,128)(2,1)S(1)} collective-permute-done((bf16[64,3072]{1,0:T(8,128)(2,1)S(1)}, bf16[64,3072]{1,0:T(8,128)(2,1)S(1)}, u32[]{:S(2)}, u32[]{:S(2)}) %collective-permute-start.6) | collective-permute-done | bytes 393248 | tf_op jit(solution)/shard_map/ppermute | solution.py:62
  136.0 4.2 %collective-permute-done.7.r2b = bf16[64,3072]{1,0:T(8,128)(2,1)S(1)} collective-permute-done((bf16[64,3072]{1,0:T(8,128)(2,1)S(1)}, bf16[64,3072]{1,0:T(8,128)(2,1)S(1)}, u32[]{:S(2)}, u32[]{:S(2)}) %collective-permute-start.7) | collective-permute-done | bytes 393248 | tf_op jit(solution)/shard_map/ppermute | solution.py:62
  142.8 16.6 %all_to_all.34.parts = bf16[4,32,3072]{2,1,0:T(8,128)(2,1)S(1)} all-to-all(bf16[4,32,3072]{2,1,0:T(8,128)(2,1)S(1)} %get-tuple-element.34), channel_id=1, replica_groups={{0,128,256,384},{16,17,18,19},{1,129,257,385},{144,145,146,147},{2,130,..., dimensions={0} | all-to-all | bytes 1572864 | tf_op jit(solution)/shard_map/all_to_all | solution.py:331
  160.1 17.2 %all_to_all.35.parts = bf16[4,8,3072]{2,1,0:T(8,128)(2,1)S(1)} all-to-all(bf16[4,8,3072]{2,1,0:T(8,128)(2,1)S(1)} %bitcast.20), channel_id=1, replica_groups=mesh['z_lo'=4,'x'=4,'core'=2,'z_hi'=4,'y'=4] {'z_hi'}, dimensions={0} | all-to-all | bytes 393216 | tf_op jit(solution)/shard_map/all_to_all | solution.py:342
  (23 shorter events, 12.1 us)
Async XLA Ops:
  1.4 66.5 %copy-start = (bf16[1536,384]{1,0:T(8,128)(2,1)S(1)}, bf16[1536,384]{1,0:T(8,128)(2,1)}, u32[]{:S(2)}) copy-start(bf16[1536,384]{1,0:T(8,128)(2,1)} %first.7) | copy-start | bytes 3538948
  1.4 66.5 %copy-start.1 = (bf16[384,1536]{1,0:T(8,128)(2,1)S(1)}, bf16[384,1536]{1,0:T(8,128)(2,1)}, u32[]{:S(2)}) copy-start(bf16[384,1536]{1,0:T(8,128)(2,1)} %second.7) | copy-start | bytes 3538948
  52.5 23.7 %collective-permute-start = (bf16[128,3072]{1,0:T(8,128)(2,1)S(1)}, bf16[128,3072]{1,0:T(8,128)(2,1)}, u32[]{:S(2)}, u32[]{:S(2)}) collective-permute-start(bf16[128,3072]{1,0:T(8,128)(2,1)S(1)} %bitcast.13), channel_id=1, source_target_pairs={{0,3},{1,0},{2,1},{3,2},{4,7},{5,4},{6,5},{7,6},{8,11},{9,8},{10,9... | collective-permute-start | bytes 2359304 | tf_op jit(solution)/shard_map/ppermute | solution.py:62
  55.1 22.4 %collective-permute-start.1 = (bf16[128,3072]{1,0:T(8,128)(2,1)S(1)}, bf16[128,3072]{1,0:T(8,128)(2,1)}, u32[]{:S(2)}, u32[]{:S(2)}) collective-permute-start(bf16[128,3072]{1,0:T(8,128)(2,1)S(1)} %bitcast.14), channel_id=1, source_target_pairs={{0,1},{1,2},{2,3},{3,0},{4,5},{5,6},{6,7},{7,4},{8,9},{9,10},{10,1... | collective-permute-start | bytes 2359304 | tf_op jit(solution)/shard_map/ppermute | solution.py:62
  60.5 11.4 %collective-permute-start.2 = (bf16[64,3072]{1,0:T(8,128)(2,1)}, bf16[64,3072]{1,0:T(8,128)(2,1)S(1)}, u32[]{:S(2)}, u32[]{:S(2)}) collective-permute-start(bf16[64,3072]{1,0:T(8,128)(2,1)} %bitcast.7), channel_id=1, source_target_pairs={{0,2},{1,3},{2,0},{3,1},{4,6},{5,7},{6,4},{7,5},{8,10},{9,11},{10,... | collective-permute-start | bytes 1179656 | tf_op jit(solution)/shard_map/ppermute | solution.py:62
  62.4 13.8 %collective-permute-start.3 = (bf16[64,3072]{1,0:T(8,128)(2,1)}, bf16[64,3072]{1,0:T(8,128)(2,1)}, u32[]{:S(2)}, u32[]{:S(2)}) collective-permute-start(bf16[64,3072]{1,0:T(8,128)(2,1)} %bitcast.8), channel_id=1, source_target_pairs={{0,2},{1,3},{2,0},{3,1},{4,6},{5,7},{6,4},{7,5},{8,10},{9,11},{10,... | collective-permute-start | bytes 1179656 | tf_op jit(solution)/shard_map/ppermute | solution.py:62
  80.7 4.2 %collective-permute-start.4 = (f32[256,768]{1,0:T(8,128)S(1)}, f32[256,768]{1,0:T(8,128)S(1)}, u32[]{:S(2)}, u32[]{:S(2)}) collective-permute-start(f32[256,768]{1,0:T(8,128)S(1)} %get-tuple-element.24), channel_id=1, source_target_pairs={{0,16},{16,0},{1,17},{17,1},{2,18},{18,2},{3,19},{19,3},{4,20},{20... | collective-permute-start | bytes 2359304 | tf_op jit(solution)/shard_map/ppermute | solution.py:276
  112.7 27.5 %collective-permute-start.5 = (bf16[128,3072]{1,0:T(8,128)(2,1)S(1)}, bf16[128,3072]{1,0:T(8,128)(2,1)S(1)}, u32[]{:S(2)}, u32[]{:S(2)}) collective-permute-start(bf16[128,3072]{1,0:T(8,128)(2,1)S(1)} %get-tuple-element.30), channel_id=1, source_target_pairs={{0,1},{1,2},{2,3},{3,0},{4,5},{5,6},{6,7},{7,4},{8,9},{9,10},{10,1... | collective-permute-start | bytes 2359304 | tf_op jit(solution)/shard_map/ppermute | solution.py:62
  118.3 23.5 %collective-permute-start.8 = (bf16[128,3072]{1,0:T(8,128)(2,1)S(1)}, bf16[128,3072]{1,0:T(8,128)(2,1)S(1)}, u32[]{:S(2)}, u32[]{:S(2)}) collective-permute-start(bf16[128,3072]{1,0:T(8,128)(2,1)S(1)} %get-tuple-element.33), channel_id=1, source_target_pairs={{0,3},{1,0},{2,1},{3,2},{4,7},{5,4},{6,5},{7,6},{8,11},{9,8},{10,9... | collective-permute-start | bytes 2359304 | tf_op jit(solution)/shard_map/ppermute | solution.py:62
  120.3 15.7 %collective-permute-start.6 = (bf16[64,3072]{1,0:T(8,128)(2,1)S(1)}, bf16[64,3072]{1,0:T(8,128)(2,1)S(1)}, u32[]{:S(2)}, u32[]{:S(2)}) collective-permute-start(bf16[64,3072]{1,0:T(8,128)(2,1)S(1)} %get-tuple-element.31), channel_id=1, source_target_pairs={{0,2},{1,3},{2,0},{3,1},{4,6},{5,7},{6,4},{7,5},{8,10},{9,11},{10,... | collective-permute-start | bytes 1179656 | tf_op jit(solution)/shard_map/ppermute | solution.py:62
  123.6 16.6 %collective-permute-start.7 = (bf16[64,3072]{1,0:T(8,128)(2,1)S(1)}, bf16[64,3072]{1,0:T(8,128)(2,1)S(1)}, u32[]{:S(2)}, u32[]{:S(2)}) collective-permute-start(bf16[64,3072]{1,0:T(8,128)(2,1)S(1)} %get-tuple-element.32), channel_id=1, source_target_pairs={{0,2},{1,3},{2,0},{3,1},{4,6},{5,7},{6,4},{7,5},{8,10},{9,11},{10,... | collective-permute-start | bytes 1179656 | tf_op jit(solution)/shard_map/ppermute | solution.py:62

commit v4 on v3

--- a/solution.py
+++ b/solution.py
@@ -17,9 +17,6 @@
 BLOCK = 32
 PIECE = 128
 SHARE = 64
-LONG = 64
-SHORT = PIECE - LONG
-ORDER = (0, 1, 3, 2)
 params = pltpu.CompilerParams(vmem_limit_bytes=20 << 20)
 
 
@@ -36,30 +33,39 @@
                         yield z_lo, x, core, z_hi, y
 
 
-def near_groups():
+def pair_groups():
     groups = []
     for x in range(4):
-        for z_hi in range(4):
-            for other in range(4):
-                groups.append([place_of(i, x, 0, z_hi, other) for i in range(4)])
-                groups.append([place_of(other, x, 1, z_hi, i) for i in range(4)])
+        for core in range(2):
+            for z in range(0, 16, 2):
+                for y in range(0, 4, 2):
+                    group = []
+                    for part in range(4):
+                        real_z = (z + part // 2 + 1 - core) % 16
+                        real_y = (y + part % 2 + 1 - core) % 4
+                        group.append(place_of(real_z % 4, x, core, real_z // 4, real_y))
+                    groups.append(group)
     return groups
 
 
-def far_shift(step):
+def swapped(place, size):
+    return (place + 1 if place % 2 else place - 1) % size
+
+
+def moved(value, slot):
     pairs = []
     for z_lo, x, core, z_hi, y in every_place():
-        if core == 0:
-            target = place_of(z_lo, x, core, z_hi, (y + step) % 4)
-        else:
-            z = (z_hi * 4 + z_lo + step) % 16
-            target = place_of(z % 4, x, core, z // 4, y)
+        shift = 1 - core
+        z = (z_hi * 4 + z_lo - shift) % 16
+        other_y, other_z = (y - shift) % 4, z
+        if slot % 2:
+            other_y = swapped(other_y, 4)
+        if slot // 2:
+            other_z = swapped(z, 16)
+        other_y, other_z = (other_y + shift) % 4, (other_z + shift) % 16
+        target = place_of(other_z % 4, x, core, other_z // 4, other_y)
         pairs.append((place_of(z_lo, x, core, z_hi, y), target))
-    return pairs
-
-
-def moved(value, step):
-    return lax.ppermute(value, GRID, far_shift(step))
+    return lax.ppermute(value, GRID, pairs)
 
 
 def dot_over(left_side, right_side, left_dim, right_dim):
@@ -75,9 +81,12 @@
     return jnp.broadcast_to(block[None], (count,) + block.shape)
 
 
-def common_block(core, own, piece, part):
-    index = lax.rem(own + piece, 4)
-    return jnp.where(core == 0, index * 4 + part, part * 4 + index)
+def common_block(core, own, slot, part):
+    pair = lax.bitwise_xor(own, jnp.int32(slot))
+    shift = 1 - core
+    y = lax.rem(lax.rem(pair, 2) * 2 + part % 2 + shift, 4)
+    z = lax.rem(pair // 2 * 2 + part // 2 + shift, 4)
+    return y * 4 + z
 
 
 def first_kernel(p0, first, second, sums):
@@ -87,20 +96,19 @@
     sums[:, units:] = dot_over(p0[:, width:], second[...], 1, 1)
 
 
-def last_kernel(place, sums, p1, p3, p2a, p2b, first, second, both, kept, given, rest):
+def last_kernel(place, p3, p1, p2, sums, first, second, both, kept, given, rest):
     core, own = place[0], place[1]
     width = first.shape[0]
     units = first.shape[1]
     both[0:128, :] = p1[...]
-    both[128:256, :] = p3[...]
-    both[256 : 256 + SHORT, :] = p2a[...]
-    both[256 + SHORT : 384, :] = p2b[...]
+    both[128:256, :] = p2[...]
+    both[256:384, :] = p3[...]
     rest[:, :units] = dot_over(both[:, :width], first[...], 1, 0)
     rest[:, units:] = dot_over(both[:, width:], second[...], 1, 1)
     for slot in range(4):
         source, base = (sums, 0) if slot == 0 else (rest, PIECE)
         for part in range(4):
-            block = common_block(core, own, ORDER[slot], part)
+            block = common_block(core, own, slot, part)
             start = pl.multiple_of(lax.rem(block, 8) * BLOCK, BLOCK)
             at = (slot * 4 + part) * BLOCK - base
             mine = block // 8 == core
@@ -153,12 +161,12 @@
     )
 
 
-def second_kernel(place, shares, first, second, o1, o2a, o2b, o3, local):
+def second_kernel(place, shares, first, second, o1, o2, o3, local):
     core, own = place[0], place[1]
     width = first.shape[0]
     for slot in range(4):
         for part in range(4):
-            block = common_block(core, own, ORDER[slot], part)
+            block = common_block(core, own, slot, part)
             start = pl.multiple_of(block * BLOCK, BLOCK)
             at = (slot * 4 + part) * BLOCK
             local[at : at + BLOCK, :] = shares[pl.ds(start, BLOCK), :]
@@ -167,9 +175,8 @@
         outs = sides[side].astype(jnp.bfloat16)
         columns = slice(side * width, (side + 1) * width)
         o1[:, columns] = outs[0:128]
-        o3[:, columns] = outs[128:256]
-        o2a[:, columns] = outs[256 : 256 + LONG]
-        o2b[:, columns] = outs[256 + LONG : 384]
+        o2[:, columns] = outs[128:256]
+        o3[:, columns] = outs[256:384]
 
 
 def own_kernel(local, first, second, o0):
@@ -179,15 +186,11 @@
     o0[:, width:] = sides[1]
 
 
-def far_kernel(place, o0, r1, r2a, r2b, r3, outs, own_lost):
+def far_kernel(place, r3, r1, r2, o0, outs, own_lost):
     for part in range(4):
         rows = slice(part * BLOCK, (part + 1) * BLOCK)
-        if part < 2:
-            r2 = r2a[rows, :]
-        else:
-            r2 = r2b[part * BLOCK - LONG : part * BLOCK - LONG + BLOCK, :]
         total = o0[rows, :] + r1[rows, :].astype(jnp.float32)
-        total = total + r3[rows, :].astype(jnp.float32) + r2.astype(jnp.float32)
+        total = total + r2[rows, :].astype(jnp.float32) + r3[rows, :].astype(jnp.float32)
         outs[part] = total.astype(jnp.bfloat16)
 
         @pl.when(place[3] == part)
@@ -225,23 +228,20 @@
 def on_device(tokens, first_weight, second_weight, grad_out):
     width = tokens.shape[1]
     units = first_weight.shape[1]
-    core = lax.axis_index("core")
-    y, z_lo = lax.axis_index("y"), lax.axis_index("z_lo")
-    own, other = jnp.where(core == 0, y, z_lo), jnp.where(core == 0, z_lo, y)
-    x, z_hi = lax.axis_index("x"), lax.axis_index("z_hi")
-    place = jnp.stack([core, own, x, other, z_hi]).astype(jnp.int32)
+    core, x = lax.axis_index("core"), lax.axis_index("x")
+    y, z_lo, z_hi = lax.axis_index("y"), lax.axis_index("z_lo"), lax.axis_index("z_hi")
+    y, z_lo = (y + 3 + core) % 4, (z_lo + 3 + core) % 4
+    own, part = z_lo // 2 * 2 + y // 2, z_lo % 2 * 2 + y % 2
+    place = jnp.stack([core, own, x, part, z_hi]).astype(jnp.int32)
     scalars = pl.BlockSpec(memory_space=pltpu.SMEM)
     whole = pl.BlockSpec(memory_space=pltpu.VMEM)
-    near = near_groups()
+    near = pair_groups()
 
     both = jnp.concatenate([tokens, grad_out], axis=1)
     both = lax.all_to_all(copies_of(both, 4), "z_hi", 0, 0).reshape(BLOCK, 2 * width)
     both = lax.all_to_all(copies_of(both, 4), GRID, 0, 0, axis_index_groups=near)
     both = both.reshape(PIECE, 2 * width)
-    p3 = moved(both, 1)
-    p1 = moved(both, -1)
-    p2b = moved(both[SHORT:], 2)
-    p2a = moved(both[:SHORT], -2)
+    p3, p1, p2 = moved(both, 3), moved(both, 1), moved(both, 2)
 
     sums = pl.pallas_call(
         first_kernel,
@@ -258,12 +258,12 @@
             shape_of(256, 2 * units, jnp.float32),
             shape_of(256, 2 * units, jnp.float32),
         ),
-        in_specs=[scalars] + [whole] * 7,
+        in_specs=[scalars] + [whole] * 6,
         out_specs=(whole, whole, whole),
         scratch_shapes=[pltpu.VMEM((384, 2 * units), jnp.float32)],
         compiler_params=params,
         cost_estimate=cost_of(384),
-    )(place, sums, p1, p3, p2a, p2b, first_weight, second_weight)
+    )(place, p3, p1, p2, sums, first_weight, second_weight)
     kept, sent = pl.pallas_call(
         add_kernel,
         out_shape=(
@@ -284,24 +284,20 @@
     )(place, parts, kept.reshape(4, SHARE, 2 * units))
     shares = lax.all_to_all(shares, "x", 0, 0).reshape(256, 2 * units)
     shares = lax.all_gather(shares, "core", axis=0, tiled=True)
-    o1, o2a, o2b, o3, local = pl.pallas_call(
+    o1, o2, o3, local = pl.pallas_call(
         second_kernel,
         out_shape=(
             shape_of(PIECE, 2 * width, jnp.bfloat16),
-            shape_of(LONG, 2 * width, jnp.bfloat16),
-            shape_of(SHORT, 2 * width, jnp.bfloat16),
+            shape_of(PIECE, 2 * width, jnp.bfloat16),
             shape_of(PIECE, 2 * width, jnp.bfloat16),
             shape_of(512, 2 * units, jnp.bfloat16),
         ),
         in_specs=[scalars] + [whole] * 3,
-        out_specs=(whole,) * 5,
+        out_specs=(whole,) * 4,
         compiler_params=params,
         cost_estimate=cost_of(384),
     )(place, shares, first_weight, second_weight)
-    r1 = moved(o1, 1)
-    r3 = moved(o3, -1)
-    r2a = moved(o2a, 2)
-    r2b = moved(o2b, -2)
+    r3, r1, r2 = moved(o3, 3), moved(o1, 1), moved(o2, 2)
     o0 = pl.pallas_call(
         own_kernel,
         out_shape=shape_of(PIECE, 2 * width, jnp.float32),
@@ -324,10 +320,10 @@
             jax.ShapeDtypeStruct((4, BLOCK, 2 * width), jnp.bfloat16),
             shape_of(BLOCK, 2 * width, jnp.float32),
         ),
-        in_specs=[scalars] + [whole] * 5,
+        in_specs=[scalars] + [whole] * 4,
         out_specs=(whole, whole),
         compiler_params=params,
-    )(place, o0, r1, r2a, r2b, r3)
+    )(place, r3, r1, r2, o0)
     outs = lax.all_to_all(outs, GRID, 0, 0, axis_index_groups=near)
     outs, own_lost = pl.pallas_call(
         near_kernel,

time: 179 us -> 166 us (0.927)
  starting transfers between devices: 31.2 us -> 20.5 us
  blocking collectives: 109 us -> 103 us
  waiting for transfers between devices: 20.3 us -> 24.2 us
    ppermute x8 -> x6, starting transfers between devices: 29.3 us -> 18.6 us  [moved(): return lax.ppermute(value, GRID, pairs)]
    all_to_all x1, blocking collectives: 19 us -> 12.9 us  [on_device(): lax.all_to_all(copies_of(both, 4), GRID, 0, 0, axis_index_groups=near)]
    ppermute x8 -> x6, waiting for transfers between devices: 18 us -> 22 us  [moved(): return lax.ppermute(value, GRID, pairs)]
    all_to_all x1, blocking collectives: 17.2 us -> 20.7 us  [on_device(): outs = lax.all_to_all(outs.reshape(4, 8, 2 * width), 'z_hi', 0, 0)]
    all_to_all x1, blocking collectives: 16.6 us -> 13.4 us  [on_device(): outs = lax.all_to_all(outs, GRID, 0, 0, axis_index_groups=near)]
  transfers between devices with their start and end apart: 9 -> 7, of which waited for: 7 -> 5; matrix products, arithmetic and copies ran while one was open for 3% -> 3% of each run, Pallas kernels for 1% -> 1%
where the time goes in v4:
time: 166 us; the launch traced here: 165 us
  blocking collectives  103 us (62%)
  waiting for transfers between devices  24.2 us (15%)
  starting transfers between devices  20.5 us (12%)
  Pallas kernels  9.79 us (6%)
  matrix products  4.8 us (3%)
    all_to_all x1, blocking collectives, on_device(): lax.all_to_all(copies_of(both, 4), 'z_hi', 0, 0).reshape(BLOCK, 2 * width)  31.8 us
    ppermute x6, waiting for transfers between devices, moved(): return lax.ppermute(value, GRID, pairs)  22 us
    all_to_all x1, blocking collectives, on_device(): outs = lax.all_to_all(outs.reshape(4, 8, 2 * width), 'z_hi', 0, 0)  20.7 us
    ppermute x6, starting transfers between devices, moved(): return lax.ppermute(value, GRID, pairs)  18.6 us
    all_to_all x1, blocking collectives, on_device(): outs = lax.all_to_all(outs, GRID, 0, 0, axis_index_groups=near)  13.4 us
    all_to_all x1, blocking collectives, on_device(): lax.all_to_all(copies_of(both, 4), GRID, 0, 0, axis_index_groups=near)  12.9 us
    all_to_all x1, blocking collectives, on_device(): parts = lax.all_to_all(sent.reshape(4, SHARE, 2 * units), 'x', 0, 0)  12.5 us
    all_to_all x1, blocking collectives, on_device(): shares = lax.all_to_all(shares, 'x', 0, 0).reshape(256, 2 * units)  9.77 us
  transfers between devices with their start and end apart: 7, of which 5 were waited for; matrix products, arithmetic and copies ran while one was open for 3% of the time, Pallas kernels for 1%

profile of v4, /device:TPU:24, one launch (start us, length us, event | category | flops | bytes accessed | tf_op | source)
XLA Modules:
  0.0 164.6 jit_solution(6177275940706095068)
XLA Ops:
  0.7 0.9 pad_maximum_fusion
  1.6 31.8 %all_to_all.30 = bf16[4,8,3072]{2,1,0:T(8,128)(2,1)S(1)} all-to-all(bf16[4,8,3072]{2,1,0:T(8,128)(2,1)S(1)} %broadcast_in_dim.6), channel_id=1, replica_groups=mesh['z_lo'=4,'x'=4,'core'=2,'z_hi'=4,'y'=4] {'z_hi'}, dimensions={0} | all-to-all | bytes 393216 | tf_op jit(solution)/shard_map/all_to_all | solution.py:241
  33.5 12.9 %all_to_all.31 = bf16[4,32,3072]{2,1,0:T(8,128)(2,1)S(1)} all-to-all(bf16[4,32,3072]{2,1,0:T(8,128)(2,1)S(1)} %broadcast_in_dim.15), channel_id=1, replica_groups={{129,130,257,258},{131,128,259,256},{385,386,5,6},{387,384,7,4},{133,13..., dimensions={0} | all-to-all | bytes 1572864 | tf_op jit(solution)/shard_map/all_to_all | solution.py:242
  46.4 3.0 %collective-permute-start = (bf16[128,3072]{1,0:T(8,128)(2,1)S(1)}, bf16[128,3072]{1,0:T(8,128)(2,1)}, u32[]{:S(2)}, u32[]{:S(2)}) collective-permute-start(bf16[128,3072]{1,0:T(8,128)(2,1)S(1)} %bitcast.11), channel_id=1, source_target_pairs={{0,129},{1,128},{2,131},{3,130},{4,133},{5,132},{6,135},{7,134},{8... | collective-permute-start | bytes 2359304 | tf_op jit(solution)/shard_map/ppermute | solution.py:68
  49.4 4.3 %collective-permute-start.1 = (bf16[128,3072]{1,0:T(8,128)(2,1)S(1)}, bf16[128,3072]{1,0:T(8,128)(2,1)}, u32[]{:S(2)}, u32[]{:S(2)}) collective-permute-start(bf16[128,3072]{1,0:T(8,128)(2,1)S(1)} %bitcast.12), channel_id=1, source_target_pairs={{0,1},{1,0},{2,3},{3,2},{4,5},{5,4},{6,7},{7,6},{8,9},{9,8},{10,11... | collective-permute-start | bytes 2359304 | tf_op jit(solution)/shard_map/ppermute | solution.py:68
  53.8 1.9 %collective-permute-start.2 = (bf16[128,3072]{1,0:T(8,128)(2,1)S(1)}, bf16[128,3072]{1,0:T(8,128)(2,1)}, u32[]{:S(2)}, u32[]{:S(2)}) collective-permute-start(bf16[128,3072]{1,0:T(8,128)(2,1)S(1)} %bitcast.13), channel_id=1, source_target_pairs={{0,128},{1,129},{2,130},{3,131},{4,132},{5,133},{6,134},{7,135},{8... | collective-permute-start | bytes 2359304 | tf_op jit(solution)/shard_map/ppermute | solution.py:68
  56.6 4.8 %collective-permute-done.p3 = bf16[128,3072]{1,0:T(8,128)(2,1)} collective-permute-done((bf16[128,3072]{1,0:T(8,128)(2,1)S(1)}, bf16[128,3072]{1,0:T(8,128)(2,1)}, u32[]{:S(2)}, u32[]{:S(2)}) %collective-permute-start) | collective-permute-done | bytes 786464 | tf_op jit(solution)/shard_map/ppermute | solution.py:68
  61.4 8.3 %collective-permute-done.1.p1 = bf16[128,3072]{1,0:T(8,128)(2,1)} collective-permute-done((bf16[128,3072]{1,0:T(8,128)(2,1)S(1)}, bf16[128,3072]{1,0:T(8,128)(2,1)}, u32[]{:S(2)}, u32[]{:S(2)}) %collective-permute-start.1) | collective-permute-done | bytes 786464 | tf_op jit(solution)/shard_map/ppermute | solution.py:68
  69.7 3.4 %shard_map.76 = (bf16[384,3072]{1,0:T(8,128)(2,1)S(1)}, f32[256,768]{1,0:T(8,128)S(1)}, f32[256,768]{1,0:T(8,128)S(1)}) custom-call(s32[5]{0:T(128)S(1)} %stack.23.place, bf16[128,3072]{1,0:T(8,128)(2,1)} %collective-permute-done.p3, bf16[128,3072]{1,0:T(8,128)(2,1)} %collective-permute-done.1.p1, bf16[128,3072]{1,0:T(8,128)(2,1)} %collective-permute-done.2.p2, ...), custom_call_target="tpu_custom_call" | custom-call | flops 905969664 | bytes 7118592 | tf_op jit(solution)/shard_map/pallas_call | solution.py:254
  73.1 1.9 %collective-permute-start.3 = (f32[256,768]{1,0:T(8,128)S(1)}, f32[256,768]{1,0:T(8,128)S(1)}, u32[]{:S(2)}, u32[]{:S(2)}) collective-permute-start(f32[256,768]{1,0:T(8,128)S(1)} %get-tuple-element.23), channel_id=1, source_target_pairs={{0,16},{16,0},{1,17},{17,1},{2,18},{18,2},{3,19},{19,3},{4,20},{20... | collective-permute-start | bytes 2359304 | tf_op jit(solution)/shard_map/ppermute | solution.py:276
  75.1 2.3 %collective-permute-done.3.more = f32[256,768]{1,0:T(8,128)S(1)} collective-permute-done((f32[256,768]{1,0:T(8,128)S(1)}, f32[256,768]{1,0:T(8,128)S(1)}, u32[]{:S(2)}, u32[]{:S(2)}) %collective-permute-start.3) | collective-permute-done | bytes 786464 | tf_op jit(solution)/shard_map/ppermute | solution.py:276
  77.4 12.5 %all_to_all.32.parts = bf16[4,64,768]{2,1,0:T(8,128)(2,1)S(1)} all-to-all(bf16[4,64,768]{2,1,0:T(8,128)(2,1)S(1)} %bitcast.18), channel_id=1, replica_groups=mesh['z_lo'=4,'x'=4,'core'=2,'z_hi'=4,'y'=4] {'x'}, dimensions={0} | all-to-all | bytes 786432 | tf_op jit(solution)/shard_map/all_to_all | solution.py:277
  90.6 9.8 %all_to_all.33 = bf16[4,64,768]{2,1,0:T(8,128)(2,1)S(1)} all-to-all(bf16[4,64,768]{2,1,0:T(8,128)(2,1)S(1)} %shard_map.78), channel_id=1, replica_groups=mesh['z_lo'=4,'x'=4,'core'=2,'z_hi'=4,'y'=4] {'x'}, dimensions={0} | all-to-all | bytes 786432 | tf_op jit(solution)/shard_map/all_to_all | solution.py:285
  100.3 2.4 %all_gather.3.shares = bf16[512,768]{1,0:T(8,128)(2,1)S(1)} all-gather(bf16[256,768]{1,0:T(8,128)(2,1)S(1)} %bitcast.20), channel_id=1, replica_groups=mesh['z_lo'=4,'x'=4,'core'=2,'z_hi'=4,'y'=4] {'core'}, dimensions={0}, use_global_device_ids=true | all-gather | bytes 1179648 | tf_op jit(solution)/shard_map/all_gather | solution.py:286
  102.7 1.9 %shard_map.79 = (bf16[128,3072]{1,0:T(8,128)(2,1)S(1)}, bf16[128,3072]{1,0:T(8,128)(2,1)S(1)}, bf16[128,3072]{1,0:T(8,128)(2,1)S(1)}, bf16[512,768]{1,0:T(8,128)(2,1)S(1)}) custom-call(s32[5]{0:T(128)S(1)} %stack.23.place, bf16[512,768]{1,0:T(8,128)(2,1)S(1)} %all_gather.3.shares, bf16[1536,384]{1,0:T(8,128)(2,1)S(1)} %copy-done, bf16[384,1536]{1,0:T(8,128)(2,1)S(1)} %copy-done.1), custom_call_target="tpu_custom_call" | custom-call | flops 905969664 | bytes 7118592 | tf_op jit(solution)/shard_map/pallas_call | solution.py:287
  105.1 4.0 %collective-permute-start.4 = (bf16[128,3072]{1,0:T(8,128)(2,1)S(1)}, bf16[128,3072]{1,0:T(8,128)(2,1)S(1)}, u32[]{:S(2)}, u32[]{:S(2)}) collective-permute-start(bf16[128,3072]{1,0:T(8,128)(2,1)S(1)} %get-tuple-element.26), channel_id=1, source_target_pairs={{0,129},{1,128},{2,131},{3,130},{4,133},{5,132},{6,135},{7,134},{8... | collective-permute-start | bytes 2359304 | tf_op jit(solution)/shard_map/ppermute | solution.py:68
  109.2 3.3 %collective-permute-start.5 = (bf16[128,3072]{1,0:T(8,128)(2,1)S(1)}, bf16[128,3072]{1,0:T(8,128)(2,1)S(1)}, u32[]{:S(2)}, u32[]{:S(2)}) collective-permute-start(bf16[128,3072]{1,0:T(8,128)(2,1)S(1)} %get-tuple-element.27), channel_id=1, source_target_pairs={{0,1},{1,0},{2,3},{3,2},{4,5},{5,4},{6,7},{7,6},{8,9},{9,8},{10,11... | collective-permute-start | bytes 2359304 | tf_op jit(solution)/shard_map/ppermute | solution.py:68
  112.5 1.9 %collective-permute-start.6 = (bf16[128,3072]{1,0:T(8,128)(2,1)S(1)}, bf16[128,3072]{1,0:T(8,128)(2,1)S(1)}, u32[]{:S(2)}, u32[]{:S(2)}) collective-permute-start(bf16[128,3072]{1,0:T(8,128)(2,1)S(1)} %get-tuple-element.28), channel_id=1, source_target_pairs={{0,128},{1,129},{2,130},{3,131},{4,132},{5,133},{6,134},{7,135},{8... | collective-permute-start | bytes 2359304 | tf_op jit(solution)/shard_map/ppermute | solution.py:68
  115.7 1.8 %fusion.1 = bf16[384,1536]{1,0:T(8,128)(2,1)} fusion(f32[384,1536]{1,0:T(8,128)S(1)} %fusion.4, bf16[384,3072]{1,0:T(8,128)(2,1)S(1)} %get-tuple-element.30, bf16[512,768]{1,0:T(8,128)(2,1)S(1)} %get-tuple-element.29.local), kind=kOutput, calls=%fused_computation.3 | convolution fusion | flops 454164480 | bytes 5013504 | tf_op jit(solution)/shard_map/dot_general | solution.py:72
  117.5 2.0 %fusion = bf16[1536,384]{1,0:T(8,128)(2,1)} fusion(f32[1536,384]{1,0:T(8,128)S(1)} %fusion.6, bf16[384,3072]{1,0:T(8,128)(2,1)S(1)} %get-tuple-element.30, bf16[512,768]{1,0:T(8,128)(2,1)S(1)} %get-tuple-element.29.local), kind=kOutput, calls=%fused_computation.2 | convolution fusion | flops 454164480 | bytes 5013504 | tf_op jit(solution)/shard_map/dot_general | solution.py:72
  120.0 8.3 %collective-permute-done.5.r1 = bf16[128,3072]{1,0:T(8,128)(2,1)S(1)} collective-permute-done((bf16[128,3072]{1,0:T(8,128)(2,1)S(1)}, bf16[128,3072]{1,0:T(8,128)(2,1)S(1)}, u32[]{:S(2)}, u32[]{:S(2)}) %collective-permute-start.5) | collective-permute-done | bytes 786464 | tf_op jit(solution)/shard_map/ppermute | solution.py:68
  128.3 0.9 shard_map.81
  129.3 13.4 %all_to_all.34.parts = bf16[4,32,3072]{2,1,0:T(8,128)(2,1)S(1)} all-to-all(bf16[4,32,3072]{2,1,0:T(8,128)(2,1)S(1)} %get-tuple-element.32), channel_id=1, replica_groups={{129,130,257,258},{131,128,259,256},{385,386,5,6},{387,384,7,4},{133,13..., dimensions={0} | all-to-all | bytes 1572864 | tf_op jit(solution)/shard_map/all_to_all | solution.py:327
  143.3 20.7 %all_to_all.35.parts = bf16[4,8,3072]{2,1,0:T(8,128)(2,1)S(1)} all-to-all(bf16[4,8,3072]{2,1,0:T(8,128)(2,1)S(1)} %bitcast.19), channel_id=1, replica_groups=mesh['z_lo'=4,'x'=4,'core'=2,'z_hi'=4,'y'=4] {'z_hi'}, dimensions={0} | all-to-all | bytes 393216 | tf_op jit(solution)/shard_map/all_to_all | solution.py:338
  (18 shorter events, 5.2 us)
Async XLA Ops:
  0.6 55.3 %copy-start = (bf16[1536,384]{1,0:T(8,128)(2,1)S(1)}, bf16[1536,384]{1,0:T(8,128)(2,1)}, u32[]{:S(2)}) copy-start(bf16[1536,384]{1,0:T(8,128)(2,1)} %first.7) | copy-start | bytes 3538948
  0.6 55.3 %copy-start.1 = (bf16[384,1536]{1,0:T(8,128)(2,1)S(1)}, bf16[384,1536]{1,0:T(8,128)(2,1)}, u32[]{:S(2)}) copy-start(bf16[384,1536]{1,0:T(8,128)(2,1)} %second.7) | copy-start | bytes 3538948
  46.4 15.0 %collective-permute-start = (bf16[128,3072]{1,0:T(8,128)(2,1)S(1)}, bf16[128,3072]{1,0:T(8,128)(2,1)}, u32[]{:S(2)}, u32[]{:S(2)}) collective-permute-start(bf16[128,3072]{1,0:T(8,128)(2,1)S(1)} %bitcast.11), channel_id=1, source_target_pairs={{0,129},{1,128},{2,131},{3,130},{4,133},{5,132},{6,135},{7,134},{8... | collective-permute-start | bytes 2359304 | tf_op jit(solution)/shard_map/ppermute | solution.py:68
  49.4 20.3 %collective-permute-start.1 = (bf16[128,3072]{1,0:T(8,128)(2,1)S(1)}, bf16[128,3072]{1,0:T(8,128)(2,1)}, u32[]{:S(2)}, u32[]{:S(2)}) collective-permute-start(bf16[128,3072]{1,0:T(8,128)(2,1)S(1)} %bitcast.12), channel_id=1, source_target_pairs={{0,1},{1,0},{2,3},{3,2},{4,5},{5,4},{6,7},{7,6},{8,9},{9,8},{10,11... | collective-permute-start | bytes 2359304 | tf_op jit(solution)/shard_map/ppermute | solution.py:68
  53.8 15.9 %collective-permute-start.2 = (bf16[128,3072]{1,0:T(8,128)(2,1)S(1)}, bf16[128,3072]{1,0:T(8,128)(2,1)}, u32[]{:S(2)}, u32[]{:S(2)}) collective-permute-start(bf16[128,3072]{1,0:T(8,128)(2,1)S(1)} %bitcast.13), channel_id=1, source_target_pairs={{0,128},{1,129},{2,130},{3,131},{4,132},{5,133},{6,134},{7,135},{8... | collective-permute-start | bytes 2359304 | tf_op jit(solution)/shard_map/ppermute | solution.py:68
  73.1 4.2 %collective-permute-start.3 = (f32[256,768]{1,0:T(8,128)S(1)}, f32[256,768]{1,0:T(8,128)S(1)}, u32[]{:S(2)}, u32[]{:S(2)}) collective-permute-start(f32[256,768]{1,0:T(8,128)S(1)} %get-tuple-element.23), channel_id=1, source_target_pairs={{0,16},{16,0},{1,17},{17,1},{2,18},{18,2},{3,19},{19,3},{4,20},{20... | collective-permute-start | bytes 2359304 | tf_op jit(solution)/shard_map/ppermute | solution.py:276
  105.1 14.9 %collective-permute-start.4 = (bf16[128,3072]{1,0:T(8,128)(2,1)S(1)}, bf16[128,3072]{1,0:T(8,128)(2,1)S(1)}, u32[]{:S(2)}, u32[]{:S(2)}) collective-permute-start(bf16[128,3072]{1,0:T(8,128)(2,1)S(1)} %get-tuple-element.26), channel_id=1, source_target_pairs={{0,129},{1,128},{2,131},{3,130},{4,133},{5,132},{6,135},{7,134},{8... | collective-permute-start | bytes 2359304 | tf_op jit(solution)/shard_map/ppermute | solution.py:68
  109.2 19.2 %collective-permute-start.5 = (bf16[128,3072]{1,0:T(8,128)(2,1)S(1)}, bf16[128,3072]{1,0:T(8,128)(2,1)S(1)}, u32[]{:S(2)}, u32[]{:S(2)}) collective-permute-start(bf16[128,3072]{1,0:T(8,128)(2,1)S(1)} %get-tuple-element.27), channel_id=1, source_target_pairs={{0,1},{1,0},{2,3},{3,2},{4,5},{5,4},{6,7},{7,6},{8,9},{9,8},{10,11... | collective-permute-start | bytes 2359304 | tf_op jit(solution)/shard_map/ppermute | solution.py:68
  112.5 15.8 %collective-permute-start.6 = (bf16[128,3072]{1,0:T(8,128)(2,1)S(1)}, bf16[128,3072]{1,0:T(8,128)(2,1)S(1)}, u32[]{:S(2)}, u32[]{:S(2)}) collective-permute-start(bf16[128,3072]{1,0:T(8,128)(2,1)S(1)} %get-tuple-element.28), channel_id=1, source_target_pairs={{0,128},{1,129},{2,130},{3,131},{4,132},{5,133},{6,134},{7,135},{8... | collective-permute-start | bytes 2359304 | tf_op jit(solution)/shard_map/ppermute | solution.py:68

commit v5 on v4

--- a/solution.py
+++ b/solution.py
@@ -96,21 +96,20 @@
     sums[:, units:] = dot_over(p0[:, width:], second[...], 1, 1)
 
 
-def last_kernel(place, p3, p1, p2, sums, first, second, both, kept, given, rest):
+def last_kernel(place, sums, sums3, p1, p2, first, second, both, kept, given, rest):
     core, own = place[0], place[1]
     width = first.shape[0]
     units = first.shape[1]
     both[0:128, :] = p1[...]
     both[128:256, :] = p2[...]
-    both[256:384, :] = p3[...]
     rest[:, :units] = dot_over(both[:, :width], first[...], 1, 0)
     rest[:, units:] = dot_over(both[:, width:], second[...], 1, 1)
     for slot in range(4):
-        source, base = (sums, 0) if slot == 0 else (rest, PIECE)
+        source, base = ((sums, 0), (rest, 1), (rest, 1), (sums3, 3))[slot]
         for part in range(4):
             block = common_block(core, own, slot, part)
             start = pl.multiple_of(lax.rem(block, 8) * BLOCK, BLOCK)
-            at = (slot * 4 + part) * BLOCK - base
+            at = ((slot - base) * 4 + part) * BLOCK
             mine = block // 8 == core
 
             @pl.when(mine)
@@ -243,27 +242,30 @@
     both = both.reshape(PIECE, 2 * width)
     p3, p1, p2 = moved(both, 3), moved(both, 1), moved(both, 2)
 
-    sums = pl.pallas_call(
-        first_kernel,
-        out_shape=shape_of(PIECE, 2 * units, jnp.float32),
-        in_specs=[whole] * 3,
-        out_specs=whole,
-        compiler_params=params,
-        cost_estimate=cost_of(128),
-    )(both, first_weight, second_weight)
+    def early(rows):
+        return pl.pallas_call(
+            first_kernel,
+            out_shape=shape_of(PIECE, 2 * units, jnp.float32),
+            in_specs=[whole] * 3,
+            out_specs=whole,
+            compiler_params=params,
+            cost_estimate=cost_of(128),
+        )(rows, first_weight, second_weight)
+
+    sums, sums3 = early(both), early(p3)
     every, kept, given = pl.pallas_call(
         last_kernel,
         out_shape=(
-            shape_of(384, 2 * width, jnp.bfloat16),
+            shape_of(256, 2 * width, jnp.bfloat16),
             shape_of(256, 2 * units, jnp.float32),
             shape_of(256, 2 * units, jnp.float32),
         ),
         in_specs=[scalars] + [whole] * 6,
         out_specs=(whole, whole, whole),
-        scratch_shapes=[pltpu.VMEM((384, 2 * units), jnp.float32)],
-        compiler_params=params,
-        cost_estimate=cost_of(384),
-    )(place, p3, p1, p2, sums, first_weight, second_weight)
+        scratch_shapes=[pltpu.VMEM((256, 2 * units), jnp.float32)],
+        compiler_params=params,
+        cost_estimate=cost_of(256),
+    )(place, sums, sums3, p1, p2, first_weight, second_weight)
     kept, sent = pl.pallas_call(
         add_kernel,
         out_shape=(
@@ -298,6 +300,7 @@
         cost_estimate=cost_of(384),
     )(place, shares, first_weight, second_weight)
     r3, r1, r2 = moved(o3, 3), moved(o1, 1), moved(o2, 2)
+    late, r3 = lax.optimization_barrier((local, r3))
     o0 = pl.pallas_call(
         own_kernel,
         out_shape=shape_of(PIECE, 2 * width, jnp.float32),
@@ -305,12 +308,15 @@
         out_specs=whole,
         compiler_params=params,
         cost_estimate=cost_of(128),
-    )(local, first_weight, second_weight)
-    hidden, grad_pre = local[:, :units], local[:, units:]
-    first_grad = dot_over(every[:, :width], grad_pre[PIECE:], 0, 0)
-    first_grad = first_grad + dot_over(both[:, :width], grad_pre[:PIECE], 0, 0)
-    second_grad = dot_over(hidden[PIECE:], every[:, width:], 0, 0)
-    second_grad = second_grad + dot_over(hidden[:PIECE], both[:, width:], 0, 0)
+    )(late, first_weight, second_weight)
+    hidden, grad_pre = local[128:384, :units], local[128:384, units:]
+    late_hidden, late_pre = late[:, :units], late[:, units:]
+    first_grad = dot_over(every[:, :width], grad_pre, 0, 0)
+    first_grad = first_grad + dot_over(both[:, :width], late_pre[:128], 0, 0)
+    first_grad = first_grad + dot_over(p3[:, :width], late_pre[384:], 0, 0)
+    second_grad = dot_over(hidden, every[:, width:], 0, 0)
+    second_grad = second_grad + dot_over(late_hidden[:128], both[:, width:], 0, 0)
+    second_grad = second_grad + dot_over(late_hidden[384:], p3[:, width:], 0, 0)
     first_grad = first_grad.astype(jnp.bfloat16)
     second_grad = second_grad.astype(jnp.bfloat16)
     o0, first_grad, second_grad = lax.optimization_barrier((o0, first_grad, second_grad))

time: 166 us -> 165 us (level)
  waiting for transfers between devices: 24.2 us -> 19.6 us
  matrix products: 4.8 us -> 7.1 us
    ppermute x6, waiting for transfers between devices: 22 us -> 17.4 us  [moved(): return lax.ppermute(value, GRID, pairs)]
    dot_general x4 -> x6, matrix products: 4.8 us -> 7.1 us  [dot_over(): lax.dot_general(left_side, right_side, (((left_dim,), (right_dim,)), ((),...]
    pallas_call x2 -> x3, Pallas kernels: 4.07 us -> 5.24 us  [the longest x1 2.74 us: on_device(): pl.pallas_call(last_kernel, out_shape=(shape_of(256, 2 * width, jnp.bfloa...]
  transfers between devices with their start and end apart: 7 -> 7, of which waited for: 5 -> 5; matrix products, arithmetic and copies ran while one was open for 3% -> 4% of each run, Pallas kernels for 1% -> 2%
where the time goes in v5:
time: 165 us; the launch traced here: 163 us
  blocking collectives  103 us (62%)
  starting transfers between devices  20.5 us (12%)
  waiting for transfers between devices  19.6 us (12%)
  Pallas kernels  11 us (7%)
  matrix products  7.1 us (4%)
    all_to_all x1, blocking collectives, on_device(): lax.all_to_all(copies_of(both, 4), 'z_hi', 0, 0).reshape(BLOCK, 2 * width)  31.8 us
    all_to_all x1, blocking collectives, on_device(): outs = lax.all_to_all(outs.reshape(4, 8, 2 * width), 'z_hi', 0, 0)  20.7 us
    ppermute x6, starting transfers between devices, moved(): return lax.ppermute(value, GRID, pairs)  18.6 us
    ppermute x6, waiting for transfers between devices, moved(): return lax.ppermute(value, GRID, pairs)  17.4 us
    all_to_all x1, blocking collectives, on_device(): outs = lax.all_to_all(outs, GRID, 0, 0, axis_index_groups=near)  13.4 us
    all_to_all x1, blocking collectives, on_device(): lax.all_to_all(copies_of(both, 4), GRID, 0, 0, axis_index_groups=near)  12.9 us
    all_to_all x1, blocking collectives, on_device(): parts = lax.all_to_all(sent.reshape(4, SHARE, 2 * units), 'x', 0, 0)  12.5 us
    all_to_all x1, blocking collectives, on_device(): shares = lax.all_to_all(shares, 'x', 0, 0).reshape(256, 2 * units)  9.77 us
  transfers between devices with their start and end apart: 7, of which 5 were waited for; matrix products, arithmetic and copies ran while one was open for 4% of the time, Pallas kernels for 2%

profile of v5, /device:TPU:24, one launch (start us, length us, event | category | flops | bytes accessed | tf_op | source)
XLA Modules:
  0.0 163.5 jit_solution(14143035919638343396)
XLA Ops:
  1.6 31.8 %all_to_all.30 = bf16[4,8,3072]{2,1,0:T(8,128)(2,1)S(1)} all-to-all(bf16[4,8,3072]{2,1,0:T(8,128)(2,1)S(1)} %broadcast_in_dim.6), channel_id=1, replica_groups=mesh['z_lo'=4,'x'=4,'core'=2,'z_hi'=4,'y'=4] {'z_hi'}, dimensions={0} | all-to-all | bytes 393216 | tf_op jit(solution)/shard_map/all_to_all | solution.py:240
  33.5 12.9 %all_to_all.31 = bf16[4,32,3072]{2,1,0:T(8,128)(2,1)S(1)} all-to-all(bf16[4,32,3072]{2,1,0:T(8,128)(2,1)S(1)} %broadcast_in_dim.15), channel_id=1, replica_groups={{129,130,257,258},{131,128,259,256},{385,386,5,6},{387,384,7,4},{133,13..., dimensions={0} | all-to-all | bytes 1572864 | tf_op jit(solution)/shard_map/all_to_all | solution.py:241
  46.4 3.0 %collective-permute-start = (bf16[128,3072]{1,0:T(8,128)(2,1)S(1)}, bf16[128,3072]{1,0:T(8,128)(2,1)}, u32[]{:S(2)}, u32[]{:S(2)}) collective-permute-start(bf16[128,3072]{1,0:T(8,128)(2,1)S(1)} %bitcast.11), channel_id=1, source_target_pairs={{0,129},{1,128},{2,131},{3,130},{4,133},{5,132},{6,135},{7,134},{8... | collective-permute-start | bytes 2359304 | tf_op jit(solution)/shard_map/ppermute | solution.py:68
  49.4 4.3 %collective-permute-start.1 = (bf16[128,3072]{1,0:T(8,128)(2,1)S(1)}, bf16[128,3072]{1,0:T(8,128)(2,1)}, u32[]{:S(2)}, u32[]{:S(2)}) collective-permute-start(bf16[128,3072]{1,0:T(8,128)(2,1)S(1)} %bitcast.12), channel_id=1, source_target_pairs={{0,1},{1,0},{2,3},{3,2},{4,5},{5,4},{6,7},{7,6},{8,9},{9,8},{10,11... | collective-permute-start | bytes 2359304 | tf_op jit(solution)/shard_map/ppermute | solution.py:68
  53.8 1.9 %collective-permute-start.2 = (bf16[128,3072]{1,0:T(8,128)(2,1)S(1)}, bf16[128,3072]{1,0:T(8,128)(2,1)}, u32[]{:S(2)}, u32[]{:S(2)}) collective-permute-start(bf16[128,3072]{1,0:T(8,128)(2,1)S(1)} %bitcast.13), channel_id=1, source_target_pairs={{0,128},{1,129},{2,130},{3,131},{4,132},{5,133},{6,134},{7,135},{8... | collective-permute-start | bytes 2359304 | tf_op jit(solution)/shard_map/ppermute | solution.py:68
  56.6 4.8 %collective-permute-done.p0 = bf16[128,3072]{1,0:T(8,128)(2,1)} collective-permute-done((bf16[128,3072]{1,0:T(8,128)(2,1)S(1)}, bf16[128,3072]{1,0:T(8,128)(2,1)}, u32[]{:S(2)}, u32[]{:S(2)}) %collective-permute-start) | collective-permute-done | bytes 786464 | tf_op jit(solution)/shard_map/ppermute | solution.py:68
  61.4 1.8 %shard_map.76.sums3 = f32[128,768]{1,0:T(8,128)S(1)} custom-call(bf16[128,3072]{1,0:T(8,128)(2,1)} %collective-permute-done.p0, bf16[1536,384]{1,0:T(8,128)(2,1)S(1)} %copy-done, bf16[384,1536]{1,0:T(8,128)(2,1)S(1)} %copy-done.1), custom_call_target="tpu_custom_call" | custom-call | flops 301989888 | bytes 3972864 | tf_op jit(solution)/shard_map/pallas_call | solution.py:246
  63.2 6.5 %collective-permute-done.1.p1 = bf16[128,3072]{1,0:T(8,128)(2,1)} collective-permute-done((bf16[128,3072]{1,0:T(8,128)(2,1)S(1)}, bf16[128,3072]{1,0:T(8,128)(2,1)}, u32[]{:S(2)}, u32[]{:S(2)}) %collective-permute-start.1) | collective-permute-done | bytes 786464 | tf_op jit(solution)/shard_map/ppermute | solution.py:68
  69.7 2.7 %shard_map.77 = (bf16[256,3072]{1,0:T(8,128)(2,1)S(1)}, f32[256,768]{1,0:T(8,128)S(1)}, f32[256,768]{1,0:T(8,128)S(1)}) custom-call(s32[5]{0:T(128)S(1)} %stack.23.place, f32[128,768]{1,0:T(8,128)S(1)} %shard_map.75.sums, f32[128,768]{1,0:T(8,128)S(1)} %shard_map.76.sums3, bf16[128,3072]{1,0:T(8,128)(2,1)} %collective-permute-done.1.p1, ...), custom_call_target="tpu_custom_call" | custom-call | flops 603979776 | bytes 5545728 | tf_op jit(solution)/shard_map/pallas_call | solution.py:256
  72.5 1.9 %collective-permute-start.3 = (f32[256,768]{1,0:T(8,128)S(1)}, f32[256,768]{1,0:T(8,128)S(1)}, u32[]{:S(2)}, u32[]{:S(2)}) collective-permute-start(f32[256,768]{1,0:T(8,128)S(1)} %get-tuple-element.25), channel_id=1, source_target_pairs={{0,16},{16,0},{1,17},{17,1},{2,18},{18,2},{3,19},{19,3},{4,20},{20... | collective-permute-start | bytes 2359304 | tf_op jit(solution)/shard_map/ppermute | solution.py:278
  74.4 2.3 %collective-permute-done.3.more = f32[256,768]{1,0:T(8,128)S(1)} collective-permute-done((f32[256,768]{1,0:T(8,128)S(1)}, f32[256,768]{1,0:T(8,128)S(1)}, u32[]{:S(2)}, u32[]{:S(2)}) %collective-permute-start.3) | collective-permute-done | bytes 786464 | tf_op jit(solution)/shard_map/ppermute | solution.py:278
  76.8 12.5 %all_to_all.32.parts = bf16[4,64,768]{2,1,0:T(8,128)(2,1)S(1)} all-to-all(bf16[4,64,768]{2,1,0:T(8,128)(2,1)S(1)} %bitcast.18), channel_id=1, replica_groups=mesh['z_lo'=4,'x'=4,'core'=2,'z_hi'=4,'y'=4] {'x'}, dimensions={0} | all-to-all | bytes 786432 | tf_op jit(solution)/shard_map/all_to_all | solution.py:279
  89.9 9.8 %all_to_all.33 = bf16[4,64,768]{2,1,0:T(8,128)(2,1)S(1)} all-to-all(bf16[4,64,768]{2,1,0:T(8,128)(2,1)S(1)} %shard_map.79), channel_id=1, replica_groups=mesh['z_lo'=4,'x'=4,'core'=2,'z_hi'=4,'y'=4] {'x'}, dimensions={0} | all-to-all | bytes 786432 | tf_op jit(solution)/shard_map/all_to_all | solution.py:287
  99.7 2.4 %all_gather.3.shares = bf16[512,768]{1,0:T(8,128)(2,1)S(1)} all-gather(bf16[256,768]{1,0:T(8,128)(2,1)S(1)} %bitcast.20), channel_id=1, replica_groups=mesh['z_lo'=4,'x'=4,'core'=2,'z_hi'=4,'y'=4] {'core'}, dimensions={0}, use_global_device_ids=true | all-gather | bytes 1179648 | tf_op jit(solution)/shard_map/all_gather | solution.py:288
  102.1 1.9 %shard_map.80 = (bf16[128,3072]{1,0:T(8,128)(2,1)S(1)}, bf16[128,3072]{1,0:T(8,128)(2,1)S(1)}, bf16[128,3072]{1,0:T(8,128)(2,1)S(1)}, bf16[512,768]{1,0:T(8,128)(2,1)S(1)}) custom-call(s32[5]{0:T(128)S(1)} %stack.23.place, bf16[512,768]{1,0:T(8,128)(2,1)S(1)} %all_gather.3.shares, bf16[1536,384]{1,0:T(8,128)(2,1)S(1)} %copy-done, bf16[384,1536]{1,0:T(8,128)(2,1)S(1)} %copy-done.1), custom_call_target="tpu_custom_call" | custom-call | flops 905969664 | bytes 7118592 | tf_op jit(solution)/shard_map/pallas_call | solution.py:289
  104.0 4.0 %collective-permute-start.4 = (bf16[128,3072]{1,0:T(8,128)(2,1)S(1)}, bf16[128,3072]{1,0:T(8,128)(2,1)S(1)}, u32[]{:S(2)}, u32[]{:S(2)}) collective-permute-start(bf16[128,3072]{1,0:T(8,128)(2,1)S(1)} %get-tuple-element.29), channel_id=1, source_target_pairs={{0,129},{1,128},{2,131},{3,130},{4,133},{5,132},{6,135},{7,134},{8... | collective-permute-start | bytes 2359304 | tf_op jit(solution)/shard_map/ppermute | solution.py:68
  108.0 3.3 %collective-permute-start.5 = (bf16[128,3072]{1,0:T(8,128)(2,1)S(1)}, bf16[128,3072]{1,0:T(8,128)(2,1)S(1)}, u32[]{:S(2)}, u32[]{:S(2)}) collective-permute-start(bf16[128,3072]{1,0:T(8,128)(2,1)S(1)} %get-tuple-element.31), channel_id=1, source_target_pairs={{0,1},{1,0},{2,3},{3,2},{4,5},{5,4},{6,7},{7,6},{8,9},{9,8},{10,11... | collective-permute-start | bytes 2359304 | tf_op jit(solution)/shard_map/ppermute | solution.py:68
  111.4 1.9 %collective-permute-start.6 = (bf16[128,3072]{1,0:T(8,128)(2,1)S(1)}, bf16[128,3072]{1,0:T(8,128)(2,1)S(1)}, u32[]{:S(2)}, u32[]{:S(2)}) collective-permute-start(bf16[128,3072]{1,0:T(8,128)(2,1)S(1)} %get-tuple-element.32), channel_id=1, source_target_pairs={{0,128},{1,129},{2,130},{3,131},{4,132},{5,133},{6,134},{7,135},{8... | collective-permute-start | bytes 2359304 | tf_op jit(solution)/shard_map/ppermute | solution.py:68
  113.3 5.6 %collective-permute-done.4.r3 = bf16[128,3072]{1,0:T(8,128)(2,1)S(1)} collective-permute-done((bf16[128,3072]{1,0:T(8,128)(2,1)S(1)}, bf16[128,3072]{1,0:T(8,128)(2,1)S(1)}, u32[]{:S(2)}, u32[]{:S(2)}) %collective-permute-start.4) | collective-permute-done | bytes 786464 | tf_op jit(solution)/shard_map/ppermute | solution.py:68
  122.1 1.5 fusion.10
  123.6 1.5 fusion.3
  125.1 1.6 fusion.2
  128.1 13.4 %all_to_all.34.parts = bf16[4,32,3072]{2,1,0:T(8,128)(2,1)S(1)} all-to-all(bf16[4,32,3072]{2,1,0:T(8,128)(2,1)S(1)} %get-tuple-element.36), channel_id=1, replica_groups={{129,130,257,258},{131,128,259,256},{385,386,5,6},{387,384,7,4},{133,13..., dimensions={0} | all-to-all | bytes 1572864 | tf_op jit(solution)/shard_map/all_to_all | solution.py:333
  142.2 20.7 %all_to_all.35.parts = bf16[4,8,3072]{2,1,0:T(8,128)(2,1)S(1)} all-to-all(bf16[4,8,3072]{2,1,0:T(8,128)(2,1)S(1)} %bitcast.19), channel_id=1, replica_groups=mesh['z_lo'=4,'x'=4,'core'=2,'z_hi'=4,'y'=4] {'z_hi'}, dimensions={0} | all-to-all | bytes 393216 | tf_op jit(solution)/shard_map/all_to_all | solution.py:344
  (21 shorter events, 8.5 us)
Async XLA Ops:
  0.6 55.3 %copy-start = (bf16[1536,384]{1,0:T(8,128)(2,1)S(1)}, bf16[1536,384]{1,0:T(8,128)(2,1)}, u32[]{:S(2)}) copy-start(bf16[1536,384]{1,0:T(8,128)(2,1)} %first.9) | copy-start | bytes 3538948
  0.6 55.3 %copy-start.1 = (bf16[384,1536]{1,0:T(8,128)(2,1)S(1)}, bf16[384,1536]{1,0:T(8,128)(2,1)}, u32[]{:S(2)}) copy-start(bf16[384,1536]{1,0:T(8,128)(2,1)} %second.9) | copy-start | bytes 3538948
  46.4 15.0 %collective-permute-start = (bf16[128,3072]{1,0:T(8,128)(2,1)S(1)}, bf16[128,3072]{1,0:T(8,128)(2,1)}, u32[]{:S(2)}, u32[]{:S(2)}) collective-permute-start(bf16[128,3072]{1,0:T(8,128)(2,1)S(1)} %bitcast.11), channel_id=1, source_target_pairs={{0,129},{1,128},{2,131},{3,130},{4,133},{5,132},{6,135},{7,134},{8... | collective-permute-start | bytes 2359304 | tf_op jit(solution)/shard_map/ppermute | solution.py:68
  49.4 20.3 %collective-permute-start.1 = (bf16[128,3072]{1,0:T(8,128)(2,1)S(1)}, bf16[128,3072]{1,0:T(8,128)(2,1)}, u32[]{:S(2)}, u32[]{:S(2)}) collective-permute-start(bf16[128,3072]{1,0:T(8,128)(2,1)S(1)} %bitcast.12), channel_id=1, source_target_pairs={{0,1},{1,0},{2,3},{3,2},{4,5},{5,4},{6,7},{7,6},{8,9},{9,8},{10,11... | collective-permute-start | bytes 2359304 | tf_op jit(solution)/shard_map/ppermute | solution.py:68
  53.8 15.9 %collective-permute-start.2 = (bf16[128,3072]{1,0:T(8,128)(2,1)S(1)}, bf16[128,3072]{1,0:T(8,128)(2,1)}, u32[]{:S(2)}, u32[]{:S(2)}) collective-permute-start(bf16[128,3072]{1,0:T(8,128)(2,1)S(1)} %bitcast.13), channel_id=1, source_target_pairs={{0,128},{1,129},{2,130},{3,131},{4,132},{5,133},{6,134},{7,135},{8... | collective-permute-start | bytes 2359304 | tf_op jit(solution)/shard_map/ppermute | solution.py:68
  72.5 4.2 %collective-permute-start.3 = (f32[256,768]{1,0:T(8,128)S(1)}, f32[256,768]{1,0:T(8,128)S(1)}, u32[]{:S(2)}, u32[]{:S(2)}) collective-permute-start(f32[256,768]{1,0:T(8,128)S(1)} %get-tuple-element.25), channel_id=1, source_target_pairs={{0,16},{16,0},{1,17},{17,1},{2,18},{18,2},{3,19},{19,3},{4,20},{20... | collective-permute-start | bytes 2359304 | tf_op jit(solution)/shard_map/ppermute | solution.py:278
  104.0 14.9 %collective-permute-start.4 = (bf16[128,3072]{1,0:T(8,128)(2,1)S(1)}, bf16[128,3072]{1,0:T(8,128)(2,1)S(1)}, u32[]{:S(2)}, u32[]{:S(2)}) collective-permute-start(bf16[128,3072]{1,0:T(8,128)(2,1)S(1)} %get-tuple-element.29), channel_id=1, source_target_pairs={{0,129},{1,128},{2,131},{3,130},{4,133},{5,132},{6,135},{7,134},{8... | collective-permute-start | bytes 2359304 | tf_op jit(solution)/shard_map/ppermute | solution.py:68
  108.0 19.2 %collective-permute-start.5 = (bf16[128,3072]{1,0:T(8,128)(2,1)S(1)}, bf16[128,3072]{1,0:T(8,128)(2,1)S(1)}, u32[]{:S(2)}, u32[]{:S(2)}) collective-permute-start(bf16[128,3072]{1,0:T(8,128)(2,1)S(1)} %get-tuple-element.31), channel_id=1, source_target_pairs={{0,1},{1,0},{2,3},{3,2},{4,5},{5,4},{6,7},{7,6},{8,9},{9,8},{10,11... | collective-permute-start | bytes 2359304 | tf_op jit(solution)/shard_map/ppermute | solution.py:68
  111.4 15.8 %collective-permute-start.6 = (bf16[128,3072]{1,0:T(8,128)(2,1)S(1)}, bf16[128,3072]{1,0:T(8,128)(2,1)S(1)}, u32[]{:S(2)}, u32[]{:S(2)}) collective-permute-start(bf16[128,3072]{1,0:T(8,128)(2,1)S(1)} %get-tuple-element.32), channel_id=1, source_target_pairs={{0,128},{1,129},{2,130},{3,131},{4,132},{5,133},{6,134},{7,135},{8... | collective-permute-start | bytes 2359304 | tf_op jit(solution)/shard_map/ppermute | solution.py:68

commit v6 on v5

--- a/solution.py
+++ b/solution.py
@@ -83,10 +83,11 @@
 
 def common_block(core, own, slot, part):
     pair = lax.bitwise_xor(own, jnp.int32(slot))
+    odd = lax.rem(part % 2 + part // 2, 2)
     shift = 1 - core
     y = lax.rem(lax.rem(pair, 2) * 2 + part % 2 + shift, 4)
     z = lax.rem(pair // 2 * 2 + part // 2 + shift, 4)
-    return y * 4 + z
+    return odd * 8 + y * 2 + z // 2
 
 
 def first_kernel(p0, first, second, sums):
@@ -96,29 +97,40 @@
     sums[:, units:] = dot_over(p0[:, width:], second[...], 1, 1)
 
 
-def last_kernel(place, sums, sums3, p1, p2, first, second, both, kept, given, rest):
+def half_rows(place, half, sums, sums3, p1, p2, first, second, out, rows, rest):
     core, own = place[0], place[1]
     width = first.shape[0]
     units = first.shape[1]
+    parts = (half, 3 - half)
+    starts = [pl.multiple_of(part * BLOCK, BLOCK) for part in parts]
+    for index in range(2):
+        at = index * BLOCK
+        rows[at : at + BLOCK, :] = p1[pl.ds(starts[index], BLOCK), :]
+        rows[64 + at : 64 + at + BLOCK, :] = p2[pl.ds(starts[index], BLOCK), :]
+    rest[:, :units] = dot_over(rows[:, :width], first[...], 1, 0)
+    rest[:, units:] = dot_over(rows[:, width:], second[...], 1, 1)
+    for index in range(2):
+        for slot in range(4):
+            block = common_block(core, own, slot, parts[index])
+            start = pl.multiple_of(lax.rem(block, 8) * BLOCK, BLOCK)
+            if slot == 0:
+                values = sums[pl.ds(starts[index], BLOCK), :]
+            elif slot == 3:
+                values = sums3[pl.ds(starts[index], BLOCK), :]
+            else:
+                at = (slot - 1) * 64 + index * BLOCK
+                values = rest[at : at + BLOCK, :]
+            out[pl.ds(start, BLOCK), :] = values
+
+
+def given_kernel(place, sums, sums3, p1, p2, first, second, given, rows, rest):
+    half_rows(place, 1 - place[0], sums, sums3, p1, p2, first, second, given, rows, rest)
+
+
+def kept_kernel(place, sums, sums3, p1, p2, first, second, kept, both, rows, rest):
+    half_rows(place, place[0], sums, sums3, p1, p2, first, second, kept, rows, rest)
     both[0:128, :] = p1[...]
     both[128:256, :] = p2[...]
-    rest[:, :units] = dot_over(both[:, :width], first[...], 1, 0)
-    rest[:, units:] = dot_over(both[:, width:], second[...], 1, 1)
-    for slot in range(4):
-        source, base = ((sums, 0), (rest, 1), (rest, 1), (sums3, 3))[slot]
-        for part in range(4):
-            block = common_block(core, own, slot, part)
-            start = pl.multiple_of(lax.rem(block, 8) * BLOCK, BLOCK)
-            at = ((slot - base) * 4 + part) * BLOCK
-            mine = block // 8 == core
-
-            @pl.when(mine)
-            def _():
-                kept[pl.ds(start, BLOCK), :] = source[at : at + BLOCK, :]
-
-            @pl.when(jnp.logical_not(mine))
-            def _():
-                given[pl.ds(start, BLOCK), :] = source[at : at + BLOCK, :]
 
 
 def add_kernel(kept, more, total, sent):
@@ -253,19 +265,33 @@
         )(rows, first_weight, second_weight)
 
     sums, sums3 = early(both), early(p3)
-    every, kept, given = pl.pallas_call(
-        last_kernel,
-        out_shape=(
+    scratch = [
+        pltpu.VMEM((PIECE, 2 * width), jnp.bfloat16),
+        pltpu.VMEM((PIECE, 2 * units), jnp.float32),
+    ]
+    inputs = (place, sums, sums3, p1, p2, first_weight, second_weight)
+    given = pl.pallas_call(
+        given_kernel,
+        out_shape=shape_of(256, 2 * units, jnp.float32),
+        in_specs=[scalars] + [whole] * 6,
+        out_specs=whole,
+        scratch_shapes=scratch,
+        compiler_params=params,
+        cost_estimate=cost_of(128),
+    )(*inputs)
+    more = lax.ppermute(given, "core", SWAP)
+    kept, every = pl.pallas_call(
+        kept_kernel,
+        out_shape=(
+            shape_of(256, 2 * units, jnp.float32),
             shape_of(256, 2 * width, jnp.bfloat16),
-            shape_of(256, 2 * units, jnp.float32),
-            shape_of(256, 2 * units, jnp.float32),
         ),
         in_specs=[scalars] + [whole] * 6,
-        out_specs=(whole, whole, whole),
-        scratch_shapes=[pltpu.VMEM((256, 2 * units), jnp.float32)],
-        compiler_params=params,
-        cost_estimate=cost_of(256),
-    )(place, sums, sums3, p1, p2, first_weight, second_weight)
+        out_specs=(whole, whole),
+        scratch_shapes=scratch,
+        compiler_params=params,
+        cost_estimate=cost_of(128),
+    )(*inputs)
     kept, sent = pl.pallas_call(
         add_kernel,
         out_shape=(
@@ -275,7 +301,7 @@
         in_specs=[whole] * 2,
         out_specs=(whole, whole),
         compiler_params=params,
-    )(kept, lax.ppermute(given, "core", SWAP))
+    )(kept, more)
     parts = lax.all_to_all(sent.reshape(4, SHARE, 2 * units), "x", 0, 0)
     shares = pl.pallas_call(
         gelu_kernel,

time: 165 us -> 165 us (level)
  waiting for transfers between devices: 19.6 us -> 17.5 us
    ppermute x1, waiting for transfers between devices: 2.25 us -> 0.12 us  [on_device(): more = lax.ppermute(given, 'core', SWAP)]
    pallas_call x1 -> x2, Pallas kernels: 2.74 us -> 4.22 us  [the longest x1 2.13 us: on_device(): pl.pallas_call(kept_kernel, out_shape=(shape_of(256, 2 * units, jnp.float...]
  transfers between devices with their start and end apart: 7 -> 7, of which waited for: 5 -> 5; matrix products, arithmetic and copies ran while one was open for 4% -> 4% of each run, Pallas kernels for 2% -> 3%
where the time goes in v6:
time: 165 us; the launch traced here: 164 us
  blocking collectives  104 us (63%)
  starting transfers between devices  20.5 us (12%)
  waiting for transfers between devices  17.5 us (11%)
  Pallas kernels  12.5 us (8%)
  matrix products  7.1 us (4%)
    all_to_all x1, blocking collectives, on_device(): lax.all_to_all(copies_of(both, 4), 'z_hi', 0, 0).reshape(BLOCK, 2 * width)  31.8 us
    all_to_all x1, blocking collectives, on_device(): outs = lax.all_to_all(outs.reshape(4, 8, 2 * width), 'z_hi', 0, 0)  20.7 us
    ppermute x6, starting transfers between devices, moved(): return lax.ppermute(value, GRID, pairs)  18.5 us
    ppermute x6, waiting for transfers between devices, moved(): return lax.ppermute(value, GRID, pairs)  17.4 us
    all_to_all x1, blocking collectives, on_device(): outs = lax.all_to_all(outs, GRID, 0, 0, axis_index_groups=near)  13.4 us
    all_to_all x1, blocking collectives, on_device(): lax.all_to_all(copies_of(both, 4), GRID, 0, 0, axis_index_groups=near)  12.9 us
    all_to_all x1, blocking collectives, on_device(): parts = lax.all_to_all(sent.reshape(4, SHARE, 2 * units), 'x', 0, 0)  12.7 us
    all_to_all x1, blocking collectives, on_device(): shares = lax.all_to_all(shares, 'x', 0, 0).reshape(256, 2 * units)  10.2 us
  transfers between devices with their start and end apart: 7, of which 5 were waited for; matrix products, arithmetic and copies ran while one was open for 4% of the time, Pallas kernels for 3%

profile of v6, /device:TPU:24, one launch (start us, length us, event | category | flops | bytes accessed | tf_op | source)
XLA Modules:
  0.0 163.5 jit_solution(14968699202542388930)
XLA Ops:
  1.6 31.8 %all_to_all.30 = bf16[4,8,3072]{2,1,0:T(8,128)(2,1)S(1)} all-to-all(bf16[4,8,3072]{2,1,0:T(8,128)(2,1)S(1)} %broadcast_in_dim.6), channel_id=1, replica_groups=mesh['z_lo'=4,'x'=4,'core'=2,'z_hi'=4,'y'=4] {'z_hi'}, dimensions={0} | all-to-all | bytes 393216 | tf_op jit(solution)/shard_map/all_to_all | solution.py:252
  33.5 12.9 %all_to_all.31 = bf16[4,32,3072]{2,1,0:T(8,128)(2,1)S(1)} all-to-all(bf16[4,32,3072]{2,1,0:T(8,128)(2,1)S(1)} %broadcast_in_dim.15), channel_id=1, replica_groups={{129,130,257,258},{131,128,259,256},{385,386,5,6},{387,384,7,4},{133,13..., dimensions={0} | all-to-all | bytes 1572864 | tf_op jit(solution)/shard_map/all_to_all | solution.py:253
  46.4 3.0 %collective-permute-start = (bf16[128,3072]{1,0:T(8,128)(2,1)S(1)}, bf16[128,3072]{1,0:T(8,128)(2,1)}, u32[]{:S(2)}, u32[]{:S(2)}) collective-permute-start(bf16[128,3072]{1,0:T(8,128)(2,1)S(1)} %bitcast.11), channel_id=1, source_target_pairs={{0,129},{1,128},{2,131},{3,130},{4,133},{5,132},{6,135},{7,134},{8... | collective-permute-start | bytes 2359304 | tf_op jit(solution)/shard_map/ppermute | solution.py:68
  49.4 4.3 %collective-permute-start.1 = (bf16[128,3072]{1,0:T(8,128)(2,1)S(1)}, bf16[128,3072]{1,0:T(8,128)(2,1)}, u32[]{:S(2)}, u32[]{:S(2)}) collective-permute-start(bf16[128,3072]{1,0:T(8,128)(2,1)S(1)} %bitcast.12), channel_id=1, source_target_pairs={{0,1},{1,0},{2,3},{3,2},{4,5},{5,4},{6,7},{7,6},{8,9},{9,8},{10,11... | collective-permute-start | bytes 2359304 | tf_op jit(solution)/shard_map/ppermute | solution.py:68
  53.8 1.9 %collective-permute-start.2 = (bf16[128,3072]{1,0:T(8,128)(2,1)S(1)}, bf16[128,3072]{1,0:T(8,128)(2,1)}, u32[]{:S(2)}, u32[]{:S(2)}) collective-permute-start(bf16[128,3072]{1,0:T(8,128)(2,1)S(1)} %bitcast.13), channel_id=1, source_target_pairs={{0,128},{1,129},{2,130},{3,131},{4,132},{5,133},{6,134},{7,135},{8... | collective-permute-start | bytes 2359304 | tf_op jit(solution)/shard_map/ppermute | solution.py:68
  56.6 4.8 %collective-permute-done.p0 = bf16[128,3072]{1,0:T(8,128)(2,1)} collective-permute-done((bf16[128,3072]{1,0:T(8,128)(2,1)S(1)}, bf16[128,3072]{1,0:T(8,128)(2,1)}, u32[]{:S(2)}, u32[]{:S(2)}) %collective-permute-start) | collective-permute-done | bytes 786464 | tf_op jit(solution)/shard_map/ppermute | solution.py:68
  61.4 1.8 %shard_map.76.sums3 = f32[128,768]{1,0:T(8,128)S(1)} custom-call(bf16[128,3072]{1,0:T(8,128)(2,1)} %collective-permute-done.p0, bf16[1536,384]{1,0:T(8,128)(2,1)S(1)} %copy-done, bf16[384,1536]{1,0:T(8,128)(2,1)S(1)} %copy-done.1), custom_call_target="tpu_custom_call" | custom-call | flops 301989888 | bytes 3972864 | tf_op jit(solution)/shard_map/pallas_call | solution.py:258
  63.2 6.5 %collective-permute-done.1.p1 = bf16[128,3072]{1,0:T(8,128)(2,1)} collective-permute-done((bf16[128,3072]{1,0:T(8,128)(2,1)S(1)}, bf16[128,3072]{1,0:T(8,128)(2,1)}, u32[]{:S(2)}, u32[]{:S(2)}) %collective-permute-start.1) | collective-permute-done | bytes 786464 | tf_op jit(solution)/shard_map/ppermute | solution.py:68
  69.7 2.1 %shard_map.78 = f32[256,768]{1,0:T(8,128)S(1)} custom-call(s32[5]{0:T(128)S(1)} %stack.23.place, f32[128,768]{1,0:T(8,128)S(1)} %shard_map.75.sums, f32[128,768]{1,0:T(8,128)S(1)} %shard_map.76.sums3, bf16[128,3072]{1,0:T(8,128)(2,1)} %collective-permute-done.1.p1, bf16[128,3072]{1,0:T(8,128)(2,1)} %collective-permute-done.2.p2, ...), custom_call_target="tpu_custom_call" | custom-call | flops 301989888 | bytes 3972864 | tf_op jit(solution)/shard_map/pallas_call | solution.py:273
  71.8 1.9 %collective-permute-start.3 = (f32[256,768]{1,0:T(8,128)S(1)}, f32[256,768]{1,0:T(8,128)S(1)}, u32[]{:S(2)}, u32[]{:S(2)}) collective-permute-start(f32[256,768]{1,0:T(8,128)S(1)} %shard_map.78), channel_id=1, source_target_pairs={{0,16},{16,0},{1,17},{17,1},{2,18},{18,2},{3,19},{19,3},{4,20},{20... | collective-permute-start | bytes 2359304 | tf_op jit(solution)/shard_map/ppermute | solution.py:282
  73.8 2.1 %shard_map.77 = (f32[256,768]{1,0:T(8,128)S(1)}, bf16[256,3072]{1,0:T(8,128)(2,1)S(1)}) custom-call(s32[5]{0:T(128)S(1)} %stack.23.place, f32[128,768]{1,0:T(8,128)S(1)} %shard_map.75.sums, f32[128,768]{1,0:T(8,128)S(1)} %shard_map.76.sums3, bf16[128,3072]{1,0:T(8,128)(2,1)} %collective-permute-done.1.p1, bf16[128,3072]{1,0:T(8,128)(2,1)} %collective-permute-done.2.p2, ...), custom_call_target="tpu_custom_call" | custom-call | flops 301989888 | bytes 3972864 | tf_op jit(solution)/shard_map/pallas_call | solution.py:283
  76.2 12.7 %all_to_all.32.parts = bf16[4,64,768]{2,1,0:T(8,128)(2,1)S(1)} all-to-all(bf16[4,64,768]{2,1,0:T(8,128)(2,1)S(1)} %bitcast.18), channel_id=1, replica_groups=mesh['z_lo'=4,'x'=4,'core'=2,'z_hi'=4,'y'=4] {'x'}, dimensions={0} | all-to-all | bytes 786432 | tf_op jit(solution)/shard_map/all_to_all | solution.py:305
  89.6 10.2 %all_to_all.33 = bf16[4,64,768]{2,1,0:T(8,128)(2,1)S(1)} all-to-all(bf16[4,64,768]{2,1,0:T(8,128)(2,1)S(1)} %shard_map.80), channel_id=1, replica_groups=mesh['z_lo'=4,'x'=4,'core'=2,'z_hi'=4,'y'=4] {'x'}, dimensions={0} | all-to-all | bytes 786432 | tf_op jit(solution)/shard_map/all_to_all | solution.py:313
  99.7 2.4 %all_gather.3.shares = bf16[512,768]{1,0:T(8,128)(2,1)S(1)} all-gather(bf16[256,768]{1,0:T(8,128)(2,1)S(1)} %bitcast.20), channel_id=1, replica_groups=mesh['z_lo'=4,'x'=4,'core'=2,'z_hi'=4,'y'=4] {'core'}, dimensions={0}, use_global_device_ids=true | all-gather | bytes 1179648 | tf_op jit(solution)/shard_map/all_gather | solution.py:314
  102.1 1.9 %shard_map.81 = (bf16[128,3072]{1,0:T(8,128)(2,1)S(1)}, bf16[128,3072]{1,0:T(8,128)(2,1)S(1)}, bf16[128,3072]{1,0:T(8,128)(2,1)S(1)}, bf16[512,768]{1,0:T(8,128)(2,1)S(1)}) custom-call(s32[5]{0:T(128)S(1)} %stack.23.place, bf16[512,768]{1,0:T(8,128)(2,1)S(1)} %all_gather.3.shares, bf16[1536,384]{1,0:T(8,128)(2,1)S(1)} %copy-done, bf16[384,1536]{1,0:T(8,128)(2,1)S(1)} %copy-done.1), custom_call_target="tpu_custom_call" | custom-call | flops 905969664 | bytes 7118592 | tf_op jit(solution)/shard_map/pallas_call | solution.py:315
  104.0 4.0 %collective-permute-start.4 = (bf16[128,3072]{1,0:T(8,128)(2,1)S(1)}, bf16[128,3072]{1,0:T(8,128)(2,1)S(1)}, u32[]{:S(2)}, u32[]{:S(2)}) collective-permute-start(bf16[128,3072]{1,0:T(8,128)(2,1)S(1)} %get-tuple-element.27), channel_id=1, source_target_pairs={{0,129},{1,128},{2,131},{3,130},{4,133},{5,132},{6,135},{7,134},{8... | collective-permute-start | bytes 2359304 | tf_op jit(solution)/shard_map/ppermute | solution.py:68
  108.1 3.3 %collective-permute-start.5 = (bf16[128,3072]{1,0:T(8,128)(2,1)S(1)}, bf16[128,3072]{1,0:T(8,128)(2,1)S(1)}, u32[]{:S(2)}, u32[]{:S(2)}) collective-permute-start(bf16[128,3072]{1,0:T(8,128)(2,1)S(1)} %get-tuple-element.29), channel_id=1, source_target_pairs={{0,1},{1,0},{2,3},{3,2},{4,5},{5,4},{6,7},{7,6},{8,9},{9,8},{10,11... | collective-permute-start | bytes 2359304 | tf_op jit(solution)/shard_map/ppermute | solution.py:68
  111.4 1.9 %collective-permute-start.6 = (bf16[128,3072]{1,0:T(8,128)(2,1)S(1)}, bf16[128,3072]{1,0:T(8,128)(2,1)S(1)}, u32[]{:S(2)}, u32[]{:S(2)}) collective-permute-start(bf16[128,3072]{1,0:T(8,128)(2,1)S(1)} %get-tuple-element.30), channel_id=1, source_target_pairs={{0,128},{1,129},{2,130},{3,131},{4,132},{5,133},{6,134},{7,135},{8... | collective-permute-start | bytes 2359304 | tf_op jit(solution)/shard_map/ppermute | solution.py:68
  113.3 5.6 %collective-permute-done.4.r3 = bf16[128,3072]{1,0:T(8,128)(2,1)S(1)} collective-permute-done((bf16[128,3072]{1,0:T(8,128)(2,1)S(1)}, bf16[128,3072]{1,0:T(8,128)(2,1)S(1)}, u32[]{:S(2)}, u32[]{:S(2)}) %collective-permute-start.4) | collective-permute-done | bytes 786464 | tf_op jit(solution)/shard_map/ppermute | solution.py:68
  122.1 1.5 fusion.10
  123.6 1.5 fusion.3
  125.2 1.6 fusion.2
  128.2 13.4 %all_to_all.34.parts = bf16[4,32,3072]{2,1,0:T(8,128)(2,1)S(1)} all-to-all(bf16[4,32,3072]{2,1,0:T(8,128)(2,1)S(1)} %get-tuple-element.34), channel_id=1, replica_groups={{129,130,257,258},{131,128,259,256},{385,386,5,6},{387,384,7,4},{133,13..., dimensions={0} | all-to-all | bytes 1572864 | tf_op jit(solution)/shard_map/all_to_all | solution.py:359
  142.3 20.7 %all_to_all.35.parts = bf16[4,8,3072]{2,1,0:T(8,128)(2,1)S(1)} all-to-all(bf16[4,8,3072]{2,1,0:T(8,128)(2,1)S(1)} %bitcast.19), channel_id=1, replica_groups=mesh['z_lo'=4,'x'=4,'core'=2,'z_hi'=4,'y'=4] {'z_hi'}, dimensions={0} | all-to-all | bytes 393216 | tf_op jit(solution)/shard_map/all_to_all | solution.py:370
  (22 shorter events, 8.7 us)
Async XLA Ops:
  0.6 55.3 %copy-start = (bf16[1536,384]{1,0:T(8,128)(2,1)S(1)}, bf16[1536,384]{1,0:T(8,128)(2,1)}, u32[]{:S(2)}) copy-start(bf16[1536,384]{1,0:T(8,128)(2,1)} %first.11) | copy-start | bytes 3538948
  0.6 55.3 %copy-start.1 = (bf16[384,1536]{1,0:T(8,128)(2,1)S(1)}, bf16[384,1536]{1,0:T(8,128)(2,1)}, u32[]{:S(2)}) copy-start(bf16[384,1536]{1,0:T(8,128)(2,1)} %second.11) | copy-start | bytes 3538948
  46.4 15.0 %collective-permute-start = (bf16[128,3072]{1,0:T(8,128)(2,1)S(1)}, bf16[128,3072]{1,0:T(8,128)(2,1)}, u32[]{:S(2)}, u32[]{:S(2)}) collective-permute-start(bf16[128,3072]{1,0:T(8,128)(2,1)S(1)} %bitcast.11), channel_id=1, source_target_pairs={{0,129},{1,128},{2,131},{3,130},{4,133},{5,132},{6,135},{7,134},{8... | collective-permute-start | bytes 2359304 | tf_op jit(solution)/shard_map/ppermute | solution.py:68
  49.4 20.3 %collective-permute-start.1 = (bf16[128,3072]{1,0:T(8,128)(2,1)S(1)}, bf16[128,3072]{1,0:T(8,128)(2,1)}, u32[]{:S(2)}, u32[]{:S(2)}) collective-permute-start(bf16[128,3072]{1,0:T(8,128)(2,1)S(1)} %bitcast.12), channel_id=1, source_target_pairs={{0,1},{1,0},{2,3},{3,2},{4,5},{5,4},{6,7},{7,6},{8,9},{9,8},{10,11... | collective-permute-start | bytes 2359304 | tf_op jit(solution)/shard_map/ppermute | solution.py:68
  53.8 15.9 %collective-permute-start.2 = (bf16[128,3072]{1,0:T(8,128)(2,1)S(1)}, bf16[128,3072]{1,0:T(8,128)(2,1)}, u32[]{:S(2)}, u32[]{:S(2)}) collective-permute-start(bf16[128,3072]{1,0:T(8,128)(2,1)S(1)} %bitcast.13), channel_id=1, source_target_pairs={{0,128},{1,129},{2,130},{3,131},{4,132},{5,133},{6,134},{7,135},{8... | collective-permute-start | bytes 2359304 | tf_op jit(solution)/shard_map/ppermute | solution.py:68
  71.8 4.2 %collective-permute-start.3 = (f32[256,768]{1,0:T(8,128)S(1)}, f32[256,768]{1,0:T(8,128)S(1)}, u32[]{:S(2)}, u32[]{:S(2)}) collective-permute-start(f32[256,768]{1,0:T(8,128)S(1)} %shard_map.78), channel_id=1, source_target_pairs={{0,16},{16,0},{1,17},{17,1},{2,18},{18,2},{3,19},{19,3},{4,20},{20... | collective-permute-start | bytes 2359304 | tf_op jit(solution)/shard_map/ppermute | solution.py:282
  104.0 14.9 %collective-permute-start.4 = (bf16[128,3072]{1,0:T(8,128)(2,1)S(1)}, bf16[128,3072]{1,0:T(8,128)(2,1)S(1)}, u32[]{:S(2)}, u32[]{:S(2)}) collective-permute-start(bf16[128,3072]{1,0:T(8,128)(2,1)S(1)} %get-tuple-element.27), channel_id=1, source_target_pairs={{0,129},{1,128},{2,131},{3,130},{4,133},{5,132},{6,135},{7,134},{8... | collective-permute-start | bytes 2359304 | tf_op jit(solution)/shard_map/ppermute | solution.py:68
  108.1 19.2 %collective-permute-start.5 = (bf16[128,3072]{1,0:T(8,128)(2,1)S(1)}, bf16[128,3072]{1,0:T(8,128)(2,1)S(1)}, u32[]{:S(2)}, u32[]{:S(2)}) collective-permute-start(bf16[128,3072]{1,0:T(8,128)(2,1)S(1)} %get-tuple-element.29), channel_id=1, source_target_pairs={{0,1},{1,0},{2,3},{3,2},{4,5},{5,4},{6,7},{7,6},{8,9},{9,8},{10,11... | collective-permute-start | bytes 2359304 | tf_op jit(solution)/shard_map/ppermute | solution.py:68
  111.4 15.8 %collective-permute-start.6 = (bf16[128,3072]{1,0:T(8,128)(2,1)S(1)}, bf16[128,3072]{1,0:T(8,128)(2,1)S(1)}, u32[]{:S(2)}, u32[]{:S(2)}) collective-permute-start(bf16[128,3072]{1,0:T(8,128)(2,1)S(1)} %get-tuple-element.30), channel_id=1, source_target_pairs={{0,128},{1,129},{2,130},{3,131},{4,132},{5,133},{6,134},{7,135},{8... | collective-permute-start | bytes 2359304 | tf_op jit(solution)/shard_map/ppermute | solution.py:68

commit v7 on v5

--- a/solution.py
+++ b/solution.py
@@ -178,18 +178,18 @@
         o3[:, columns] = outs[256:384]
 
 
-def own_kernel(local, first, second, o0):
+def own_kernel(local, first, second, r3, o0):
     width = first.shape[0]
     sides = out_rows(local[0:128, :], first, second)
-    o0[:, :width] = sides[0]
-    o0[:, width:] = sides[1]
-
-
-def far_kernel(place, r3, r1, r2, o0, outs, own_lost):
+    o0[:, :width] = sides[0] + r3[:, :width].astype(jnp.float32)
+    o0[:, width:] = sides[1] + r3[:, width:].astype(jnp.float32)
+
+
+def far_kernel(place, r1, r2, o0, outs, own_lost):
     for part in range(4):
         rows = slice(part * BLOCK, (part + 1) * BLOCK)
         total = o0[rows, :] + r1[rows, :].astype(jnp.float32)
-        total = total + r2[rows, :].astype(jnp.float32) + r3[rows, :].astype(jnp.float32)
+        total = total + r2[rows, :].astype(jnp.float32)
         outs[part] = total.astype(jnp.bfloat16)
 
         @pl.when(place[3] == part)
@@ -304,11 +304,11 @@
     o0 = pl.pallas_call(
         own_kernel,
         out_shape=shape_of(PIECE, 2 * width, jnp.float32),
-        in_specs=[whole] * 3,
+        in_specs=[whole] * 4,
         out_specs=whole,
         compiler_params=params,
         cost_estimate=cost_of(128),
-    )(late, first_weight, second_weight)
+    )(late, first_weight, second_weight, r3)
     hidden, grad_pre = local[128:384, :units], local[128:384, units:]
     late_hidden, late_pre = late[:, :units], late[:, units:]
     first_grad = dot_over(every[:, :width], grad_pre, 0, 0)
@@ -326,10 +326,10 @@
             jax.ShapeDtypeStruct((4, BLOCK, 2 * width), jnp.bfloat16),
             shape_of(BLOCK, 2 * width, jnp.float32),
         ),
-        in_specs=[scalars] + [whole] * 4,
+        in_specs=[scalars] + [whole] * 3,
         out_specs=(whole, whole),
         compiler_params=params,
-    )(place, r3, r1, r2, o0)
+    )(place, r1, r2, o0)
     outs = lax.all_to_all(outs, GRID, 0, 0, axis_index_groups=near)
     outs, own_lost = pl.pallas_call(
         near_kernel,

time: 165 us -> 165 us (level)
  no operation moved by 1% of the time
where the time goes in v7:
time: 165 us; the launch traced here: 163 us
  blocking collectives  103 us (62%)
  starting transfers between devices  20.5 us (12%)
  waiting for transfers between devices  19.6 us (12%)
  Pallas kernels  10.9 us (7%)
  matrix products  7.1 us (4%)
    all_to_all x1, blocking collectives, on_device(): lax.all_to_all(copies_of(both, 4), 'z_hi', 0, 0).reshape(BLOCK, 2 * width)  31.8 us
    all_to_all x1, blocking collectives, on_device(): outs = lax.all_to_all(outs.reshape(4, 8, 2 * width), 'z_hi', 0, 0)  20.7 us
    ppermute x6, starting transfers between devices, moved(): return lax.ppermute(value, GRID, pairs)  18.6 us
    ppermute x6, waiting for transfers between devices, moved(): return lax.ppermute(value, GRID, pairs)  17.4 us
    all_to_all x1, blocking collectives, on_device(): outs = lax.all_to_all(outs, GRID, 0, 0, axis_index_groups=near)  13.4 us
    all_to_all x1, blocking collectives, on_device(): lax.all_to_all(copies_of(both, 4), GRID, 0, 0, axis_index_groups=near)  12.9 us
    all_to_all x1, blocking collectives, on_device(): parts = lax.all_to_all(sent.reshape(4, SHARE, 2 * units), 'x', 0, 0)  12.5 us
    all_to_all x1, blocking collectives, on_device(): shares = lax.all_to_all(shares, 'x', 0, 0).reshape(256, 2 * units)  9.77 us
  transfers between devices with their start and end apart: 7, of which 5 were waited for; matrix products, arithmetic and copies ran while one was open for 4% of the time, Pallas kernels for 2%

profile of v7, /device:TPU:24, one launch (start us, length us, event | category | flops | bytes accessed | tf_op | source)
XLA Modules:
  0.0 163.4 jit_solution(9768599357621327731)
XLA Ops:
  1.6 31.8 %all_to_all.30 = bf16[4,8,3072]{2,1,0:T(8,128)(2,1)S(1)} all-to-all(bf16[4,8,3072]{2,1,0:T(8,128)(2,1)S(1)} %broadcast_in_dim.6), channel_id=1, replica_groups=mesh['z_lo'=4,'x'=4,'core'=2,'z_hi'=4,'y'=4] {'z_hi'}, dimensions={0} | all-to-all | bytes 393216 | tf_op jit(solution)/shard_map/all_to_all | solution.py:240
  33.5 12.9 %all_to_all.31 = bf16[4,32,3072]{2,1,0:T(8,128)(2,1)S(1)} all-to-all(bf16[4,32,3072]{2,1,0:T(8,128)(2,1)S(1)} %broadcast_in_dim.15), channel_id=1, replica_groups={{129,130,257,258},{131,128,259,256},{385,386,5,6},{387,384,7,4},{133,13..., dimensions={0} | all-to-all | bytes 1572864 | tf_op jit(solution)/shard_map/all_to_all | solution.py:241
  46.4 3.0 %collective-permute-start = (bf16[128,3072]{1,0:T(8,128)(2,1)S(1)}, bf16[128,3072]{1,0:T(8,128)(2,1)}, u32[]{:S(2)}, u32[]{:S(2)}) collective-permute-start(bf16[128,3072]{1,0:T(8,128)(2,1)S(1)} %bitcast.11), channel_id=1, source_target_pairs={{0,129},{1,128},{2,131},{3,130},{4,133},{5,132},{6,135},{7,134},{8... | collective-permute-start | bytes 2359304 | tf_op jit(solution)/shard_map/ppermute | solution.py:68
  49.4 4.3 %collective-permute-start.1 = (bf16[128,3072]{1,0:T(8,128)(2,1)S(1)}, bf16[128,3072]{1,0:T(8,128)(2,1)}, u32[]{:S(2)}, u32[]{:S(2)}) collective-permute-start(bf16[128,3072]{1,0:T(8,128)(2,1)S(1)} %bitcast.12), channel_id=1, source_target_pairs={{0,1},{1,0},{2,3},{3,2},{4,5},{5,4},{6,7},{7,6},{8,9},{9,8},{10,11... | collective-permute-start | bytes 2359304 | tf_op jit(solution)/shard_map/ppermute | solution.py:68
  53.8 1.9 %collective-permute-start.2 = (bf16[128,3072]{1,0:T(8,128)(2,1)S(1)}, bf16[128,3072]{1,0:T(8,128)(2,1)}, u32[]{:S(2)}, u32[]{:S(2)}) collective-permute-start(bf16[128,3072]{1,0:T(8,128)(2,1)S(1)} %bitcast.13), channel_id=1, source_target_pairs={{0,128},{1,129},{2,130},{3,131},{4,132},{5,133},{6,134},{7,135},{8... | collective-permute-start | bytes 2359304 | tf_op jit(solution)/shard_map/ppermute | solution.py:68
  56.6 4.8 %collective-permute-done.p0 = bf16[128,3072]{1,0:T(8,128)(2,1)} collective-permute-done((bf16[128,3072]{1,0:T(8,128)(2,1)S(1)}, bf16[128,3072]{1,0:T(8,128)(2,1)}, u32[]{:S(2)}, u32[]{:S(2)}) %collective-permute-start) | collective-permute-done | bytes 786464 | tf_op jit(solution)/shard_map/ppermute | solution.py:68
  61.4 1.8 %shard_map.76.sums3 = f32[128,768]{1,0:T(8,128)S(1)} custom-call(bf16[128,3072]{1,0:T(8,128)(2,1)} %collective-permute-done.p0, bf16[1536,384]{1,0:T(8,128)(2,1)S(1)} %copy-done, bf16[384,1536]{1,0:T(8,128)(2,1)S(1)} %copy-done.1), custom_call_target="tpu_custom_call" | custom-call | flops 301989888 | bytes 3972864 | tf_op jit(solution)/shard_map/pallas_call | solution.py:246
  63.2 6.5 %collective-permute-done.1.p1 = bf16[128,3072]{1,0:T(8,128)(2,1)} collective-permute-done((bf16[128,3072]{1,0:T(8,128)(2,1)S(1)}, bf16[128,3072]{1,0:T(8,128)(2,1)}, u32[]{:S(2)}, u32[]{:S(2)}) %collective-permute-start.1) | collective-permute-done | bytes 786464 | tf_op jit(solution)/shard_map/ppermute | solution.py:68
  69.7 2.7 %shard_map.77 = (bf16[256,3072]{1,0:T(8,128)(2,1)S(1)}, f32[256,768]{1,0:T(8,128)S(1)}, f32[256,768]{1,0:T(8,128)S(1)}) custom-call(s32[5]{0:T(128)S(1)} %stack.23.place, f32[128,768]{1,0:T(8,128)S(1)} %shard_map.75.sums, f32[128,768]{1,0:T(8,128)S(1)} %shard_map.76.sums3, bf16[128,3072]{1,0:T(8,128)(2,1)} %collective-permute-done.1.p1, ...), custom_call_target="tpu_custom_call" | custom-call | flops 603979776 | bytes 5545728 | tf_op jit(solution)/shard_map/pallas_call | solution.py:256
  72.5 1.9 %collective-permute-start.3 = (f32[256,768]{1,0:T(8,128)S(1)}, f32[256,768]{1,0:T(8,128)S(1)}, u32[]{:S(2)}, u32[]{:S(2)}) collective-permute-start(f32[256,768]{1,0:T(8,128)S(1)} %get-tuple-element.25), channel_id=1, source_target_pairs={{0,16},{16,0},{1,17},{17,1},{2,18},{18,2},{3,19},{19,3},{4,20},{20... | collective-permute-start | bytes 2359304 | tf_op jit(solution)/shard_map/ppermute | solution.py:278
  74.4 2.3 %collective-permute-done.3.more = f32[256,768]{1,0:T(8,128)S(1)} collective-permute-done((f32[256,768]{1,0:T(8,128)S(1)}, f32[256,768]{1,0:T(8,128)S(1)}, u32[]{:S(2)}, u32[]{:S(2)}) %collective-permute-start.3) | collective-permute-done | bytes 786464 | tf_op jit(solution)/shard_map/ppermute | solution.py:278
  76.8 12.5 %all_to_all.32.parts = bf16[4,64,768]{2,1,0:T(8,128)(2,1)S(1)} all-to-all(bf16[4,64,768]{2,1,0:T(8,128)(2,1)S(1)} %bitcast.18), channel_id=1, replica_groups=mesh['z_lo'=4,'x'=4,'core'=2,'z_hi'=4,'y'=4] {'x'}, dimensions={0} | all-to-all | bytes 786432 | tf_op jit(solution)/shard_map/all_to_all | solution.py:279
  89.9 9.8 %all_to_all.33 = bf16[4,64,768]{2,1,0:T(8,128)(2,1)S(1)} all-to-all(bf16[4,64,768]{2,1,0:T(8,128)(2,1)S(1)} %shard_map.79), channel_id=1, replica_groups=mesh['z_lo'=4,'x'=4,'core'=2,'z_hi'=4,'y'=4] {'x'}, dimensions={0} | all-to-all | bytes 786432 | tf_op jit(solution)/shard_map/all_to_all | solution.py:287
  99.7 2.4 %all_gather.3.shares = bf16[512,768]{1,0:T(8,128)(2,1)S(1)} all-gather(bf16[256,768]{1,0:T(8,128)(2,1)S(1)} %bitcast.20), channel_id=1, replica_groups=mesh['z_lo'=4,'x'=4,'core'=2,'z_hi'=4,'y'=4] {'core'}, dimensions={0}, use_global_device_ids=true | all-gather | bytes 1179648 | tf_op jit(solution)/shard_map/all_gather | solution.py:288
  102.1 1.9 %shard_map.80 = (bf16[128,3072]{1,0:T(8,128)(2,1)S(1)}, bf16[128,3072]{1,0:T(8,128)(2,1)S(1)}, bf16[128,3072]{1,0:T(8,128)(2,1)S(1)}, bf16[512,768]{1,0:T(8,128)(2,1)S(1)}) custom-call(s32[5]{0:T(128)S(1)} %stack.23.place, bf16[512,768]{1,0:T(8,128)(2,1)S(1)} %all_gather.3.shares, bf16[1536,384]{1,0:T(8,128)(2,1)S(1)} %copy-done, bf16[384,1536]{1,0:T(8,128)(2,1)S(1)} %copy-done.1), custom_call_target="tpu_custom_call" | custom-call | flops 905969664 | bytes 7118592 | tf_op jit(solution)/shard_map/pallas_call | solution.py:289
  104.0 4.0 %collective-permute-start.6 = (bf16[128,3072]{1,0:T(8,128)(2,1)S(1)}, bf16[128,3072]{1,0:T(8,128)(2,1)S(1)}, u32[]{:S(2)}, u32[]{:S(2)}) collective-permute-start(bf16[128,3072]{1,0:T(8,128)(2,1)S(1)} %get-tuple-element.31), channel_id=1, source_target_pairs={{0,129},{1,128},{2,131},{3,130},{4,133},{5,132},{6,135},{7,134},{8... | collective-permute-start | bytes 2359304 | tf_op jit(solution)/shard_map/ppermute | solution.py:68
  108.0 3.3 %collective-permute-start.4 = (bf16[128,3072]{1,0:T(8,128)(2,1)S(1)}, bf16[128,3072]{1,0:T(8,128)(2,1)S(1)}, u32[]{:S(2)}, u32[]{:S(2)}) collective-permute-start(bf16[128,3072]{1,0:T(8,128)(2,1)S(1)} %get-tuple-element.28), channel_id=1, source_target_pairs={{0,1},{1,0},{2,3},{3,2},{4,5},{5,4},{6,7},{7,6},{8,9},{9,8},{10,11... | collective-permute-start | bytes 2359304 | tf_op jit(solution)/shard_map/ppermute | solution.py:68
  111.4 1.9 %collective-permute-start.5 = (bf16[128,3072]{1,0:T(8,128)(2,1)S(1)}, bf16[128,3072]{1,0:T(8,128)(2,1)S(1)}, u32[]{:S(2)}, u32[]{:S(2)}) collective-permute-start(bf16[128,3072]{1,0:T(8,128)(2,1)S(1)} %get-tuple-element.29), channel_id=1, source_target_pairs={{0,128},{1,129},{2,130},{3,131},{4,132},{5,133},{6,134},{7,135},{8... | collective-permute-start | bytes 2359304 | tf_op jit(solution)/shard_map/ppermute | solution.py:68
  113.3 5.6 %collective-permute-done.6.r3 = bf16[128,3072]{1,0:T(8,128)(2,1)S(1)} collective-permute-done((bf16[128,3072]{1,0:T(8,128)(2,1)S(1)}, bf16[128,3072]{1,0:T(8,128)(2,1)S(1)}, u32[]{:S(2)}, u32[]{:S(2)}) %collective-permute-start.6) | collective-permute-done | bytes 786464 | tf_op jit(solution)/shard_map/ppermute | solution.py:68
  122.1 1.5 fusion.10
  123.6 1.5 fusion.3
  125.1 1.6 fusion.2
  128.0 13.4 %all_to_all.34.parts = bf16[4,32,3072]{2,1,0:T(8,128)(2,1)S(1)} all-to-all(bf16[4,32,3072]{2,1,0:T(8,128)(2,1)S(1)} %get-tuple-element.36), channel_id=1, replica_groups={{129,130,257,258},{131,128,259,256},{385,386,5,6},{387,384,7,4},{133,13..., dimensions={0} | all-to-all | bytes 1572864 | tf_op jit(solution)/shard_map/all_to_all | solution.py:333
  142.1 20.7 %all_to_all.35.parts = bf16[4,8,3072]{2,1,0:T(8,128)(2,1)S(1)} all-to-all(bf16[4,8,3072]{2,1,0:T(8,128)(2,1)S(1)} %bitcast.19), channel_id=1, replica_groups=mesh['z_lo'=4,'x'=4,'core'=2,'z_hi'=4,'y'=4] {'z_hi'}, dimensions={0} | all-to-all | bytes 393216 | tf_op jit(solution)/shard_map/all_to_all | solution.py:344
  (21 shorter events, 8.4 us)
Async XLA Ops:
  0.6 55.3 %copy-start = (bf16[1536,384]{1,0:T(8,128)(2,1)S(1)}, bf16[1536,384]{1,0:T(8,128)(2,1)}, u32[]{:S(2)}) copy-start(bf16[1536,384]{1,0:T(8,128)(2,1)} %first.9) | copy-start | bytes 3538948
  0.6 55.3 %copy-start.1 = (bf16[384,1536]{1,0:T(8,128)(2,1)S(1)}, bf16[384,1536]{1,0:T(8,128)(2,1)}, u32[]{:S(2)}) copy-start(bf16[384,1536]{1,0:T(8,128)(2,1)} %second.9) | copy-start | bytes 3538948
  46.4 15.0 %collective-permute-start = (bf16[128,3072]{1,0:T(8,128)(2,1)S(1)}, bf16[128,3072]{1,0:T(8,128)(2,1)}, u32[]{:S(2)}, u32[]{:S(2)}) collective-permute-start(bf16[128,3072]{1,0:T(8,128)(2,1)S(1)} %bitcast.11), channel_id=1, source_target_pairs={{0,129},{1,128},{2,131},{3,130},{4,133},{5,132},{6,135},{7,134},{8... | collective-permute-start | bytes 2359304 | tf_op jit(solution)/shard_map/ppermute | solution.py:68
  49.4 20.3 %collective-permute-start.1 = (bf16[128,3072]{1,0:T(8,128)(2,1)S(1)}, bf16[128,3072]{1,0:T(8,128)(2,1)}, u32[]{:S(2)}, u32[]{:S(2)}) collective-permute-start(bf16[128,3072]{1,0:T(8,128)(2,1)S(1)} %bitcast.12), channel_id=1, source_target_pairs={{0,1},{1,0},{2,3},{3,2},{4,5},{5,4},{6,7},{7,6},{8,9},{9,8},{10,11... | collective-permute-start | bytes 2359304 | tf_op jit(solution)/shard_map/ppermute | solution.py:68
  53.8 15.9 %collective-permute-start.2 = (bf16[128,3072]{1,0:T(8,128)(2,1)S(1)}, bf16[128,3072]{1,0:T(8,128)(2,1)}, u32[]{:S(2)}, u32[]{:S(2)}) collective-permute-start(bf16[128,3072]{1,0:T(8,128)(2,1)S(1)} %bitcast.13), channel_id=1, source_target_pairs={{0,128},{1,129},{2,130},{3,131},{4,132},{5,133},{6,134},{7,135},{8... | collective-permute-start | bytes 2359304 | tf_op jit(solution)/shard_map/ppermute | solution.py:68
  72.5 4.2 %collective-permute-start.3 = (f32[256,768]{1,0:T(8,128)S(1)}, f32[256,768]{1,0:T(8,128)S(1)}, u32[]{:S(2)}, u32[]{:S(2)}) collective-permute-start(f32[256,768]{1,0:T(8,128)S(1)} %get-tuple-element.25), channel_id=1, source_target_pairs={{0,16},{16,0},{1,17},{17,1},{2,18},{18,2},{3,19},{19,3},{4,20},{20... | collective-permute-start | bytes 2359304 | tf_op jit(solution)/shard_map/ppermute | solution.py:278
  104.0 14.9 %collective-permute-start.6 = (bf16[128,3072]{1,0:T(8,128)(2,1)S(1)}, bf16[128,3072]{1,0:T(8,128)(2,1)S(1)}, u32[]{:S(2)}, u32[]{:S(2)}) collective-permute-start(bf16[128,3072]{1,0:T(8,128)(2,1)S(1)} %get-tuple-element.31), channel_id=1, source_target_pairs={{0,129},{1,128},{2,131},{3,130},{4,133},{5,132},{6,135},{7,134},{8... | collective-permute-start | bytes 2359304 | tf_op jit(solution)/shard_map/ppermute | solution.py:68
  108.0 19.2 %collective-permute-start.4 = (bf16[128,3072]{1,0:T(8,128)(2,1)S(1)}, bf16[128,3072]{1,0:T(8,128)(2,1)S(1)}, u32[]{:S(2)}, u32[]{:S(2)}) collective-permute-start(bf16[128,3072]{1,0:T(8,128)(2,1)S(1)} %get-tuple-element.28), channel_id=1, source_target_pairs={{0,1},{1,0},{2,3},{3,2},{4,5},{5,4},{6,7},{7,6},{8,9},{9,8},{10,11... | collective-permute-start | bytes 2359304 | tf_op jit(solution)/shard_map/ppermute | solution.py:68
  111.4 15.8 %collective-permute-start.5 = (bf16[128,3072]{1,0:T(8,128)(2,1)S(1)}, bf16[128,3072]{1,0:T(8,128)(2,1)S(1)}, u32[]{:S(2)}, u32[]{:S(2)}) collective-permute-start(bf16[128,3072]{1,0:T(8,128)(2,1)S(1)} %get-tuple-element.29), channel_id=1, source_target_pairs={{0,128},{1,129},{2,130},{3,131},{4,132},{5,133},{6,134},{7,135},{8... | collective-permute-start | bytes 2359304 | tf_op jit(solution)/shard_map/ppermute | solution.py:68

commit v8 on v5

--- a/solution.py
+++ b/solution.py
@@ -197,19 +197,14 @@
             own_lost[...] = lost(total)
 
 
-def near_kernel(place, parts, own_lost, outs, next_lost):
-    total = total_of(parts, own_lost[...])
-    outs[...] = total.astype(jnp.bfloat16)
-    for part in range(4):
-
-        @pl.when(place[4] == part)
-        def _():
-            next_lost[...] = lost(total[part * 8 : part * 8 + 8, :])
-
-
-def end_kernel(parts, own_lost, block_out, input_grad):
+def near_kernel(parts, own_lost, outs):
+    outs[...] = total_of(parts, own_lost[...]).astype(jnp.bfloat16)
+
+
+def end_kernel(parts, block_out, input_grad):
     width = block_out.shape[1]
-    outs = total_of(parts, own_lost[...]).astype(jnp.bfloat16)
+    wide = [parts[i].astype(jnp.float32) for i in range(4)]
+    outs = ((wide[0] + wide[1]) + (wide[2] + wide[3])).astype(jnp.bfloat16)
     block_out[...] = outs[:, :width]
     input_grad[...] = outs[:, width:]
 
@@ -331,24 +326,21 @@
         compiler_params=params,
     )(place, r3, r1, r2, o0)
     outs = lax.all_to_all(outs, GRID, 0, 0, axis_index_groups=near)
-    outs, own_lost = pl.pallas_call(
+    outs = pl.pallas_call(
         near_kernel,
-        out_shape=(
-            shape_of(BLOCK, 2 * width, jnp.bfloat16),
-            shape_of(8, 2 * width, jnp.float32),
-        ),
-        in_specs=[scalars, whole, whole],
-        out_specs=(whole, whole),
-        compiler_params=params,
-    )(place, outs, own_lost)
+        out_shape=shape_of(BLOCK, 2 * width, jnp.bfloat16),
+        in_specs=[whole, whole],
+        out_specs=whole,
+        compiler_params=params,
+    )(outs, own_lost)
     outs = lax.all_to_all(outs.reshape(4, 8, 2 * width), "z_hi", 0, 0)
     block_out, input_grad = pl.pallas_call(
         end_kernel,
         out_shape=(shape_of(8, width, jnp.bfloat16), shape_of(8, width, jnp.bfloat16)),
-        in_specs=[whole, whole],
+        in_specs=[whole],
         out_specs=(whole, whole),
         compiler_params=params,
-    )(outs, own_lost)
+    )(outs)
     return (block_out, input_grad, first_grad, second_grad)
 
 

time: 165 us -> 164 us (level)
  no operation moved by 1% of the time
where the time goes in v8:
time: 164 us; the launch traced here: 163 us
  blocking collectives  103 us (63%)
  starting transfers between devices  20.5 us (12%)
  waiting for transfers between devices  19.6 us (12%)
  Pallas kernels  10.4 us (6%)
  matrix products  7.1 us (4%)
    all_to_all x1, blocking collectives, on_device(): lax.all_to_all(copies_of(both, 4), 'z_hi', 0, 0).reshape(BLOCK, 2 * width)  31.8 us
    all_to_all x1, blocking collectives, on_device(): outs = lax.all_to_all(outs.reshape(4, 8, 2 * width), 'z_hi', 0, 0)  20.7 us
    ppermute x6, starting transfers between devices, moved(): return lax.ppermute(value, GRID, pairs)  18.6 us
    ppermute x6, waiting for transfers between devices, moved(): return lax.ppermute(value, GRID, pairs)  17.4 us
    all_to_all x1, blocking collectives, on_device(): outs = lax.all_to_all(outs, GRID, 0, 0, axis_index_groups=near)  13.4 us
    all_to_all x1, blocking collectives, on_device(): lax.all_to_all(copies_of(both, 4), GRID, 0, 0, axis_index_groups=near)  12.9 us
    all_to_all x1, blocking collectives, on_device(): parts = lax.all_to_all(sent.reshape(4, SHARE, 2 * units), 'x', 0, 0)  12.5 us
    all_to_all x1, blocking collectives, on_device(): shares = lax.all_to_all(shares, 'x', 0, 0).reshape(256, 2 * units)  9.77 us
  transfers between devices with their start and end apart: 7, of which 5 were waited for; matrix products, arithmetic and copies ran while one was open for 4% of the time, Pallas kernels for 2%

profile of v8, /device:TPU:24, one launch (start us, length us, event | category | flops | bytes accessed | tf_op | source)
XLA Modules:
  0.0 162.9 jit_solution(7376016613437659542)
XLA Ops:
  1.6 31.8 %all_to_all.30 = bf16[4,8,3072]{2,1,0:T(8,128)(2,1)S(1)} all-to-all(bf16[4,8,3072]{2,1,0:T(8,128)(2,1)S(1)} %broadcast_in_dim.6), channel_id=1, replica_groups=mesh['z_lo'=4,'x'=4,'core'=2,'z_hi'=4,'y'=4] {'z_hi'}, dimensions={0} | all-to-all | bytes 393216 | tf_op jit(solution)/shard_map/all_to_all | solution.py:235
  33.5 12.9 %all_to_all.31 = bf16[4,32,3072]{2,1,0:T(8,128)(2,1)S(1)} all-to-all(bf16[4,32,3072]{2,1,0:T(8,128)(2,1)S(1)} %broadcast_in_dim.15), channel_id=1, replica_groups={{129,130,257,258},{131,128,259,256},{385,386,5,6},{387,384,7,4},{133,13..., dimensions={0} | all-to-all | bytes 1572864 | tf_op jit(solution)/shard_map/all_to_all | solution.py:236
  46.4 3.0 %collective-permute-start = (bf16[128,3072]{1,0:T(8,128)(2,1)S(1)}, bf16[128,3072]{1,0:T(8,128)(2,1)}, u32[]{:S(2)}, u32[]{:S(2)}) collective-permute-start(bf16[128,3072]{1,0:T(8,128)(2,1)S(1)} %bitcast.11), channel_id=1, source_target_pairs={{0,129},{1,128},{2,131},{3,130},{4,133},{5,132},{6,135},{7,134},{8... | collective-permute-start | bytes 2359304 | tf_op jit(solution)/shard_map/ppermute | solution.py:68
  49.4 4.3 %collective-permute-start.1 = (bf16[128,3072]{1,0:T(8,128)(2,1)S(1)}, bf16[128,3072]{1,0:T(8,128)(2,1)}, u32[]{:S(2)}, u32[]{:S(2)}) collective-permute-start(bf16[128,3072]{1,0:T(8,128)(2,1)S(1)} %bitcast.12), channel_id=1, source_target_pairs={{0,1},{1,0},{2,3},{3,2},{4,5},{5,4},{6,7},{7,6},{8,9},{9,8},{10,11... | collective-permute-start | bytes 2359304 | tf_op jit(solution)/shard_map/ppermute | solution.py:68
  53.8 1.9 %collective-permute-start.2 = (bf16[128,3072]{1,0:T(8,128)(2,1)S(1)}, bf16[128,3072]{1,0:T(8,128)(2,1)}, u32[]{:S(2)}, u32[]{:S(2)}) collective-permute-start(bf16[128,3072]{1,0:T(8,128)(2,1)S(1)} %bitcast.13), channel_id=1, source_target_pairs={{0,128},{1,129},{2,130},{3,131},{4,132},{5,133},{6,134},{7,135},{8... | collective-permute-start | bytes 2359304 | tf_op jit(solution)/shard_map/ppermute | solution.py:68
  56.6 4.8 %collective-permute-done.p0 = bf16[128,3072]{1,0:T(8,128)(2,1)} collective-permute-done((bf16[128,3072]{1,0:T(8,128)(2,1)S(1)}, bf16[128,3072]{1,0:T(8,128)(2,1)}, u32[]{:S(2)}, u32[]{:S(2)}) %collective-permute-start) | collective-permute-done | bytes 786464 | tf_op jit(solution)/shard_map/ppermute | solution.py:68
  61.4 1.8 %shard_map.76.sums3 = f32[128,768]{1,0:T(8,128)S(1)} custom-call(bf16[128,3072]{1,0:T(8,128)(2,1)} %collective-permute-done.p0, bf16[1536,384]{1,0:T(8,128)(2,1)S(1)} %copy-done, bf16[384,1536]{1,0:T(8,128)(2,1)S(1)} %copy-done.1), custom_call_target="tpu_custom_call" | custom-call | flops 301989888 | bytes 3972864 | tf_op jit(solution)/shard_map/pallas_call | solution.py:241
  63.2 6.5 %collective-permute-done.1.p1 = bf16[128,3072]{1,0:T(8,128)(2,1)} collective-permute-done((bf16[128,3072]{1,0:T(8,128)(2,1)S(1)}, bf16[128,3072]{1,0:T(8,128)(2,1)}, u32[]{:S(2)}, u32[]{:S(2)}) %collective-permute-start.1) | collective-permute-done | bytes 786464 | tf_op jit(solution)/shard_map/ppermute | solution.py:68
  69.7 2.7 %shard_map.77 = (bf16[256,3072]{1,0:T(8,128)(2,1)S(1)}, f32[256,768]{1,0:T(8,128)S(1)}, f32[256,768]{1,0:T(8,128)S(1)}) custom-call(s32[5]{0:T(128)S(1)} %stack.23.place, f32[128,768]{1,0:T(8,128)S(1)} %shard_map.75.sums, f32[128,768]{1,0:T(8,128)S(1)} %shard_map.76.sums3, bf16[128,3072]{1,0:T(8,128)(2,1)} %collective-permute-done.1.p1, ...), custom_call_target="tpu_custom_call" | custom-call | flops 603979776 | bytes 5545728 | tf_op jit(solution)/shard_map/pallas_call | solution.py:251
  72.5 1.9 %collective-permute-start.3 = (f32[256,768]{1,0:T(8,128)S(1)}, f32[256,768]{1,0:T(8,128)S(1)}, u32[]{:S(2)}, u32[]{:S(2)}) collective-permute-start(f32[256,768]{1,0:T(8,128)S(1)} %get-tuple-element.23), channel_id=1, source_target_pairs={{0,16},{16,0},{1,17},{17,1},{2,18},{18,2},{3,19},{19,3},{4,20},{20... | collective-permute-start | bytes 2359304 | tf_op jit(solution)/shard_map/ppermute | solution.py:273
  74.4 2.3 %collective-permute-done.3.more = f32[256,768]{1,0:T(8,128)S(1)} collective-permute-done((f32[256,768]{1,0:T(8,128)S(1)}, f32[256,768]{1,0:T(8,128)S(1)}, u32[]{:S(2)}, u32[]{:S(2)}) %collective-permute-start.3) | collective-permute-done | bytes 786464 | tf_op jit(solution)/shard_map/ppermute | solution.py:273
  76.8 12.5 %all_to_all.32.parts = bf16[4,64,768]{2,1,0:T(8,128)(2,1)S(1)} all-to-all(bf16[4,64,768]{2,1,0:T(8,128)(2,1)S(1)} %bitcast.19), channel_id=1, replica_groups=mesh['z_lo'=4,'x'=4,'core'=2,'z_hi'=4,'y'=4] {'x'}, dimensions={0} | all-to-all | bytes 786432 | tf_op jit(solution)/shard_map/all_to_all | solution.py:274
  89.9 9.8 %all_to_all.33 = bf16[4,64,768]{2,1,0:T(8,128)(2,1)S(1)} all-to-all(bf16[4,64,768]{2,1,0:T(8,128)(2,1)S(1)} %shard_map.79), channel_id=1, replica_groups=mesh['z_lo'=4,'x'=4,'core'=2,'z_hi'=4,'y'=4] {'x'}, dimensions={0} | all-to-all | bytes 786432 | tf_op jit(solution)/shard_map/all_to_all | solution.py:282
  99.7 2.4 %all_gather.3.shares = bf16[512,768]{1,0:T(8,128)(2,1)S(1)} all-gather(bf16[256,768]{1,0:T(8,128)(2,1)S(1)} %bitcast.20), channel_id=1, replica_groups=mesh['z_lo'=4,'x'=4,'core'=2,'z_hi'=4,'y'=4] {'core'}, dimensions={0}, use_global_device_ids=true | all-gather | bytes 1179648 | tf_op jit(solution)/shard_map/all_gather | solution.py:283
  102.1 1.9 %shard_map.80 = (bf16[128,3072]{1,0:T(8,128)(2,1)S(1)}, bf16[128,3072]{1,0:T(8,128)(2,1)S(1)}, bf16[128,3072]{1,0:T(8,128)(2,1)S(1)}, bf16[512,768]{1,0:T(8,128)(2,1)S(1)}) custom-call(s32[5]{0:T(128)S(1)} %stack.23.place, bf16[512,768]{1,0:T(8,128)(2,1)S(1)} %all_gather.3.shares, bf16[1536,384]{1,0:T(8,128)(2,1)S(1)} %copy-done, bf16[384,1536]{1,0:T(8,128)(2,1)S(1)} %copy-done.1), custom_call_target="tpu_custom_call" | custom-call | flops 905969664 | bytes 7118592 | tf_op jit(solution)/shard_map/pallas_call | solution.py:284
  104.0 4.0 %collective-permute-start.4 = (bf16[128,3072]{1,0:T(8,128)(2,1)S(1)}, bf16[128,3072]{1,0:T(8,128)(2,1)S(1)}, u32[]{:S(2)}, u32[]{:S(2)}) collective-permute-start(bf16[128,3072]{1,0:T(8,128)(2,1)S(1)} %get-tuple-element.27), channel_id=1, source_target_pairs={{0,129},{1,128},{2,131},{3,130},{4,133},{5,132},{6,135},{7,134},{8... | collective-permute-start | bytes 2359304 | tf_op jit(solution)/shard_map/ppermute | solution.py:68
  108.0 3.3 %collective-permute-start.5 = (bf16[128,3072]{1,0:T(8,128)(2,1)S(1)}, bf16[128,3072]{1,0:T(8,128)(2,1)S(1)}, u32[]{:S(2)}, u32[]{:S(2)}) collective-permute-start(bf16[128,3072]{1,0:T(8,128)(2,1)S(1)} %get-tuple-element.29), channel_id=1, source_target_pairs={{0,1},{1,0},{2,3},{3,2},{4,5},{5,4},{6,7},{7,6},{8,9},{9,8},{10,11... | collective-permute-start | bytes 2359304 | tf_op jit(solution)/shard_map/ppermute | solution.py:68
  111.4 1.9 %collective-permute-start.6 = (bf16[128,3072]{1,0:T(8,128)(2,1)S(1)}, bf16[128,3072]{1,0:T(8,128)(2,1)S(1)}, u32[]{:S(2)}, u32[]{:S(2)}) collective-permute-start(bf16[128,3072]{1,0:T(8,128)(2,1)S(1)} %get-tuple-element.30), channel_id=1, source_target_pairs={{0,128},{1,129},{2,130},{3,131},{4,132},{5,133},{6,134},{7,135},{8... | collective-permute-start | bytes 2359304 | tf_op jit(solution)/shard_map/ppermute | solution.py:68
  113.3 5.6 %collective-permute-done.4.r3 = bf16[128,3072]{1,0:T(8,128)(2,1)S(1)} collective-permute-done((bf16[128,3072]{1,0:T(8,128)(2,1)S(1)}, bf16[128,3072]{1,0:T(8,128)(2,1)S(1)}, u32[]{:S(2)}, u32[]{:S(2)}) %collective-permute-start.4) | collective-permute-done | bytes 786464 | tf_op jit(solution)/shard_map/ppermute | solution.py:68
  122.1 1.5 fusion.10
  123.6 1.5 fusion.3
  125.1 1.6 fusion.2
  128.1 13.4 %all_to_all.34.parts = bf16[4,32,3072]{2,1,0:T(8,128)(2,1)S(1)} all-to-all(bf16[4,32,3072]{2,1,0:T(8,128)(2,1)S(1)} %get-tuple-element.34), channel_id=1, replica_groups={{129,130,257,258},{131,128,259,256},{385,386,5,6},{387,384,7,4},{133,13..., dimensions={0} | all-to-all | bytes 1572864 | tf_op jit(solution)/shard_map/all_to_all | solution.py:328
  141.6 20.7 %all_to_all.35.parts = bf16[4,8,3072]{2,1,0:T(8,128)(2,1)S(1)} all-to-all(bf16[4,8,3072]{2,1,0:T(8,128)(2,1)S(1)} %bitcast.18), channel_id=1, replica_groups=mesh['z_lo'=4,'x'=4,'core'=2,'z_hi'=4,'y'=4] {'z_hi'}, dimensions={0} | all-to-all | bytes 393216 | tf_op jit(solution)/shard_map/all_to_all | solution.py:336
  (21 shorter events, 7.9 us)
Async XLA Ops:
  0.6 55.3 %copy-start = (bf16[1536,384]{1,0:T(8,128)(2,1)S(1)}, bf16[1536,384]{1,0:T(8,128)(2,1)}, u32[]{:S(2)}) copy-start(bf16[1536,384]{1,0:T(8,128)(2,1)} %first.9) | copy-start | bytes 3538948
  0.6 55.3 %copy-start.1 = (bf16[384,1536]{1,0:T(8,128)(2,1)S(1)}, bf16[384,1536]{1,0:T(8,128)(2,1)}, u32[]{:S(2)}) copy-start(bf16[384,1536]{1,0:T(8,128)(2,1)} %second.9) | copy-start | bytes 3538948
  46.4 15.0 %collective-permute-start = (bf16[128,3072]{1,0:T(8,128)(2,1)S(1)}, bf16[128,3072]{1,0:T(8,128)(2,1)}, u32[]{:S(2)}, u32[]{:S(2)}) collective-permute-start(bf16[128,3072]{1,0:T(8,128)(2,1)S(1)} %bitcast.11), channel_id=1, source_target_pairs={{0,129},{1,128},{2,131},{3,130},{4,133},{5,132},{6,135},{7,134},{8... | collective-permute-start | bytes 2359304 | tf_op jit(solution)/shard_map/ppermute | solution.py:68
  49.4 20.3 %collective-permute-start.1 = (bf16[128,3072]{1,0:T(8,128)(2,1)S(1)}, bf16[128,3072]{1,0:T(8,128)(2,1)}, u32[]{:S(2)}, u32[]{:S(2)}) collective-permute-start(bf16[128,3072]{1,0:T(8,128)(2,1)S(1)} %bitcast.12), channel_id=1, source_target_pairs={{0,1},{1,0},{2,3},{3,2},{4,5},{5,4},{6,7},{7,6},{8,9},{9,8},{10,11... | collective-permute-start | bytes 2359304 | tf_op jit(solution)/shard_map/ppermute | solution.py:68
  53.8 15.9 %collective-permute-start.2 = (bf16[128,3072]{1,0:T(8,128)(2,1)S(1)}, bf16[128,3072]{1,0:T(8,128)(2,1)}, u32[]{:S(2)}, u32[]{:S(2)}) collective-permute-start(bf16[128,3072]{1,0:T(8,128)(2,1)S(1)} %bitcast.13), channel_id=1, source_target_pairs={{0,128},{1,129},{2,130},{3,131},{4,132},{5,133},{6,134},{7,135},{8... | collective-permute-start | bytes 2359304 | tf_op jit(solution)/shard_map/ppermute | solution.py:68
  72.5 4.2 %collective-permute-start.3 = (f32[256,768]{1,0:T(8,128)S(1)}, f32[256,768]{1,0:T(8,128)S(1)}, u32[]{:S(2)}, u32[]{:S(2)}) collective-permute-start(f32[256,768]{1,0:T(8,128)S(1)} %get-tuple-element.23), channel_id=1, source_target_pairs={{0,16},{16,0},{1,17},{17,1},{2,18},{18,2},{3,19},{19,3},{4,20},{20... | collective-permute-start | bytes 2359304 | tf_op jit(solution)/shard_map/ppermute | solution.py:273
  104.0 14.9 %collective-permute-start.4 = (bf16[128,3072]{1,0:T(8,128)(2,1)S(1)}, bf16[128,3072]{1,0:T(8,128)(2,1)S(1)}, u32[]{:S(2)}, u32[]{:S(2)}) collective-permute-start(bf16[128,3072]{1,0:T(8,128)(2,1)S(1)} %get-tuple-element.27), channel_id=1, source_target_pairs={{0,129},{1,128},{2,131},{3,130},{4,133},{5,132},{6,135},{7,134},{8... | collective-permute-start | bytes 2359304 | tf_op jit(solution)/shard_map/ppermute | solution.py:68
  108.0 19.2 %collective-permute-start.5 = (bf16[128,3072]{1,0:T(8,128)(2,1)S(1)}, bf16[128,3072]{1,0:T(8,128)(2,1)S(1)}, u32[]{:S(2)}, u32[]{:S(2)}) collective-permute-start(bf16[128,3072]{1,0:T(8,128)(2,1)S(1)} %get-tuple-element.29), channel_id=1, source_target_pairs={{0,1},{1,0},{2,3},{3,2},{4,5},{5,4},{6,7},{7,6},{8,9},{9,8},{10,11... | collective-permute-start | bytes 2359304 | tf_op jit(solution)/shard_map/ppermute | solution.py:68
  111.4 15.8 %collective-permute-start.6 = (bf16[128,3072]{1,0:T(8,128)(2,1)S(1)}, bf16[128,3072]{1,0:T(8,128)(2,1)S(1)}, u32[]{:S(2)}, u32[]{:S(2)}) collective-permute-start(bf16[128,3072]{1,0:T(8,128)(2,1)S(1)} %get-tuple-element.30), channel_id=1, source_target_pairs={{0,128},{1,129},{2,130},{3,131},{4,132},{5,133},{6,134},{7,135},{8... | collective-permute-start | bytes 2359304 | tf_op jit(solution)/shard_map/ppermute | solution.py:68
